TPU v7x, 32 devices: a whole 2x2x4 slice. The times are simulated.
32 devices in a mesh: groups: 2 (over y), lat: 4 (over z), chan: 2 (over x), pair: 2 (over core).
Axes of the slice: x: 2, y: 2, z: 4, core: 2. Of those that a mesh axis runs over, the one named last changes fastest.
Arguments:
- atmosphere: bfloat16 [512, 64, 1440], P('chan', ('groups', 'lat'), 'pair'), parts along dimension 1, may hold values from -6 to 6
- ocean_state: bfloat16 [256, 16384], P('chan', ('groups', 'lat', 'pair')), parts along dimension 1, may hold values from -6 to 6
- conv_taps: bfloat16 [512, 9], P('chan'), may hold values from -1.5 to 1.5
- atmos_gain: float32 [512], replicated, may hold values from 0.1 to 1.9
- atmos_up: bfloat16 [2048, 512], P('chan'), may hold values from -0.25 to 0.25
- atmos_down: bfloat16 [2048, 512], P('chan'), may hold values from -0.125 to 0.125
- ocean_gain: float32 [256], replicated, may hold values from 0.1 to 1.9
- ocean_up: bfloat16 [1024, 256], P('chan'), may hold values from -0.375 to 0.375
- ocean_down: bfloat16 [1024, 256], P('chan'), may hold values from -0.1875 to 0.1875
- remap_blocks: bfloat16 [64, 128, 128], replicated, may hold values from 0 to 4
- flux_sends: int32 [8, 8, 8], P(('lat', 'pair')), may hold values from 0 to 44
- flux_pattern: int32 [8, 128, 3], P(('lat', 'pair')), may hold values from 0 to 63, as said below
- sea_sends: int32 [8, 8, 1], P(('lat', 'pair')), may hold values from 0 to 7
- sea_pattern: int32 [8, 16, 3], P(('lat', 'pair')), may hold values from 0 to 63, as said below
- ocean_mask: int32 [64], P(('lat', 'pair')), may hold values 0 or 1
Outputs:
- atmos_next: bfloat16 [512, 64, 1440], P('chan', ('groups', 'lat'), 'pair'), parts along dimension 1
- ocean_next: bfloat16 [256, 16384], P('chan', ('groups', 'lat', 'pair')), parts along dimension 1
There are 2 independent parts, one for each index of `groups`. A program takes and returns all parts, laid end to end along the dimension named above; an argument that names none is the same for every part. Nothing has to cross between parts.
Inputs may be any that keep to these rules, and one draw needn't show every extreme that they name: `flux_pattern`: on each peer every slot number below 64 appears exactly twice in column 0; column 1 is an ocean tile below 8, column 2 a block below 64. `sea_pattern`: on each peer every slot number below 8 appears exactly twice in column 0; column 1 is an atmosphere tile below 45, column 2 a block below 64.
All inputs are finite; a program needn't handle non-finite values. No bound on the sum of `ocean_mask` on one device may be relied on, other than what follows from the above.
Results may differ from a plain program's by a relative error of at most 0.0085.
Values may be sent and summed in bfloat16 or wider, within the bound.
No kernel may reach another device: no remote copies, remote signals or barrier semaphores. Data moves between devices by JAX's collectives and lax.ppermute only.
A program may use at most 128 MiB of HBM per device.

v0:
```python
import math

import jax
import jax.numpy as jnp
from jax import lax
from jax.sharding import PartitionSpec as P


def padded_2(block, sides, width):
    for axis, dim in sides:
        count = lax.axis_size(axis)
        forward = [(i, i + 1) for i in range(count - 1)]
        forward.append((count - 1, 0))
        backward = [(target, source) for source, target in forward]
        low = lax.ppermute(
            lax.slice_in_dim(block, block.shape[dim] - width, None, axis=dim), axis, forward
        )
        high = lax.ppermute(lax.slice_in_dim(block, 0, width, axis=dim), axis, backward)
        block = jnp.concatenate([low, block, high], axis=dim)
    return block


def remap_tiles(received, pattern, blocks, tile_count, factor):
    flux_depth = received.shape[0]
    entries = pattern.shape[0]
    group_size = math.gcd(entries, 64)
    grouped = pattern.reshape(entries // group_size, group_size, 3)
    targets = jnp.arange(tile_count, dtype=jnp.int32)

    def add_group(running, entry_rows):
        picked = jnp.take(received, entry_rows[:, 0], axis=1)
        weights = jnp.take(blocks, entry_rows[:, 2], axis=0)
        products = jnp.einsum("kgi,gij->kgj", picked, weights, preferred_element_type=jnp.float32)
        onehot = (entry_rows[:, 1][:, None] == targets[None, :]).astype(jnp.float32)
        return (running + jnp.einsum("kgj,gt->ktj", products, onehot), None)

    initial = jnp.zeros((flux_depth, tile_count, 128), jnp.float32)
    summed, _ = lax.scan(add_group, initial, grouped)
    return summed * factor


def normalize(values, channel_gain):
    widened = values.astype(jnp.float32)
    inverse = lax.rsqrt(jnp.mean(widened * widened, axis=0, keepdims=True) + 1e-06)
    return (widened * inverse * channel_gain[:, None]).astype(jnp.bfloat16)


def shards(
    atmosphere,
    ocean_state,
    conv_taps,
    atmos_gain,
    atmos_up,
    atmos_down,
    ocean_gain,
    ocean_up,
    ocean_down,
    remap_blocks,
    flux_sends,
    flux_pattern,
    sea_sends,
    sea_pattern,
    ocean_mask,
):
    lat_bands = lax.axis_size("lat")
    halves = lax.axis_size("pair")
    peer_count = lat_bands * halves
    channels, lat_rows, lon_cells = atmosphere.shape
    flux_depth, ocean_cells = ocean_state.shape
    atmos_count = lat_rows * lon_cells // 128
    ocean_count = ocean_cells // 128
    flux_slots = flux_sends.shape[2]
    sea_slots = sea_sends.shape[2]
    flux_tiles = atmosphere[0::2].reshape(flux_depth, atmos_count, 128)
    ocean_tiles = ocean_state.reshape(flux_depth, ocean_count, 128)
    flux_out = jnp.take(flux_tiles, flux_sends[0].reshape(-1), axis=1)
    sea_out = jnp.take(ocean_tiles, sea_sends[0].reshape(-1), axis=1)
    flux_in, sea_in = (
        lax.all_to_all(
            flux_out.reshape(flux_depth, peer_count, flux_slots, 128),
            ("lat", "pair"),
            split_axis=1,
            concat_axis=1,
            tiled=True,
        ),
        lax.all_to_all(
            sea_out.reshape(flux_depth, peer_count, sea_slots, 128),
            ("lat", "pair"),
            split_axis=1,
            concat_axis=1,
            tiled=True,
        ),
    )
    flux_in = flux_in.reshape(flux_depth, peer_count * flux_slots, 128)
    sea_in = sea_in.reshape(flux_depth, peer_count * sea_slots, 128)
    flux_ocean = remap_tiles(flux_in, flux_pattern[0], remap_blocks, ocean_count, 0.125)
    sea_atmos = remap_tiles(sea_in, sea_pattern[0], remap_blocks, atmos_count, 1.0)
    ocean_input = (
        ocean_state.astype(jnp.float32) + flux_ocean.reshape(flux_depth, ocean_cells)
    ).astype(jnp.bfloat16)
    padded = padded_2(atmosphere, (("lat", 1), ("pair", 2)), 1)
    lat_index = lax.axis_index("lat")
    edge_rows = jnp.arange(lat_rows + 2)
    row_keep = ((edge_rows > 0) | (lat_index > 0)) & (
        (edge_rows < lat_rows + 1) | (lat_index < lat_bands - 1)
    )
    padded = padded.astype(jnp.float32) * row_keep.astype(jnp.float32)[None, :, None]
    tap_table = conv_taps.astype(jnp.float32)
    smooth = jnp.zeros((channels, lat_rows, lon_cells), jnp.float32)
    for row_step in range(3):
        for col_step in range(3):
            smooth = (
                smooth
                + tap_table[:, 3 * row_step + col_step][:, None, None]
                * padded[:, row_step : row_step + lat_rows, col_step : col_step + lon_cells]
            )
    combined = atmosphere.astype(jnp.float32) + smooth
    combined = combined.at[1::2].add(sea_atmos.reshape(flux_depth, lat_rows, lon_cells))
    atmos_input = combined.astype(jnp.bfloat16)
    atmos_cells, ocean_part = (
        lax.all_to_all(
            atmos_input.reshape(channels, lat_rows * lon_cells),
            "chan",
            split_axis=1,
            concat_axis=0,
            tiled=True,
        ),
        lax.all_to_all(ocean_input, "chan", split_axis=1, concat_axis=0, tiled=True),
    )
    atmos_normed = normalize(atmos_cells, atmos_gain)
    ocean_normed = normalize(ocean_part, ocean_gain)
    up_rows = lax.all_gather(atmos_up, "chan", axis=0, tiled=True)
    down_rows = lax.all_gather(atmos_down, "chan", axis=0, tiled=True)
    ocean_up_rows = lax.all_gather(ocean_up, "chan", axis=0, tiled=True)
    ocean_down_rows = lax.all_gather(ocean_down, "chan", axis=0, tiled=True)
    hidden = jax.nn.gelu(jnp.dot(up_rows, atmos_normed, preferred_element_type=jnp.float32)).astype(
        jnp.bfloat16
    )
    atmos_sum = lax.dot_general(
        down_rows, hidden, (((0,), (0,)), ((), ())), preferred_element_type=jnp.float32
    )
    ocean_hidden = jax.nn.gelu(
        jnp.dot(ocean_up_rows, ocean_normed, preferred_element_type=jnp.float32)
    ).astype(jnp.bfloat16)
    ocean_sum = lax.dot_general(
        ocean_down_rows, ocean_hidden, (((0,), (0,)), ((), ())), preferred_element_type=jnp.float32
    )
    ocean_stretch = ocean_part.shape[1]
    mask_cells = jnp.repeat(ocean_mask.astype(jnp.float32), 128)
    mask_cells = lax.dynamic_slice_in_dim(
        mask_cells, lax.axis_index("chan") * ocean_stretch, ocean_stretch
    )
    atmos_after = (atmos_cells.astype(jnp.float32) + atmos_sum).astype(jnp.bfloat16)
    ocean_after = (ocean_part.astype(jnp.float32) + mask_cells[None, :] * ocean_sum).astype(
        jnp.bfloat16
    )
    atmos_back, ocean_back = (
        lax.all_to_all(atmos_after, "chan", split_axis=0, concat_axis=1, tiled=True),
        lax.all_to_all(ocean_after, "chan", split_axis=0, concat_axis=1, tiled=True),
    )
    return (atmos_back.reshape(channels, lat_rows, lon_cells), ocean_back)


def solution(mesh):
    in_specs = (
        P("chan", ("groups", "lat"), "pair"),
        P("chan", ("groups", "lat", "pair")),
        P("chan", None),
        P(),
        P("chan", None),
        P("chan", None),
        P(),
        P("chan", None),
        P("chan", None),
        P(),
        P(("lat", "pair"), None, None),
        P(("lat", "pair"), None, None),
        P(("lat", "pair"), None, None),
        P(("lat", "pair"), None, None),
        P(("lat", "pair")),
    )
    out_specs = (P("chan", ("groups", "lat"), "pair"), P("chan", ("groups", "lat", "pair")))
    return jax.shard_map(shards, mesh=mesh, in_specs=in_specs, out_specs=out_specs, check_vma=False)
```

profile of v0, /device:TPU:16, one launch (start us, length us, event | category | flops | bytes accessed | tf_op | source)
XLA Modules:
  0.0 397.2 jit_solution(1647773054739178041)
XLA Ops:
  15.3 5.2 %all-to-all-start = ((bf16[128,8,1,128]{3,0,2,1:T(8,128)(2,1)}), bf16[128,8,1,128]{3,0,2,1:T(8,128)(2,1)S(1)}, u32[]{:S(2)}, u32[]{:S(2)}) async-start(bf16[128,8,1,128]{3,0,2,1:T(8,128)(2,1)} %fusion.64), calls=%async_computation | async-start | bytes 524288 | tf_op jit(solution)/shard_map/all_to_all | solution.py:86
  20.6 3.9 copy.80
  24.5 3.5 collective-permute-done
  34.0 3.7 pad_maximum_fusion.2
  42.7 3.0 gather_fusion.2
  49.6 12.1 %convert_multiply_fusion = f32[256,10,722]{2,1,0:T(8,128)} fusion(bf16[256,10,1]{2,1,0:T(8,128)(2,1)} %copy.87, bf16[256,1,720]{2,1,0:T(2,128)(2,1)} %copy.83, bf16[256,8,720]{2,1,0:T(8,128)(2,1)S(1)} %copy.80, bf16[256,1,720]{2,1,0:T(2,128)(2,1)} %copy.81, bf16[256,10,1]{2,1,0:T(8,128)(2,1)} %copy.86, f32[10]{0:T(128)S(1)} %and_convert_fusion), kind=kLoop, calls=%fused_computation.41 | loop fusion | flops 20331520 | bytes 11089960 | tf_op jit(solution)/shard_map/mul | solution.py:107
  61.7 44.3 %fusion.24 = f32[256,8,720]{2,1,0:T(8,128)} fusion(f32[256,10,722]{2,1,0:T(8,128)} %convert_multiply_fusion, bf16[256,8,720]{2,1,0:T(8,128)(2,1)S(1)} %copy.80, f32[256]{0:T(256)S(1)} %bitcast.202, f32[256]{0:T(256)S(1)} %bitcast.201, f32[256]{0:T(256)S(1)} %bitcast.200, f32[256]{0:T(256)S(1)} %bitcast.199, f32[256]{0:T(256)S(1)} %bitcast.198, ...), kind=kLoop, calls=%fused_computation.46 | loop fusion | flops 28016640 | bytes 61940736 | tf_op jit(solution)/shard_map/add | solution.py:117
  116.2 16.5 %scatter_fusion = f32[256,8,720]{2,1,0:T(8,128)} fusion(f32[256,8,720]{2,1,0:T(8,128)} %fusion.24, s32[128]{0:T(128)S(1)} %add_bitcast_fusion, f32[128,8,720]{2,1,0:T(8,128)S(1)} %copy.94), kind=kCustom, calls=%fused_computation.6 | custom fusion | flops 737280 | bytes 8847872 | tf_op jit(solution)/shard_map/scatter-add | solution.py:118
  132.7 5.4 %copy.95 = bf16[256,8,720]{0,2,1:T(8,128)(2,1)} copy(f32[256,8,720]{2,1,0:T(8,128)} %scatter_fusion) | data formatting | bytes 8847360 | tf_op jit(solution)/shard_map/scatter-add | solution.py:118
  138.1 4.0 %all-to-all-start.1 = ((bf16[256,2,2880]{0,2,1:T(8,128)(2,1)}), bf16[256,2,2880]{0,2,1:T(8,128)(2,1)S(1)}, u32[]{:S(2)}, u32[]{:S(2)}) async-start(bf16[256,2,2880]{0,2,1:T(8,128)(2,1)} %bitcast.176), calls=%async_computation.1 | async-start | bytes 5898240 | tf_op jit(solution)/shard_map/all_to_all | solution.py:121
  142.2 64.7 %slice.115 = bf16[128,8,720]{0,2,1:T(8,128)(2,1)} slice(bf16[256,8,720]{0,2,1:T(8,128)(2,1)} %param.17), slice={[0:256:2], [0:8:1], [0:720:1]} | slice | bytes 2949120 | tf_op jit(solution)/shard_map/slice | solution.py:74
  206.9 3.5 gather_fusion.5
  210.5 4.1 %copy.98 = bf16[128,64,128]{2,0,1:T(8,128)(2,1)} copy(bf16[128,64,128]{0,2,1:T(8,128)(2,1)} %bitcast.180) | data formatting | bytes 4194304 | tf_op jit(solution)/shard_map/jit(_take)/gather | solution.py:76
  214.5 3.2 broadcast_select_fusion
  217.7 4.4 %all-to-all-start.3 = ((bf16[128,8,8,128]{3,0,2,1:T(8,128)(2,1)}), bf16[128,8,8,128]{3,0,2,1:T(8,128)(2,1)}, u32[]{:S(2)}, u32[]{:S(2)}) async-start(bf16[128,8,8,128]{3,0,2,1:T(8,128)(2,1)} %broadcast_select_fusion), calls=%async_computation.3 | async-start | bytes 4194304 | tf_op jit(solution)/shard_map/all_to_all | solution.py:79
  224.2 3.5 copy.108
  228.4 39.5 %all-to-all-done.3 = bf16[128,8,8,128]{3,0,2,1:T(8,128)(2,1)} async-done(((bf16[128,8,8,128]{3,0,2,1:T(8,128)(2,1)}), bf16[128,8,8,128]{3,0,2,1:T(8,128)(2,1)}, u32[]{:S(2)}, u32[]{:S(2)}) %all-to-all-start.3) | async-done | bytes 2097184 | tf_op jit(solution)/shard_map/all_to_all | solution.py:79
  267.9 30.0 %while.3 = (s32[]{:T(128)}, f32[128,8,128]{2,1,0:T(8,128)S(1)}, s32[2,64,3]{1,0,2:T(2,128)S(1)}, bf16[64,128,128]{2,1,0:T(8,128)(2,1)}, bf16[128,64,128]{2,0,1:T(8,128)(2,1)}, /*index=5*/s32[]{:T(128)}, s32[]{:T(128)}) while((s32[]{:T(128)}, f32[128,8,128]{2,1,0:T(8,128)S(1)}, s32[2,64,3]{1,0,2:T(2,128)S(1)}, ...), condition=%wide.region_3.4_spmd.clone, body=%wide.region_2.3_spmd.clone.sunk | while | flops 287575680 | bytes 22035032 | solution.py:38
  270.7 3.7 gather_fusion.1
  274.4 4.8 %convolution_bitcast_fusion.5 = bf16[128,64,128]{0,2,1:T(8,128)(2,1)} fusion(bf16[64,128,128]{2,1,0:T(8,128)(2,1)S(1)} %gather_fusion, bf16[64,128,128]{2,1,0:T(8,128)(2,1)} %gather_fusion.1, pred[64]{0:T(512)(128)(4,1)S(1)} %get-tuple-element.172, pred[64]{0:T(512)(128)(4,1)S(1)} %get-tuple-element.173), kind=kOutput, calls=%fused_computation.8.clone.1 | convolution fusion | flops 270532608 | bytes 6291584 | tf_op jit(solution)/shard_map/while/body/eval_jaxpr/kgi,gij->kgj/dot_general | solution.py:33
  279.3 3.3 copy.123
  285.6 3.7 gather_fusion.1
  289.3 4.8 %convolution_bitcast_fusion.5 = bf16[128,64,128]{0,2,1:T(8,128)(2,1)} fusion(bf16[64,128,128]{2,1,0:T(8,128)(2,1)S(1)} %gather_fusion, bf16[64,128,128]{2,1,0:T(8,128)(2,1)} %gather_fusion.1, pred[64]{0:T(512)(128)(4,1)S(1)} %get-tuple-element.172, pred[64]{0:T(512)(128)(4,1)S(1)} %get-tuple-element.173), kind=kOutput, calls=%fused_computation.8.clone.1 | convolution fusion | flops 270532608 | bytes 6291584 | tf_op jit(solution)/shard_map/while/body/eval_jaxpr/kgi,gij->kgj/dot_general | solution.py:33
  294.1 3.3 copy.123
  298.8 3.4 all-to-all-start.4
  302.3 18.5 %fusion.33 = bf16[512,2880]{0,1:T(8,128)(2,1)S(1)} fusion(f32[512,2880]{0,1:T(8,128)} %bitcast.181, bf16[2048,512]{1,0:T(8,128)(2,1)} %all-gather.5.cloned.1.call-done, bf16[2048,512]{1,0:T(8,128)(2,1)} %all-gather.3.cloned.1.call-done, f32[512]{0:T(512)S(1)} %copy-done.7, f32[2880]{0:T(1024)S(1)} %add_rsqrt_fusion), kind=kOutput, calls=%fused_computation.64 | convolution fusion | flops 12140052480 | bytes 13055232 | tf_op jit(solution)/shard_map/dot_general | solution.py:139
  322.6 4.1 %all-to-all-start.2 = ((bf16[2,256,2880]{1,2,0:T(8,128)(2,1)}), bf16[2,256,2880]{1,2,0:T(8,128)(2,1)S(1)}, u32[]{:S(2)}, u32[]{:S(2)}) async-start(bf16[2,256,2880]{1,2,0:T(8,128)(2,1)} %bitcast.175), calls=%async_computation.2 | async-start | bytes 5898240 | tf_op jit(solution)/shard_map/all_to_all | solution.py:158
  326.9 39.8 %all_gather.14 = bf16[1024,256]{1,0:T(8,128)(2,1)} all-gather(bf16[512,256]{1,0:T(8,128)(2,1)S(1)} %copy-done.1), channel_id=1, replica_groups=mesh['groups'=2,'lat'=4,'chan'=2,'pair'=2] {'chan'}, dimensions={0}, use_global_device_ids=true | all-gather | bytes 786432 | tf_op jit(solution)/shard_map/all_gather | solution.py:134
  366.7 8.5 %all_gather.15 = bf16[1024,256]{1,0:T(8,128)(2,1)} all-gather(bf16[512,256]{1,0:T(8,128)(2,1)} %param.25), channel_id=1, replica_groups=mesh['groups'=2,'lat'=4,'chan'=2,'pair'=2] {'chan'}, dimensions={0}, use_global_device_ids=true | all-gather | bytes 786432 | tf_op jit(solution)/shard_map/all_gather | solution.py:135
  376.2 3.2 fusion.51
  379.5 3.4 all-to-all-start.5
  382.9 5.2 %all-to-all-done.5 = bf16[2,128,512]{2,1,0:T(8,128)(2,1)S(1)} async-done(((bf16[2,128,512]{2,1,0:T(8,128)(2,1)}), bf16[2,128,512]{2,1,0:T(8,128)(2,1)S(1)}, u32[]{:S(2)}, u32[]{:S(2)}) %all-to-all-start.5) | async-done | bytes 262176 | tf_op jit(solution)/shard_map/all_to_all | solution.py:159
  (99 shorter events, 48.3 us)
Async XLA Ops:
  7.2 13.3 %copy-start.4 = (s32[1,16,3]{1,0,2:T(1,128)S(1)}, s32[1,16,3]{1,0,2:T(1,128)}, u32[]{:S(2)}) copy-start(s32[1,16,3]{1,0,2:T(1,128)} %param.30) | copy-start | bytes 580
  9.2 18.9 %collective-permute-start = (bf16[256,1,720]{0,2,1:T(8,128)(2,1)}, bf16[256,1,720]{0,2,1:T(8,128)(2,1)}, u32[]{:S(2)}, u32[]{:S(2)}) collective-permute-start(bf16[256,1,720]{0,2,1:T(8,128)(2,1)} %get-tuple-element.112), channel_id=1, source_target_pairs={{0,4},{4,8},{8,12},{12,0},{1,5},{5,9},{9,13},{13,1},{2,6},{6,10},{... | collective-permute-start | bytes 1105928 | tf_op jit(solution)/shard_map/ppermute | solution.py:15
  10.8 20.2 %collective-permute-start.1 = (bf16[256,1,720]{0,2,1:T(8,128)(2,1)}, bf16[256,1,720]{0,2,1:T(8,128)(2,1)}, u32[]{:S(2)}, u32[]{:S(2)}) collective-permute-start(bf16[256,1,720]{0,2,1:T(8,128)(2,1)} %get-tuple-element.113), channel_id=1, source_target_pairs={{4,0},{8,4},{12,8},{0,12},{5,1},{9,5},{13,9},{1,13},{6,2},{10,6},{... | collective-permute-start | bytes 1105928 | tf_op jit(solution)/shard_map/ppermute | solution.py:18
  15.3 90.8 %all-to-all-start = ((bf16[128,8,1,128]{3,0,2,1:T(8,128)(2,1)}), bf16[128,8,1,128]{3,0,2,1:T(8,128)(2,1)S(1)}, u32[]{:S(2)}, u32[]{:S(2)}) async-start(bf16[128,8,1,128]{3,0,2,1:T(8,128)(2,1)} %fusion.64), calls=%async_computation | async-start | bytes 524288 | tf_op jit(solution)/shard_map/all_to_all | solution.py:86
  20.5 4.0 copy-start.3
  39.9 5.8 %collective-permute-start.2 = (bf16[256,10,1]{0,1,2:T(8,128)(2,1)S(1)}, bf16[256,10,1]{0,1,2:T(8,128)(2,1)S(1)}, u32[]{:S(2)}, u32[]{:S(2)}) collective-permute-start(bf16[256,10,1]{0,1,2:T(8,128)(2,1)S(1)} %copy.84), channel_id=1, source_target_pairs={{0,1},{1,0},{2,3},{3,2},{4,5},{5,4},{6,7},{7,6},{8,9},{9,8},{10,11... | collective-permute-start | bytes 15368 | tf_op jit(solution)/shard_map/ppermute | solution.py:15
  42.2 5.5 %collective-permute-start.3 = (bf16[256,10,1]{0,1,2:T(8,128)(2,1)S(1)}, bf16[256,10,1]{0,1,2:T(8,128)(2,1)S(1)}, u32[]{:S(2)}, u32[]{:S(2)}) collective-permute-start(bf16[256,10,1]{0,1,2:T(8,128)(2,1)S(1)} %copy.85), channel_id=1, source_target_pairs={{1,0},{0,1},{3,2},{2,3},{5,4},{4,5},{7,6},{6,7},{9,8},{8,9},{11,10... | collective-permute-start | bytes 15368 | tf_op jit(solution)/shard_map/ppermute | solution.py:18
  138.1 68.7 %copy-start.2 = (s32[1,8,8]{2,1,0:T(8,128)S(1)}, s32[1,8,8]{2,1,0:T(8,128)}, u32[]{:S(2)}) copy-start(s32[1,8,8]{2,1,0:T(8,128)} %param.27) | copy-start | bytes 772
  138.1 79.6 %all-to-all-start.1 = ((bf16[256,2,2880]{0,2,1:T(8,128)(2,1)}), bf16[256,2,2880]{0,2,1:T(8,128)(2,1)S(1)}, u32[]{:S(2)}, u32[]{:S(2)}) async-start(bf16[256,2,2880]{0,2,1:T(8,128)(2,1)} %bitcast.176), calls=%async_computation.1 | async-start | bytes 5898240 | tf_op jit(solution)/shard_map/all_to_all | solution.py:121
  217.7 5.9 %copy-start.5 = (s32[1,128,3]{1,0,2:T(1,128)S(1)}, s32[1,128,3]{1,0,2:T(1,128)}, u32[]{:S(2)}) copy-start(s32[1,128,3]{1,0,2:T(1,128)} %param.28) | copy-start | bytes 4612
  217.7 50.1 %all-to-all-start.3 = ((bf16[128,8,8,128]{3,0,2,1:T(8,128)(2,1)}), bf16[128,8,8,128]{3,0,2,1:T(8,128)(2,1)}, u32[]{:S(2)}, u32[]{:S(2)}) async-start(bf16[128,8,8,128]{3,0,2,1:T(8,128)(2,1)} %broadcast_select_fusion), calls=%async_computation.3 | async-start | bytes 4194304 | tf_op jit(solution)/shard_map/all_to_all | solution.py:79
  222.2 80.1 %all-gather.3.cloned.1.call-start = ((), (), s32[]{:S(2)}) async-start(), calls=%async_computation.6 | async-start | bytes 3145728 | tf_op jit(solution)/shard_map/all_gather | solution.py:132
  222.9 79.3 %all-gather.5.cloned.1.call-start = ((), (), s32[]{:S(2)}) async-start(), calls=%async_computation.7 | async-start | bytes 3145728 | tf_op jit(solution)/shard_map/all_gather | solution.py:133
  267.9 30.0 %copy-start = (bf16[128,1024]{1,0:T(8,128)(2,1)S(1)}, bf16[128,1024]{1,0:T(8,128)(2,1)}, u32[]{:S(2)}) copy-start(bf16[128,1024]{1,0:T(8,128)(2,1)} %param.18) | copy-start | bytes 786436
  297.8 4.4 %copy-start.7 = (f32[512]{0:T(512)S(1)}, f32[512]{0:T(512)}, u32[]{:S(2)}) copy-start(f32[512]{0:T(512)} %param.20) | copy-start | bytes 6148
  298.8 23.9 %all-to-all-start.4 = ((bf16[128,2,512]{2,0,1:T(8,128)(2,1)}), bf16[128,2,512]{2,0,1:T(8,128)(2,1)S(1)}, u32[]{:S(2)}, u32[]{:S(2)}) async-start(bf16[128,2,512]{2,0,1:T(8,128)(2,1)} %bitcast.156), calls=%async_computation.4 | async-start | bytes 524288 | tf_op jit(solution)/shard_map/all_to_all | solution.py:128
  322.6 4.1 %copy-start.8 = (s32[8]{0:T(128)S(1)}, s32[8]{0:T(128)}, u32[]{:S(2)}) copy-start(s32[8]{0:T(128)} %param.31) | copy-start | bytes 100
  322.6 4.3 %copy-start.1 = (bf16[512,256]{1,0:T(8,128)(2,1)S(1)}, bf16[512,256]{1,0:T(8,128)(2,1)}, u32[]{:S(2)}) copy-start(bf16[512,256]{1,0:T(8,128)(2,1)} %param.24) | copy-start | bytes 786436
  322.6 53.5 %copy-start.6 = (f32[256]{0:T(256)S(1)}, f32[256]{0:T(256)}, u32[]{:S(2)}) copy-start(f32[256]{0:T(256)} %param.23) | copy-start | bytes 3076
  322.6 56.8 %all-to-all-start.2 = ((bf16[2,256,2880]{1,2,0:T(8,128)(2,1)}), bf16[2,256,2880]{1,2,0:T(8,128)(2,1)S(1)}, u32[]{:S(2)}, u32[]{:S(2)}) async-start(bf16[2,256,2880]{1,2,0:T(8,128)(2,1)} %bitcast.175), calls=%async_computation.2 | async-start | bytes 5898240 | tf_op jit(solution)/shard_map/all_to_all | solution.py:158
  379.5 8.6 %all-to-all-start.5 = ((bf16[2,128,512]{2,1,0:T(8,128)(2,1)}), bf16[2,128,512]{2,1,0:T(8,128)(2,1)S(1)}, u32[]{:S(2)}, u32[]{:S(2)}) async-start(bf16[2,128,512]{2,1,0:T(8,128)(2,1)} %bitcast.46), calls=%async_computation.5 | async-start | bytes 524288 | tf_op jit(solution)/shard_map/all_to_all | solution.py:159
Sparse Core Ops, SparseCore 0:
  224.5 34.4 all-gather.2
  260.6 33.1 all-gather.4
where the time goes:
time: 404 us; the launch traced here: 397 us
  local copies, waits for them, and re-layouts  138 us (34%)
  other arithmetic  84.4 us (21%)
  waiting for transfers between devices  49.4 us (12%)
  blocking collectives  48.3 us (12%)
  matrix products  35.5 us (9%)
  starting transfers between devices  27.6 us (7%)
  between operations  14.4 us (4%)
    slice x1, local copies, waits for them, and re-layouts, shards(): flux_tiles = atmosphere[0::2].reshape(flux_depth, atmos_count, 128)  64.7 us
    add x1, other arithmetic, shards(): combined = atmosphere.astype(jnp.float32) + smooth  44.3 us
    all_gather x1, blocking collectives, shards(): ocean_up_rows = lax.all_gather(ocean_up, 'chan', axis=0, tiled=True)  39.8 us
    all_to_all x1, waiting for transfers between devices, shards(): lax.all_to_all(flux_out.reshape(flux_depth, peer_count, flux_slots, 128),...  39.5 us
    dot_general x1, matrix products, shards(): lax.dot_general(down_rows, hidden, (((0,), (0,)), ((), ())), preferred_el...  18.5 us
    scatter-add x1, other arithmetic, shards(): combined.at[1::2].add(sea_atmos.reshape(flux_depth, lat_rows, lon_cells))  16.5 us
    mul x1, other arithmetic, shards(): padded.astype(jnp.float32) * row_keep.astype(jnp.float32)[None, :, None]  12.1 us
    dot_general x3, matrix products, add_group(): jnp.einsum('kgi,gij->kgj', picked, weights, preferred_element_type=jnp.fl...  11.3 us
  transfers between devices with their start and end apart: 12, of which 3 were waited for; matrix products, arithmetic and copies ran while one was open for 56% of the time, Pallas kernels for 0%

commit v1 on v0

--- a/solution.py
+++ b/solution.py
@@ -1,8 +1,11 @@
+import functools
 import math
 
 import jax
 import jax.numpy as jnp
 from jax import lax
+from jax.experimental import pallas as pl
+from jax.experimental.pallas import tpu as pltpu
 from jax.sharding import PartitionSpec as P
 
 
@@ -161,6 +164,389 @@
     return (atmos_back.reshape(channels, lat_rows, lon_cells), ocean_back)
 
 
+SWAP = [(0, 1), (1, 0)]
+LIMIT = 56 * 1024 * 1024
+
+
+def vmem():
+    return pl.BlockSpec(memory_space=pltpu.VMEM)
+
+
+def smem():
+    return pl.BlockSpec(memory_space=pltpu.SMEM)
+
+
+def local_call(body, out_shape, operands, in_specs, out_specs, scratch=(), flops=0, moved=0, exps=0, aliases=None):
+    return pl.pallas_call(
+        body,
+        grid=(1,),
+        out_shape=out_shape,
+        in_specs=in_specs,
+        out_specs=out_specs,
+        scratch_shapes=list(scratch),
+        input_output_aliases=aliases or {},
+        compiler_params=pltpu.CompilerParams(vmem_limit_bytes=LIMIT),
+        cost_estimate=pl.CostEstimate(flops=flops, bytes_accessed=moved, transcendentals=exps),
+    )(*operands)
+
+
+def sea_pick_body(sends, ocean, out):
+    count, cap = sends.shape
+    for peer in range(count):
+        for slot in range(cap):
+            at = pl.multiple_of(sends[peer, slot] * 128, 128)
+            out[peer * cap + slot] = ocean[:, pl.ds(at, 128)]
+
+
+def flux_pick_body(sends, cells, pick, out, even):
+    count, cap = sends.shape
+    step = cells.shape[0] // 15
+    for block in range(15):
+        rows = pl.ds(block * step, step)
+        even[rows, :] = jnp.dot(
+            cells[rows, :], pick[...], preferred_element_type=jnp.float32
+        ).astype(jnp.bfloat16)
+
+    def one_peer(peer, carry):
+        for slot in range(cap):
+            at = pl.multiple_of(sends[peer, slot] * 128, 128)
+            out[peer * cap + slot] = even[pl.ds(at, 128), :]
+        return carry
+
+    lax.fori_loop(0, count, one_peer, 0)
+
+
+def sea_products_body(pattern, slots, blocks, spread, out, wide):
+    def widen(slot, carry):
+        wide[slot] = lax.dot_general(
+            slots[slot], spread[...], (((0,), (0,)), ((), ())), preferred_element_type=jnp.float32
+        ).astype(jnp.bfloat16)
+        return carry
+
+    lax.fori_loop(0, slots.shape[0], widen, 0, unroll=4)
+
+    def entry(index, carry):
+        out[index] = lax.dot_general(
+            blocks[pattern[index, 2]],
+            wide[pattern[index, 0]],
+            (((0,), (0,)), ((), ())),
+            preferred_element_type=jnp.float32,
+        )
+        return carry
+
+    lax.fori_loop(0, out.shape[0], entry, 0, unroll=4)
+
+
+def smooth_body(first_row, edge_low, edge_high, pattern, *refs):
+    rows, (sides, taps, sea, out, padded, total) = refs[:4], refs[4:]
+    cells = out.shape[1]
+    for place in range(4):
+        at_edge = (place == 0 and edge_low) or (place == 3 and edge_high)
+        for half in range(2):
+            lanes = slice(half * 128, half * 128 + 128)
+            padded[half, place, 8 : 8 + cells, :] = rows[place][0, 0:cells, lanes].astype(jnp.float32)
+            if at_edge:
+                pair = rows[place][0, cells : cells + 16, lanes].astype(jnp.float32)
+                left, right = pair[0:1], pair[1:2]
+            else:
+                at = 2 * (first_row - 1 + place)
+                pair = sides[:, lanes].astype(jnp.float32)
+                left, right = pair[at : at + 1], pair[at + 1 : at + 2]
+            padded[half, place, 7:8, :] = left
+            padded[half, place, 8 + cells : 9 + cells, :] = right
+    block = 80 if cells % 80 == 0 else 16
+    for half in range(2):
+        lanes = slice(half * 128, half * 128 + 128)
+        scale = [taps[k : k + 1, lanes] for k in range(9)]
+        for row in range(2):
+            for base in range(0, cells, block):
+                value = padded[half, row + 1, 8 + base : 8 + base + block, :] * (scale[4] + 1.0)
+                for k in (0, 1, 2, 3, 5, 6, 7, 8):
+                    start = 7 + base + k % 3
+                    value = value + scale[k] * padded[half, row + k // 3, start : start + block, :]
+                start = 128 + row * cells + base
+                total[start : start + block, lanes] = value
+    span = 2 * cells
+    for entry in range(sea.shape[0]):
+        start = pattern[entry, 1] * 128 - first_row * cells + 128
+
+        @pl.when((start > 0) & (start < span + 128))
+        def _():
+            where = pl.ds(pl.multiple_of(start, 16), 128)
+            total[where, :] = total[where, :] + sea[entry]
+
+    for row in range(2):
+        out[row] = total[128 + row * cells : 128 + (row + 1) * cells, :].astype(jnp.bfloat16)
+
+
+def gelu(v):
+    inner = v * (0.7978845608028654 + 0.035677408136300125 * (v * v))
+    half = 0.5 * v
+    return half + half * jnp.tanh(inner)
+
+
+def atmos_layer_body(chan, own, other, gain, up, down, *refs):
+    pieces, out = refs[:4], refs[-1]
+    width = own.shape[2]
+    mine = pl.ds(pl.multiple_of(chan[0] * width, 128), width)
+    theirs = pl.ds(pl.multiple_of((1 - chan[0]) * width, 128), width)
+    depth = pieces[0].shape[0] * 4 // 5
+    gain_mine, gain_theirs = gain[:, mine], gain[:, theirs]
+    cells = own.shape[1]
+    step = 360 if cells % 360 == 0 and 360 % 8 == 0 else 16
+    step = 240
+
+    def rows_step(index, carry):
+        row = index // (cells // step)
+        at = pl.ds(pl.multiple_of((index % (cells // step)) * step, 16), step)
+        a = own[row, at, :].astype(jnp.float32)
+        b = other[row, at, :].astype(jnp.float32)
+        squares = jnp.sum(a * a + b * b, axis=1, keepdims=True)
+        inverse = lax.rsqrt(squares * (1.0 / (2 * width)) + 1e-06)
+        na = (a * inverse * gain_mine).astype(jnp.bfloat16)
+        nb = (b * inverse * gain_theirs).astype(jnp.bfloat16)
+        total = a
+        nt = (((1,), (1,)), ((), ()))
+        for part in range(8):
+            if part < 4:
+                where = slice(part * depth, (part + 1) * depth)
+                ua, ub, d = up[where, mine], up[where, theirs], down[where, mine]
+            else:
+                piece = pieces[part - 4]
+                ua, ub = piece[0:depth, mine], piece[0:depth, theirs]
+                d = piece[0:depth, 2 * width : 3 * width]
+            v = lax.dot_general(na, ua, nt, preferred_element_type=jnp.float32)
+            v = v + lax.dot_general(nb, ub, nt, preferred_element_type=jnp.float32)
+            hidden = gelu(v).astype(jnp.bfloat16)
+            total = total + jnp.dot(hidden, d, preferred_element_type=jnp.float32)
+        out[row, at, :] = total.astype(jnp.bfloat16)
+        return carry
+
+    lax.fori_loop(0, own.shape[0] * (cells // step), rows_step, 0)
+
+
+def flux_remap_body(pattern, slots, blocks, ocean, out, total):
+    total[...] = jnp.zeros_like(total)
+
+    def entry(index, carry):
+        tile = pattern[index, 1]
+        total[tile] = total[tile] + lax.dot_general(
+            slots[pattern[index, 0]],
+            blocks[pattern[index, 2]],
+            (((0,), (0,)), ((), ())),
+            preferred_element_type=jnp.float32,
+        )
+        return carry
+
+    lax.fori_loop(0, pattern.shape[0], entry, 0, unroll=8)
+    for tile in range(total.shape[0]):
+        lanes = slice(tile * 128, tile * 128 + 128)
+        out[:, lanes] = (ocean[:, lanes].astype(jnp.float32) + 0.125 * total[tile]).astype(jnp.bfloat16)
+
+
+def ocean_layer_body(chan, mask, own, other, gain, up, down, *refs):
+    pieces, out = refs[:4], refs[-1]
+    width = own.shape[0]
+    mine = pl.ds(pl.multiple_of(chan[0] * width, 128), width)
+    theirs = pl.ds(pl.multiple_of((1 - chan[0]) * width, 128), width)
+    depth = pieces[0].shape[0] // 5
+    top = 4 * depth
+    gain_mine, gain_theirs = gain[mine, :], gain[theirs, :]
+    a = own[...].astype(jnp.float32)
+    b = other[...].astype(jnp.float32)
+    squares = jnp.sum(a * a + b * b, axis=0, keepdims=True)
+    inverse = lax.rsqrt(squares * (1.0 / (2 * width)) + 1e-06)
+    na = (a * inverse * gain_mine).astype(jnp.bfloat16)
+    nb = (b * inverse * gain_theirs).astype(jnp.bfloat16)
+    ups, downs = [(up[:, mine], up[:, theirs])], [down[:, mine]]
+    for piece in pieces:
+        for side in range(2):
+            base = side * 3 * width
+            left = piece[top:, pl.ds(pl.multiple_of(base + chan[0] * width, 128), width)]
+            right = piece[top:, pl.ds(pl.multiple_of(base + (1 - chan[0]) * width, 128), width)]
+            ups.append((left, right))
+            downs.append(piece[top:, base + 2 * width : base + 3 * width])
+    total = jnp.zeros_like(a)
+    for (ua, ub), d in zip(ups, downs):
+        v = jnp.dot(ua, na, preferred_element_type=jnp.float32)
+        v = v + jnp.dot(ub, nb, preferred_element_type=jnp.float32)
+        hidden = gelu(v).astype(jnp.bfloat16)
+        total = total + lax.dot_general(
+            d, hidden, (((0,), (0,)), ((), ())), preferred_element_type=jnp.float32
+        )
+    for tile in range(mask.shape[0]):
+        lanes = slice(tile * 128, tile * 128 + 128)
+        keep = mask[tile].astype(jnp.float32)
+        out[:, lanes] = (a[:, lanes] + keep * total[:, lanes]).astype(jnp.bfloat16)
+
+
+def far_weights(up, down, ocean_up, ocean_down):
+    chan = lax.axis_index("chan")
+    quarter = lax.axis_index("groups") * 2 + lax.axis_index("pair")
+    depth, shallow = up.shape[0] // 4, ocean_up.shape[0] // 4
+    width, narrow = up.shape[1] // 2, ocean_up.shape[1] // 2
+    first = lax.dynamic_slice(up, (quarter * depth, 0), (depth, 2 * width))
+    second = lax.dynamic_slice(down, (quarter * depth, (1 - chan) * width), (depth, width))
+    third = lax.dynamic_slice(ocean_up, (quarter * shallow, 0), (shallow, 2 * narrow))
+    fourth = lax.dynamic_slice(ocean_down, (quarter * shallow, (1 - chan) * narrow), (shallow, narrow))
+    low = jnp.concatenate([third, fourth], axis=1)
+    low = jnp.concatenate([low[: shallow // 2], low[shallow // 2 :]], axis=1)
+    packed = jnp.concatenate([jnp.concatenate([first, second], axis=1), low], axis=0)
+    one = lax.ppermute(packed, "chan", SWAP)
+    two = lax.ppermute(one, "groups", SWAP)
+    return one, two, lax.ppermute(one, "pair", SWAP), lax.ppermute(two, "pair", SWAP)
+
+
+def quick_shards(
+    atmosphere,
+    ocean_state,
+    conv_taps,
+    atmos_gain,
+    atmos_up,
+    atmos_down,
+    ocean_gain,
+    ocean_up,
+    ocean_down,
+    remap_blocks,
+    flux_sends,
+    flux_pattern,
+    sea_sends,
+    sea_pattern,
+    ocean_mask,
+):
+    bf16, f32 = jnp.bfloat16, jnp.float32
+    channels, lat_rows, lon_cells = atmosphere.shape
+    flux_depth, ocean_cells = ocean_state.shape
+    ocean_count = ocean_cells // 128
+    lat_bands = lax.axis_size("lat")
+    peers = ("lat", "pair")
+    chan = lax.axis_index("chan").reshape(1)
+    field = atmosphere.transpose(1, 2, 0)
+    pick = (jnp.arange(channels)[:, None] == 2 * jnp.arange(flux_depth)[None, :]).astype(bf16)
+    spread = (2 * jnp.arange(flux_depth)[:, None] + 1 == jnp.arange(channels)[None, :]).astype(bf16)
+
+    sends = sea_sends[0]
+    sea_out = local_call(
+        sea_pick_body,
+        jax.ShapeDtypeStruct((sends.size, flux_depth, 128), bf16),
+        (sends, ocean_state),
+        [smem(), vmem()],
+        vmem(),
+        moved=2**20,
+    )
+    sea_in = lax.all_to_all(sea_out, peers, split_axis=0, concat_axis=0, tiled=True)
+
+    sides = jnp.stack([field[:, lon_cells - 1, :], field[:, 0, :]], axis=1).reshape(2 * lat_rows, channels)
+    sides = lax.ppermute(sides, "pair", SWAP)
+
+    pieces = far_weights(atmos_up, atmos_down, ocean_up, ocean_down)
+
+    fill = jnp.zeros((14, channels), bf16)
+    up_chain = [(i, i + 1) for i in range(lat_bands - 1)]
+    down_chain = [(i + 1, i) for i in range(lat_bands - 1)]
+    low = lax.ppermute(jnp.concatenate([field[lat_rows - 1], sides[-2:], fill], axis=0), "lat", up_chain)
+    high = lax.ppermute(jnp.concatenate([field[0], sides[:2], fill], axis=0), "lat", down_chain)
+
+    sends = flux_sends[0]
+    flux_out = local_call(
+        flux_pick_body,
+        jax.ShapeDtypeStruct((sends.size, 128, flux_depth), bf16),
+        (sends, field.reshape(lat_rows * lon_cells, channels), pick),
+        [smem(), vmem(), vmem()],
+        vmem(),
+        scratch=[pltpu.VMEM((lat_rows * lon_cells, flux_depth), bf16)],
+        flops=2 * lat_rows * lon_cells * channels * flux_depth,
+        moved=6 * 2**20,
+    )
+    flux_in = lax.all_to_all(flux_out, peers, split_axis=0, concat_axis=0, tiled=True)
+
+    pattern = sea_pattern[0]
+    sea = local_call(
+        sea_products_body,
+        jax.ShapeDtypeStruct((pattern.shape[0], 128, channels), f32),
+        (pattern, sea_in, remap_blocks, spread),
+        [smem(), vmem(), vmem(), vmem()],
+        vmem(),
+        scratch=[pltpu.VMEM((sea_in.shape[0], 128, channels), bf16)],
+        flops=2 * pattern.shape[0] * 128 * 128 * channels,
+        moved=4 * 2**20,
+    )
+    taps = conv_taps.T.astype(f32)
+
+    def smooth_rows(first):
+        operands, specs = [], []
+        for row in range(first - 1, first + 3):
+            if row < 0 or row >= lat_rows:
+                operands.append((low if row < 0 else high)[None])
+                specs.append(vmem())
+            else:
+                operands.append(field)
+                specs.append(pl.BlockSpec((1, lon_cells, channels), lambda _, row=row: (row, 0, 0)))
+        return local_call(
+            functools.partial(smooth_body, first, first == 0, first + 2 == lat_rows),
+            jax.ShapeDtypeStruct((2, lon_cells, channels), bf16),
+            (pattern, *operands, sides, taps, sea),
+            [smem(), *specs, vmem(), vmem(), vmem()],
+            vmem(),
+            scratch=[
+                pltpu.VMEM((2, 4, lon_cells + 16, 128), f32),
+                pltpu.VMEM((2 * lon_cells + 256, channels), f32),
+            ],
+            flops=36 * lon_cells * channels,
+            moved=5 * 2**20,
+        )
+
+    order = [2, 4, 0, 6]
+    inputs = [smooth_rows(first) for first in order]
+    others = [lax.ppermute(value, "chan", SWAP) for value in inputs]
+
+    pattern = flux_pattern[0]
+    ocean_input = local_call(
+        flux_remap_body,
+        jax.ShapeDtypeStruct((flux_depth, ocean_cells), bf16),
+        (pattern, flux_in, remap_blocks, ocean_state),
+        [smem(), vmem(), vmem(), vmem()],
+        vmem(),
+        scratch=[pltpu.VMEM((ocean_count, flux_depth, 128), f32)],
+        flops=2 * pattern.shape[0] * 128 * 128 * flux_depth,
+        moved=5 * 2**20,
+    )
+    ocean_other = lax.ppermute(ocean_input, "chan", SWAP)
+
+    result = None
+    gain = atmos_gain.reshape(1, -1)
+    for first, own, other in zip(order, inputs, others):
+        operands = [chan, own, other, gain, atmos_up, atmos_down, *pieces]
+        specs = [smem()] + [vmem()] * (len(operands) - 1)
+        aliases = {}
+        if result is not None:
+            aliases = {len(operands): 0}
+            operands.append(result)
+            specs.append(pl.BlockSpec(memory_space=pl.ANY))
+        result = local_call(
+            atmos_layer_body,
+            jax.ShapeDtypeStruct((lat_rows, lon_cells, channels), bf16),
+            operands,
+            specs,
+            pl.BlockSpec((2, lon_cells, channels), lambda _, first=first: (first // 2, 0, 0)),
+            flops=2 * 2 * lon_cells * 3 * channels * 2 * atmos_up.shape[0],
+            moved=8 * 2**20,
+            exps=2 * lon_cells * 2 * atmos_up.shape[0],
+            aliases=aliases,
+        )
+    ocean_next = local_call(
+        ocean_layer_body,
+        jax.ShapeDtypeStruct((flux_depth, ocean_cells), bf16),
+        (chan, ocean_mask, ocean_input, ocean_other, ocean_gain.reshape(-1, 1), ocean_up, ocean_down, *pieces),
+        [smem(), smem()] + [vmem()] * 9,
+        vmem(),
+        flops=2 * ocean_cells * 3 * flux_depth * 2 * ocean_up.shape[0],
+        moved=4 * 2**20,
+        exps=ocean_cells * 2 * ocean_up.shape[0],
+    )
+    return result.transpose(2, 0, 1), ocean_next
+
+
 def solution(mesh):
     in_specs = (
         P("chan", ("groups", "lat"), "pair"),
@@ -180,4 +566,6 @@
         P(("lat", "pair")),
     )
     out_specs = (P("chan", ("groups", "lat"), "pair"), P("chan", ("groups", "lat", "pair")))
-    return jax.shard_map(shards, mesh=mesh, in_specs=in_specs, out_specs=out_specs, check_vma=False)
+    paired = all(mesh.shape[axis] == 2 for axis in ("groups", "chan", "pair"))
+    body = quick_shards if paired else shards
+    return jax.shard_map(body, mesh=mesh, in_specs=in_specs, out_specs=out_specs, check_vma=False)

time: 404 us -> 158 us (0.39); the launches traced: 397 us -> 157 us
  local copies, waits for them, and re-layouts: 138 us -> 11.9 us
  Pallas kernels: 0 us -> 90.2 us
  other arithmetic: 84.4 us -> 3.79 us
  blocking collectives: 48.3 us -> 0 us
  matrix products: 35.5 us -> 0 us
  waiting for transfers between devices: 49.4 us -> 24.7 us
  between operations: 14.4 us -> 0.79 us
    pallas_call x0 -> x13, Pallas kernels: none -> 90.2 us  [local_call(): pl.pallas_call(body, grid=(1,), out_shape=out_shape, in_specs=in_specs, o...]
    slice x5 -> x2, local copies, waits for them, and re-layouts: 71.2 us -> 0.8 us  [the longest x1 0.79 us: quick_shards(): field[:, lon_cells - 1, :]]
    all_gather x2 -> x0, blocking collectives: 48.3 us -> none  [the longest x1 39.8 us: shards(): ocean_up_rows = lax.all_gather(ocean_up, 'chan', axis=0, tiled=True)]
    all_to_all x6 -> x2, waiting for transfers between devices: 44.6 us -> 0.01 us  [the longest x1 0.01 us: quick_shards(): lax.all_to_all(sea_out, peers, split_axis=0, concat_axis=0, tiled=True)]
    add x2 -> x1, other arithmetic: 44.3 us -> 0.01 us  [quick_shards(): 2 * jnp.arange(flux_depth)[:, None] + 1 == jnp.arange(channels)[None, :]]
    dot_general x8 -> x0, matrix products: 35.5 us -> none  [the longest x1 18.5 us: shards(): lax.dot_general(down_rows, hidden, (((0,), (0,)), ((), ())), preferred_el...]
    gather x9 -> x0, local copies, waits for them, and re-layouts: 24.6 us -> none  [the longest x3 10.5 us: add_group(): weights = jnp.take(blocks, entry_rows[:, 2], axis=0)]
    ppermute x4 -> x12, waiting for transfers between devices: 3.55 us -> 24.7 us  [the longest x1 16.7 us: quick_shards(): lax.ppermute(jnp.concatenate([field[lat_rows - 1], sides[-2:], fill], axi...]
  transfers between devices with their start and end apart: 12 -> 14, of which waited for: 3 -> 2; matrix products, arithmetic and copies ran while one was open for 56% -> 7% of each run, Pallas kernels for 0% -> 52%
where the time goes in v1:
time: 158 us; the launch traced here: 157 us
  Pallas kernels  90.2 us (57%)
  starting transfers between devices  26 us (16%)
  waiting for transfers between devices  24.7 us (16%)
  local copies, waits for them, and re-layouts  11.9 us (8%)
  other arithmetic  3.79 us (2%)
    pallas_call x13, Pallas kernels, local_call(): pl.pallas_call(body, grid=(1,), out_shape=out_shape, in_specs=in_specs, o...  90.2 us
    ppermute x1, waiting for transfers between devices, quick_shards(): lax.ppermute(jnp.concatenate([field[lat_rows - 1], sides[-2:], fill], axi...  16.7 us
    ppermute x1, waiting for transfers between devices, far_weights(): one = lax.ppermute(packed, 'chan', SWAP)  7.94 us
    all_to_all x1, starting transfers between devices, quick_shards(): lax.all_to_all(flux_out, peers, split_axis=0, concat_axis=0, tiled=True)  5.62 us
    all_to_all x1, starting transfers between devices, quick_shards(): lax.all_to_all(sea_out, peers, split_axis=0, concat_axis=0, tiled=True)  5.21 us
    ppermute x4, starting transfers between devices, quick_shards(): others = [lax.ppermute(value, 'chan', SWAP) for value in inputs]  5.03 us
    unnamed x25, local copies, waits for them, and re-layouts  4.48 us
    ppermute x1, starting transfers between devices, quick_shards(): lax.ppermute(jnp.concatenate([field[lat_rows - 1], sides[-2:], fill], axi...  3.38 us
  transfers between devices with their start and end apart: 14, of which 2 were waited for; matrix products, arithmetic and copies ran while one was open for 7% of the time, Pallas kernels for 52%

profile of v1, /device:TPU:16, one launch (start us, length us, event | category | flops | bytes accessed | tf_op | source)
XLA Modules:
  0.0 157.4 jit_solution(7821794178758242880)
XLA Ops:
  0.6 1.3 copy.27.sends
  2.0 1.7 %shard_map.158 = bf16[8,128,128]{2,1,0:T(8,128)(2,1)} custom-call(s32[8,1]{1,0:T(8,128)} %copy.27.sends, bf16[128,1024]{1,0:T(8,128)(2,1)} %ocean.3), custom_call_target="tpu_custom_call" | custom-call | bytes 1048576 | tf_op jit(solution)/shard_map/pallas_call | solution.py:180
  3.7 5.2 %all-to-all-start = ((bf16[8,128,128]{2,1,0:T(8,128)(2,1)}), bf16[8,128,128]{2,1,0:T(8,128)(2,1)S(1)}, u32[]{:S(2)}, u32[]{:S(2)}) async-start(bf16[8,128,128]{2,1,0:T(8,128)(2,1)} %shard_map.158), calls=%async_computation | async-start | bytes 524288 | tf_op jit(solution)/shard_map/all_to_all | solution.py:437
  10.3 4.3 %shard_map.168 = bf16[64,128,128]{2,1,0:T(8,128)(2,1)} custom-call(s32[8,8]{1,0:T(8,128)} %bitcast.43, bf16[5760,256]{1,0:T(8,128)(2,1)} %bitcast.19, bf16[256,128]{1,0:T(8,128)(2,1)} %fusion.9.pick), custom_call_target="tpu_custom_call" | custom-call | flops 377487360 | bytes 6291456 | tf_op jit(solution)/shard_map/pallas_call | solution.py:180
  14.6 0.9 constant_dynamic-slice_fusion
  15.5 1.0 constant_dynamic-slice_fusion.1
  16.5 5.6 %all-to-all-start.1 = ((bf16[64,128,128]{2,1,0:T(8,128)(2,1)}), bf16[64,128,128]{2,1,0:T(8,128)(2,1)S(1)}, u32[]{:S(2)}, u32[]{:S(2)}) async-start(bf16[64,128,128]{2,1,0:T(8,128)(2,1)} %shard_map.168), calls=%async_computation.1 | async-start | bytes 4194304 | tf_op jit(solution)/shard_map/all_to_all | solution.py:461
  22.2 0.8 fusion.7
  23.0 1.5 collective-permute-start.3
  26.1 1.1 slice_bitcast_fusion
  28.6 7.9 %collective-permute-done.3.refs_0_ = bf16[320,768]{1,0:T(8,128)(2,1)} collective-permute-done((bf16[320,768]{1,0:T(8,128)(2,1)}, bf16[320,768]{1,0:T(8,128)(2,1)}, u32[]{:S(2)}, u32[]{:S(2)}) %collective-permute-start.3) | collective-permute-done | bytes 491552 | tf_op jit(solution)/shard_map/ppermute | solution.py:395
  36.6 1.5 collective-permute-start.4
  38.1 4.4 %shard_map.159.refs_6_ = f32[16,128,256]{2,1,0:T(8,128)} custom-call(s32[16,3]{1,0:T(8,128)} %bitcast.37, bf16[8,128,128]{2,1,0:T(8,128)(2,1)} %copy-done.1, bf16[64,128,128]{2,1,0:T(8,128)(2,1)} %blocks.3, bf16[128,256]{1,0:T(8,128)(2,1)} %fusion.8.spread), custom_call_target="tpu_custom_call" | custom-call | flops 134217728 | bytes 4194304 | tf_op jit(solution)/shard_map/pallas_call | solution.py:180
  42.6 4.3 %shard_map.163.own = bf16[2,720,256]{2,1,0:T(8,128)(2,1)} custom-call(s32[16,3]{1,0:T(8,128)} %bitcast.38, bf16[8,720,256]{2,1,0:T(8,128)(2,1)} %bitcast.22, bf16[8,720,256]{2,1,0:T(8,128)(2,1)} %bitcast.23, bf16[8,720,256]{2,1,0:T(8,128)(2,1)} %bitcast.24, bf16[8,720,256]{2,1,0:T(8,128)(2,1)} %bitcast.25, bf16[16,256]{1,0:T(8,128)(2,1)} %copy-done.6, ...), custom_call_target="tpu_custom_call" | custom-call | flops 6635520 | bytes 5242880 | tf_op jit(solution)/shard_map/pallas_call | solution.py:180
  46.8 1.5 collective-permute-start.10
  48.3 1.0 maximum_maximum_fusion.1
  49.3 3.4 %collective-permute-start.7 = (bf16[736,256]{1,0:T(8,128)(2,1)S(1)}, bf16[736,256]{1,0:T(8,128)(2,1)S(1)}, u32[]{:S(2)}, u32[]{:S(2)}) collective-permute-start(bf16[736,256]{1,0:T(8,128)(2,1)S(1)} %get-tuple-element.8), channel_id=1, source_target_pairs={{0,4},{4,8},{8,12},{1,5},{5,9},{9,13},{2,6},{6,10},{10,14},{3,7},{... | collective-permute-start | bytes 1130504 | tf_op jit(solution)/shard_map/ppermute | solution.py:447
  53.3 2.6 %collective-permute-start.1 = (bf16[736,256]{1,0:T(8,128)(2,1)}, bf16[736,256]{1,0:T(8,128)(2,1)}, u32[]{:S(2)}, u32[]{:S(2)}) collective-permute-start(bf16[736,256]{1,0:T(8,128)(2,1)} %get-tuple-element.9), channel_id=1, source_target_pairs={{4,0},{8,4},{12,8},{5,1},{9,5},{13,9},{6,2},{10,6},{14,10},{7,3},{... | collective-permute-start | bytes 1130504 | tf_op jit(solution)/shard_map/ppermute | solution.py:448
  55.9 4.2 %shard_map.162.own = bf16[2,720,256]{2,1,0:T(8,128)(2,1)} custom-call(s32[16,3]{1,0:T(8,128)} %bitcast.39, bf16[8,720,256]{2,1,0:T(8,128)(2,1)} %bitcast.26, bf16[8,720,256]{2,1,0:T(8,128)(2,1)} %bitcast.27, bf16[8,720,256]{2,1,0:T(8,128)(2,1)} %bitcast.28, bf16[8,720,256]{2,1,0:T(8,128)(2,1)} %bitcast.29, bf16[16,256]{1,0:T(8,128)(2,1)} %copy-done.6, ...), custom_call_target="tpu_custom_call" | custom-call | flops 6635520 | bytes 5242880 | tf_op jit(solution)/shard_map/pallas_call | solution.py:180
  60.1 16.7 %collective-permute-done.7 = bf16[736,256]{1,0:T(8,128)(2,1)S(1)} collective-permute-done((bf16[736,256]{1,0:T(8,128)(2,1)S(1)}, bf16[736,256]{1,0:T(8,128)(2,1)S(1)}, u32[]{:S(2)}, u32[]{:S(2)}) %collective-permute-start.7) | collective-permute-done | bytes 376864 | tf_op jit(solution)/shard_map/ppermute | solution.py:447
  76.8 1.4 collective-permute-start.9
  79.8 4.3 %shard_map.161.own = bf16[2,720,256]{2,1,0:T(8,128)(2,1)} custom-call(s32[16,3]{1,0:T(8,128)} %bitcast.40, bf16[1,736,256]{2,1,0:T(8,128)(2,1)} %bitcast.36, bf16[8,720,256]{2,1,0:T(8,128)(2,1)} %bitcast.30, bf16[8,720,256]{2,1,0:T(8,128)(2,1)} %bitcast.31, bf16[8,720,256]{2,1,0:T(8,128)(2,1)} %bitcast.32, bf16[16,256]{1,0:T(8,128)(2,1)} %copy-done.6, ...), custom_call_target="tpu_custom_call" | custom-call | flops 6635520 | bytes 5242880 | tf_op jit(solution)/shard_map/pallas_call | solution.py:180
  84.6 4.5 %shard_map.160.own = bf16[2,720,256]{2,1,0:T(8,128)(2,1)} custom-call(s32[16,3]{1,0:T(8,128)} %bitcast.41, bf16[8,720,256]{2,1,0:T(8,128)(2,1)} %bitcast.33, bf16[8,720,256]{2,1,0:T(8,128)(2,1)} %bitcast.34, bf16[8,720,256]{2,1,0:T(8,128)(2,1)} %bitcast.35, bf16[1,736,256]{2,1,0:T(8,128)(2,1)} %bitcast.4.refs_3_, bf16[16,256]{1,0:T(8,128)(2,1)} %copy-done.6, ...), custom_call_target="tpu_custom_call" | custom-call | flops 6635520 | bytes 5242880 | tf_op jit(solution)/shard_map/pallas_call | solution.py:180
  89.1 1.5 collective-permute-start.2
  91.4 12.2 %shard_map.164.refs_4_ = bf16[8,720,256]{2,1,0:T(8,128)(2,1)} custom-call(s32[1]{0:T(128)} %bitcast.chan, bf16[2,720,256]{2,1,0:T(8,128)(2,1)} %shard_map.163.own, bf16[2,720,256]{2,1,0:T(8,128)(2,1)} %collective-permute-done.10.other, f32[1,512]{1,0:T(1,128)} %bitcast.46, bf16[1024,512]{1,0:T(8,128)(2,1)} %up.8, bf16[1024,512]{1,0:T(8,128)(2,1)} %down.8, ...), custom_call_target="tpu_custom_call" | custom-call | flops 4529848320 | bytes 8388608 | tf_op jit(solution)/shard_map/pallas_call | solution.py:180
  103.6 12.2 %shard_map.165.refs_4_ = bf16[8,720,256]{2,1,0:T(8,128)(2,1)} custom-call(s32[1]{0:T(128)} %bitcast.chan, bf16[2,720,256]{2,1,0:T(8,128)(2,1)} %shard_map.162.own, bf16[2,720,256]{2,1,0:T(8,128)(2,1)} %collective-permute-done.9.other, f32[1,512]{1,0:T(1,128)} %bitcast.47, bf16[1024,512]{1,0:T(8,128)(2,1)} %up.8, ...), custom_call_target="tpu_custom_call", output_to_operand_aliasing={{}: (10, {})} | custom-call | flops 4529848320 | bytes 8388608 | tf_op jit(solution)/shard_map/pallas_call | solution.py:180
  115.9 0.9 copy-done.11
  116.7 12.2 %shard_map.166.refs_4_ = bf16[8,720,256]{2,1,0:T(8,128)(2,1)} custom-call(s32[1]{0:T(128)} %bitcast.chan, bf16[2,720,256]{2,1,0:T(8,128)(2,1)} %shard_map.161.own, bf16[2,720,256]{2,1,0:T(8,128)(2,1)} %copy-done.11, f32[1,512]{1,0:T(1,128)} %bitcast.48, bf16[1024,512]{1,0:T(8,128)(2,1)} %up.8, ...), custom_call_target="tpu_custom_call", output_to_operand_aliasing={{}: (10, {})} | custom-call | flops 4529848320 | bytes 8388608 | tf_op jit(solution)/shard_map/pallas_call | solution.py:180
  128.9 1.4 copy-done
  130.3 7.4 %shard_map.169.own = bf16[128,1024]{1,0:T(8,128)(2,1)} custom-call(s32[128,3]{1,0:T(8,128)} %bitcast.42, bf16[64,128,128]{2,1,0:T(8,128)(2,1)} %copy-done, bf16[64,128,128]{2,1,0:T(8,128)(2,1)} %blocks.3, bf16[128,1024]{1,0:T(8,128)(2,1)} %ocean.3), custom_call_target="tpu_custom_call" | custom-call | flops 536870912 | bytes 5242880 | tf_op jit(solution)/shard_map/pallas_call | solution.py:180
  138.3 12.2 %shard_map.167 = bf16[8,720,256]{2,1,0:T(8,128)(2,1)} custom-call(s32[1]{0:T(128)} %bitcast.chan, bf16[2,720,256]{2,1,0:T(8,128)(2,1)} %shard_map.160.own, bf16[2,720,256]{2,1,0:T(8,128)(2,1)} %collective-permute-done.2.other, f32[1,512]{1,0:T(1,128)} %bitcast.49, bf16[1024,512]{1,0:T(8,128)(2,1)} %up.8, ...), custom_call_target="tpu_custom_call", output_to_operand_aliasing={{}: (10, {})} | custom-call | flops 4529848320 | bytes 8388608 | tf_op jit(solution)/shard_map/pallas_call | solution.py:180
  151.2 6.2 %shard_map.170 = bf16[128,1024]{1,0:T(8,128)(2,1)} custom-call(s32[1]{0:T(128)} %bitcast.chan, s32[8]{0:T(128)} %mask.1, bf16[128,1024]{1,0:T(8,128)(2,1)} %shard_map.169.own, bf16[128,1024]{1,0:T(8,128)(2,1)} %copy-done.5, f32[256,1]{1,0:T(8,128)} %copy.34.gain, bf16[512,256]{1,0:T(8,128)(2,1)} %up.9, bf16[512,256]{1,0:T(8,128)(2,1)} %down.9, ...), custom_call_target="tpu_custom_call" | custom-call | flops 805306368 | bytes 4194304 | tf_op jit(solution)/shard_map/pallas_call | solution.py:180
  (57 shorter events, 9.2 us)
Async XLA Ops:
  3.7 12.8 %all-to-all-start = ((bf16[8,128,128]{2,1,0:T(8,128)(2,1)}), bf16[8,128,128]{2,1,0:T(8,128)(2,1)S(1)}, u32[]{:S(2)}, u32[]{:S(2)}) async-start(bf16[8,128,128]{2,1,0:T(8,128)(2,1)} %shard_map.158), calls=%async_computation | async-start | bytes 524288 | tf_op jit(solution)/shard_map/all_to_all | solution.py:437
  14.6 7.5 %dynamic-slice-start = ((bf16[1024,512]{1,0:T(8,128)(2,1)}, s32[]{:T(128)}, s32[]{:T(128)}), bf16[256,256]{1,0:T(8,128)(2,1)S(1)}, s32[]{:S(2)}) async-start(bf16[1024,512]{1,0:T(8,128)(2,1)} %down.8, s32[]{:T(128)} %select_n.14, s32[]{:T(128)} %select_n.15), calls=%async_computation.2 | async-start | bytes 262656 | tf_op jit(solution)/shard_map/dynamic_slice | solution.py:389
  16.5 10.8 %copy-start.7 = (bf16[256,9]{0,1:T(8,128)(2,1)S(1)}, bf16[256,9]{0,1:T(8,128)(2,1)}, u32[]{:S(2)}) copy-start(bf16[256,9]{0,1:T(8,128)(2,1)} %param.17) | copy-start | bytes 13828
  16.5 11.4 %copy-start.8 = (s32[1,16,3]{1,0,2:T(1,128)S(1)}, s32[1,16,3]{1,0,2:T(1,128)}, u32[]{:S(2)}) copy-start(s32[1,16,3]{1,0,2:T(1,128)} %param.28) | copy-start | bytes 580
  16.5 10.7 %copy-start.1 = (bf16[8,128,128]{2,1,0:T(8,128)(2,1)}, bf16[8,128,128]{2,1,0:T(8,128)(2,1)S(1)}, u32[]{:S(2)}) copy-start(bf16[8,128,128]{2,1,0:T(8,128)(2,1)S(1)} %all-to-all-done.slots) | copy-start | bytes 786436
  16.5 112.4 %all-to-all-start.1 = ((bf16[64,128,128]{2,1,0:T(8,128)(2,1)}), bf16[64,128,128]{2,1,0:T(8,128)(2,1)S(1)}, u32[]{:S(2)}, u32[]{:S(2)}) async-start(bf16[64,128,128]{2,1,0:T(8,128)(2,1)} %shard_map.168), calls=%async_computation.1 | async-start | bytes 4194304 | tf_op jit(solution)/shard_map/all_to_all | solution.py:461
  23.0 13.6 %collective-permute-start.3 = (bf16[320,768]{1,0:T(8,128)(2,1)}, bf16[320,768]{1,0:T(8,128)(2,1)}, u32[]{:S(2)}, u32[]{:S(2)}) collective-permute-start(bf16[320,768]{1,0:T(8,128)(2,1)} %fusion.7), channel_id=1, source_target_pairs={{0,2},{2,0},{1,3},{3,1},{4,6},{6,4},{5,7},{7,5},{8,10},{10,8},{9,1... | collective-permute-start | bytes 1474568 | tf_op jit(solution)/shard_map/ppermute | solution.py:395
  25.3 12.8 %collective-permute-start = (bf16[16,256]{1,0:T(8,128)(2,1)S(1)}, bf16[16,256]{1,0:T(8,128)(2,1)S(1)}, u32[]{:S(2)}, u32[]{:S(2)}) collective-permute-start(bf16[16,256]{1,0:T(8,128)(2,1)S(1)} %reshape.32), channel_id=1, source_target_pairs={{0,1},{1,0},{2,3},{3,2},{4,5},{5,4},{6,7},{7,6},{8,9},{9,8},{10,11... | collective-permute-start | bytes 24584 | tf_op jit(solution)/shard_map/ppermute | solution.py:440
  36.6 16.2 %collective-permute-start.4 = (bf16[320,768]{1,0:T(8,128)(2,1)}, bf16[320,768]{1,0:T(8,128)(2,1)}, u32[]{:S(2)}, u32[]{:S(2)}) collective-permute-start(bf16[320,768]{1,0:T(8,128)(2,1)} %collective-permute-done.3.refs_0_), channel_id=1, source_target_pairs={{0,16},{16,0},{1,17},{17,1},{2,18},{18,2},{3,19},{19,3},{4,20},{20... | collective-permute-start | bytes 1474568 | tf_op jit(solution)/shard_map/ppermute | solution.py:396
  38.1 4.4 %copy-start.6 = (bf16[16,256]{1,0:T(8,128)(2,1)}, bf16[16,256]{1,0:T(8,128)(2,1)S(1)}, u32[]{:S(2)}) copy-start(bf16[16,256]{1,0:T(8,128)(2,1)S(1)} %collective-permute-done.refs_4_) | copy-start | bytes 24580
  46.8 43.8 %collective-permute-start.10 = (bf16[2,720,256]{2,1,0:T(8,128)(2,1)}, bf16[2,720,256]{2,1,0:T(8,128)(2,1)}, u32[]{:S(2)}, u32[]{:S(2)}) collective-permute-start(bf16[2,720,256]{2,1,0:T(8,128)(2,1)} %shard_map.163.own), channel_id=1, source_target_pairs={{0,2},{2,0},{1,3},{3,1},{4,6},{6,4},{5,7},{7,5},{8,10},{10,8},{9,1... | collective-permute-start | bytes 2211848 | tf_op jit(solution)/shard_map/ppermute | solution.py:501
  49.3 27.5 %collective-permute-start.7 = (bf16[736,256]{1,0:T(8,128)(2,1)S(1)}, bf16[736,256]{1,0:T(8,128)(2,1)S(1)}, u32[]{:S(2)}, u32[]{:S(2)}) collective-permute-start(bf16[736,256]{1,0:T(8,128)(2,1)S(1)} %get-tuple-element.8), channel_id=1, source_target_pairs={{0,4},{4,8},{8,12},{1,5},{5,9},{9,13},{2,6},{6,10},{10,14},{3,7},{... | collective-permute-start | bytes 1130504 | tf_op jit(solution)/shard_map/ppermute | solution.py:447
  52.7 36.4 %collective-permute-start.5 = (bf16[320,768]{1,0:T(8,128)(2,1)}, bf16[320,768]{1,0:T(8,128)(2,1)S(1)}, u32[]{:S(2)}, u32[]{:S(2)}) collective-permute-start(bf16[320,768]{1,0:T(8,128)(2,1)} %collective-permute-done.3.refs_0_), channel_id=1, source_target_pairs={{0,1},{1,0},{2,3},{3,2},{4,5},{5,4},{6,7},{7,6},{8,9},{9,8},{10,11... | collective-permute-start | bytes 1474568 | tf_op jit(solution)/shard_map/ppermute | solution.py:397
  52.8 37.8 %collective-permute-start.6 = (bf16[320,768]{1,0:T(8,128)(2,1)}, bf16[320,768]{1,0:T(8,128)(2,1)S(1)}, u32[]{:S(2)}, u32[]{:S(2)}) collective-permute-start(bf16[320,768]{1,0:T(8,128)(2,1)} %collective-permute-done.4.refs_1_), channel_id=1, source_target_pairs={{0,1},{1,0},{2,3},{3,2},{4,5},{5,4},{6,7},{7,6},{8,9},{9,8},{10,11... | collective-permute-start | bytes 1474568 | tf_op jit(solution)/shard_map/ppermute | solution.py:397
  53.3 25.0 %copy-start.9 = (s32[1,128,3]{1,0,2:T(1,128)S(1)}, s32[1,128,3]{1,0,2:T(1,128)}, u32[]{:S(2)}) copy-start(s32[1,128,3]{1,0,2:T(1,128)} %param.26) | copy-start | bytes 4612
  53.3 25.7 %copy-start.10 = (f32[256]{0:T(256)S(1)}, f32[256]{0:T(256)}, u32[]{:S(2)}) copy-start(f32[256]{0:T(256)} %param.21) | copy-start | bytes 3076
  53.3 30.8 %collective-permute-start.1 = (bf16[736,256]{1,0:T(8,128)(2,1)}, bf16[736,256]{1,0:T(8,128)(2,1)}, u32[]{:S(2)}, u32[]{:S(2)}) collective-permute-start(bf16[736,256]{1,0:T(8,128)(2,1)} %get-tuple-element.9), channel_id=1, source_target_pairs={{4,0},{8,4},{12,8},{5,1},{9,5},{13,9},{6,2},{10,6},{14,10},{7,3},{... | collective-permute-start | bytes 1130504 | tf_op jit(solution)/shard_map/ppermute | solution.py:448
  76.8 3.0 %copy-start.4 = (bf16[736,256]{1,0:T(8,128)(2,1)}, bf16[736,256]{1,0:T(8,128)(2,1)S(1)}, u32[]{:S(2)}) copy-start(bf16[736,256]{1,0:T(8,128)(2,1)S(1)} %collective-permute-done.7) | copy-start | bytes 1130500
  76.8 26.8 %collective-permute-start.9 = (bf16[2,720,256]{2,1,0:T(8,128)(2,1)}, bf16[2,720,256]{2,1,0:T(8,128)(2,1)}, u32[]{:S(2)}, u32[]{:S(2)}) collective-permute-start(bf16[2,720,256]{2,1,0:T(8,128)(2,1)} %shard_map.162.own), channel_id=1, source_target_pairs={{0,2},{2,0},{1,3},{3,1},{4,6},{6,4},{5,7},{7,5},{8,10},{10,8},{9,1... | collective-permute-start | bytes 2211848 | tf_op jit(solution)/shard_map/ppermute | solution.py:501
  84.0 31.8 %collective-permute-start.8 = (bf16[2,720,256]{2,1,0:T(8,128)(2,1)}, bf16[2,720,256]{2,1,0:T(8,128)(2,1)S(1)}, u32[]{:S(2)}, u32[]{:S(2)}) collective-permute-start(bf16[2,720,256]{2,1,0:T(8,128)(2,1)} %shard_map.161.own), channel_id=1, source_target_pairs={{0,2},{2,0},{1,3},{3,1},{4,6},{6,4},{5,7},{7,5},{8,10},{10,8},{9,1... | collective-permute-start | bytes 2211848 | tf_op jit(solution)/shard_map/ppermute | solution.py:501
  89.1 1.5 copy-start.2
  89.1 49.2 %collective-permute-start.2 = (bf16[2,720,256]{2,1,0:T(8,128)(2,1)}, bf16[2,720,256]{2,1,0:T(8,128)(2,1)}, u32[]{:S(2)}, u32[]{:S(2)}) collective-permute-start(bf16[2,720,256]{2,1,0:T(8,128)(2,1)} %shard_map.160.own), channel_id=1, source_target_pairs={{0,2},{2,0},{1,3},{3,1},{4,6},{6,4},{5,7},{7,5},{8,10},{10,8},{9,1... | collective-permute-start | bytes 2211848 | tf_op jit(solution)/shard_map/ppermute | solution.py:501
  90.6 0.8 copy-start.3
  115.8 0.9 copy-start.11
  128.9 1.4 copy-start
  137.7 12.8 %collective-permute-start.11 = (bf16[128,1024]{1,0:T(8,128)(2,1)}, bf16[128,1024]{1,0:T(8,128)(2,1)S(1)}, u32[]{:S(2)}, u32[]{:S(2)}) collective-permute-start(bf16[128,1024]{1,0:T(8,128)(2,1)} %shard_map.169.own), channel_id=1, source_target_pairs={{0,2},{2,0},{1,3},{3,1},{4,6},{6,4},{5,7},{7,5},{8,10},{10,8},{9,1... | collective-permute-start | bytes 786440 | tf_op jit(solution)/shard_map/ppermute | solution.py:514
  150.5 0.7 copy-start.5

commit v2 on v0

--- a/solution.py
+++ b/solution.py
@@ -1,8 +1,11 @@
+import functools
 import math
 
 import jax
 import jax.numpy as jnp
 from jax import lax
+from jax.experimental import pallas as pl
+from jax.experimental.pallas import tpu as pltpu
 from jax.sharding import PartitionSpec as P
 
 
@@ -161,6 +164,458 @@
     return (atmos_back.reshape(channels, lat_rows, lon_cells), ocean_back)
 
 
+SWAP = [(0, 1), (1, 0)]
+NT = (((1,), (1,)), ((), ()))
+TN = (((0,), (0,)), ((), ()))
+
+
+def vmem():
+    return pl.BlockSpec(memory_space=pltpu.VMEM)
+
+
+def smem():
+    return pl.BlockSpec(memory_space=pltpu.SMEM)
+
+
+def anywhere():
+    return pl.BlockSpec(memory_space=pl.ANY)
+
+
+def local_call(
+    body, out_shape, operands, in_specs, out_specs, limit, grid=1, scratch=(), flops=0, moved=0, exps=0, aliases=None
+):
+    return pl.pallas_call(
+        body,
+        grid=(grid,),
+        out_shape=out_shape,
+        in_specs=in_specs,
+        out_specs=out_specs,
+        scratch_shapes=list(scratch),
+        input_output_aliases=aliases or {},
+        compiler_params=pltpu.CompilerParams(vmem_limit_bytes=limit * 2**20),
+        cost_estimate=pl.CostEstimate(flops=flops, bytes_accessed=moved, transcendentals=exps),
+    )(*operands)
+
+
+def picker(channels, odd):
+    shape = (channels, channels // 2)
+    rows = lax.broadcasted_iota(jnp.int32, shape, 0)
+    return (rows == 2 * lax.broadcasted_iota(jnp.int32, shape, 1) + odd).astype(jnp.bfloat16)
+
+
+def weaver(channels):
+    shape = (channels, channels)
+    rows = lax.broadcasted_iota(jnp.int32, shape, 0)
+    half = channels // 2
+    target = jnp.where(rows < half, 2 * rows, 2 * (rows - half) + 1)
+    return (target == lax.broadcasted_iota(jnp.int32, shape, 1)).astype(jnp.bfloat16)
+
+
+def sea_pick_body(sends, ocean, out):
+    for entry in range(out.shape[0]):
+        at = pl.multiple_of(sends[0, 0, entry] * 128, 128)
+        out[entry] = ocean[:, pl.ds(at, 128)].T
+
+
+def flux_pick_body(sends, cells, out, even):
+    _, count, cap = sends.shape
+    take = picker(cells.shape[1], 0)
+
+    def one_tile(tile, carry):
+        at = pl.multiple_of(tile * 128, 128)
+        values = jnp.dot(cells[pl.ds(at, 128), :], take, preferred_element_type=jnp.float32)
+        even[tile] = values.T.astype(jnp.bfloat16)
+        return carry
+
+    lax.fori_loop(0, even.shape[0], one_tile, 0, unroll=5)
+
+    def one_peer(peer, carry):
+        for slot in range(cap):
+            out[peer * cap + slot] = even[sends[0, peer, slot]]
+        return carry
+
+    lax.fori_loop(0, count, one_peer, 0, unroll=2)
+
+
+def sea_products_body(pattern, slots, blocks, out):
+    def entry(index, carry):
+        out[index] = lax.dot_general(
+            blocks[pattern[2, 0, index]],
+            slots[pattern[0, 0, index]],
+            TN,
+            preferred_element_type=jnp.float32,
+        )
+        return carry
+
+    lax.fori_loop(0, out.shape[0], entry, 0, unroll=8)
+
+
+def smooth_body(odd, runs, with_sea, *refs):
+    places = sum(count + 2 for _, count, _ in runs)
+    rows, rest = refs[:places], refs[places:]
+    sides, taps = rest[:2]
+    pattern, sea = rest[2:4] if with_sea else (None, None)
+    outs = rest[4:-2] if with_sea else rest[2:-1]
+    padded = rest[-2] if with_sea else rest[-1]
+    total = rest[-1]
+    cells, channels = rows[0].shape[1], rows[0].shape[2]
+    cells = min(row.shape[1] for row in rows)
+    take = picker(channels, odd)
+    edges = jnp.dot(sides[...], take, preferred_element_type=jnp.float32)
+    scale = jnp.dot(taps[...], take, preferred_element_type=jnp.float32)
+    scale = [scale[k : k + 1] + (1.0 if k == 4 else 0.0) for k in range(9)]
+    place = 0
+    for run, (first, count, halos) in enumerate(runs):
+        span = count * cells
+        for step in range(count + 2):
+            row = first - 1 + step
+            values = jnp.dot(rows[place + step][0], take, preferred_element_type=jnp.float32)
+            if row in halos:
+                left, right = values[cells : cells + 1], values[cells + 1 : cells + 2]
+            else:
+                left, right = edges[2 * row : 2 * row + 1], edges[2 * row + 1 : 2 * row + 2]
+            padded[place + step, 8 : 8 + cells, :] = values[0:cells]
+            padded[place + step, 7:8, :] = left
+            padded[place + step, 8 + cells : 9 + cells, :] = right
+        block = 144 if cells % 144 == 0 else 16
+        for step in range(count):
+            for base in range(0, cells, block):
+                value = None
+                for k in range(9):
+                    start = 7 + base + k % 3
+                    term = scale[k] * padded[place + step + k // 3, start : start + block, :]
+                    value = term if value is None else value + term
+                start = step * cells + base
+                if with_sea:
+                    total[128 + start : 128 + start + block, :] = value
+                else:
+                    outs[run][start : start + block, :] = value.astype(jnp.bfloat16)
+        if with_sea:
+            for entry in range(sea.shape[0]):
+                start = pattern[1, 0, entry] * 128 - first * cells + 128
+
+                @pl.when((start > 0) & (start < span + 128))
+                def _():
+                    where = pl.ds(pl.multiple_of(start, 16), 128)
+                    total[where, :] = total[where, :] + sea[entry]
+
+            outs[run][...] = total[128 : 128 + span, :].astype(jnp.bfloat16)
+        place += count + 2
+
+
+def gelu(v):
+    inner = v * (0.7978845608028654 + 0.035677408136300125 * (v * v))
+    half = 0.5 * v
+    return half + half * jnp.tanh(inner)
+
+
+def gather_weights_body(chan, up, down, ocean_up, ocean_down, *refs):
+    pieces, (across, back, ocean_across, ocean_back) = refs[:4], refs[4:]
+    hidden, channels = up.shape
+    width = channels // 2
+    depth, shallow = hidden // 4, ocean_up.shape[0] // 4
+    narrow = ocean_down.shape[1] // 2
+    own = chan[0] * width
+    mine = pl.ds(pl.multiple_of(own, 128), width)
+    shape = (channels, channels)
+    rows = lax.broadcasted_iota(jnp.int32, shape, 0)
+    inside = rows % width
+    half = width // 2
+    target = jnp.where(inside < half, 2 * inside, 2 * (inside - half) + 1)
+    target = target + jnp.where(rows < width, own, width - own)
+    order = (target == lax.broadcasted_iota(jnp.int32, shape, 1)).astype(jnp.bfloat16)
+    for part in range(8):
+        at = slice(part * depth, (part + 1) * depth)
+        block = up[at, :] if part < 4 else pieces[part - 4][0:depth, 0:channels]
+        across[:, at] = lax.dot_general(
+            order, block, NT, preferred_element_type=jnp.float32
+        ).astype(jnp.bfloat16)
+        back[at, :] = down[at, mine] if part < 4 else pieces[part - 4][0:depth, channels : channels + width]
+    own = chan[0] * narrow
+    mine = pl.ds(pl.multiple_of(own, 128), narrow)
+    theirs = pl.ds(pl.multiple_of(narrow - own, 128), narrow)
+    count = ocean_up.shape[0]
+    ocean_across[0:count, 0:narrow] = ocean_up[:, mine]
+    ocean_across[0:count, narrow : 2 * narrow] = ocean_up[:, theirs]
+    ocean_back[0:count, :] = ocean_down[:, mine]
+    for part in range(4):
+        for side in range(2):
+            start = count + part * shallow + side * (shallow // 2)
+            at = slice(start, start + shallow // 2)
+            low = slice(depth, depth + shallow // 2)
+            base = side * 3 * narrow
+            left = pl.multiple_of(base + own, 128)
+            right = pl.multiple_of(base + narrow - own, 128)
+            ocean_across[at, 0:narrow] = pieces[part][low, pl.ds(left, narrow)]
+            ocean_across[at, narrow : 2 * narrow] = pieces[part][low, pl.ds(right, narrow)]
+            ocean_back[at, :] = pieces[part][low, base + 2 * narrow : base + 3 * narrow]
+
+
+def atmos_layer_body(own_even, own_odd, other_even, other_odd, gain, across, back, *refs):
+    out = refs[-1]
+    values = jnp.concatenate([own_even[...], own_odd[...], other_even[...], other_odd[...]], axis=1)
+    width = values.shape[1] // 2
+    wide = values.astype(jnp.float32)
+    squares = jnp.sum(wide * wide, axis=1, keepdims=True)
+    inverse = lax.rsqrt(squares * (1.0 / (2 * width)) + 1e-06)
+    normed = (wide * inverse * gain[...]).astype(jnp.bfloat16)
+    total = jnp.dot(values[:, 0:width], weaver(width), preferred_element_type=jnp.float32)
+    step = 256
+    for base in range(0, across.shape[1], step):
+        at = slice(base, base + step)
+        v = jnp.dot(normed, across[:, at], preferred_element_type=jnp.float32)
+        total = total + jnp.dot(gelu(v).astype(jnp.bfloat16), back[at, :], preferred_element_type=jnp.float32)
+    out[0] = total.astype(jnp.bfloat16)
+
+
+def flux_remap_body(pattern, slots, blocks, ocean, out, total):
+    total[...] = jnp.zeros_like(total)
+    group = math.gcd(pattern.shape[2], 8)
+
+    def entries(step, carry):
+        found = []
+        for index in range(group):
+            at = step * group + index
+            found.append(
+                jnp.dot(slots[pattern[0, 0, at]], blocks[pattern[2, 0, at]], preferred_element_type=jnp.float32)
+            )
+        for index in range(group):
+            tile = pattern[1, 0, step * group + index]
+            total[tile] = total[tile] + found[index]
+        return carry
+
+    lax.fori_loop(0, pattern.shape[2] // group, entries, 0)
+    for tile in range(total.shape[0]):
+        lanes = slice(tile * 128, tile * 128 + 128)
+        out[:, lanes] = (ocean[:, lanes].astype(jnp.float32) + 0.125 * total[tile]).astype(jnp.bfloat16)
+
+
+def ocean_layer_body(mask, own, other, gain, across, back, out):
+    width = own.shape[0]
+    square = (width, width)
+    tall = [jnp.broadcast_to(gain[:, k * width : (k + 1) * width], square).T for k in range(2)]
+    for tile in range(mask.shape[0]):
+        lanes = slice(tile * 128, tile * 128 + 128)
+        a = own[:, lanes].astype(jnp.float32)
+        b = other[:, lanes].astype(jnp.float32)
+        squares = jnp.sum(a * a + b * b, axis=0, keepdims=True)
+        inverse = lax.rsqrt(squares * (1.0 / (2 * width)) + 1e-06)
+        normed = jnp.concatenate([a * inverse * tall[0][:, 0:128], b * inverse * tall[1][:, 0:128]], axis=0)
+        v = jnp.dot(across[...], normed.astype(jnp.bfloat16), preferred_element_type=jnp.float32)
+        hidden = gelu(v).astype(jnp.bfloat16)
+        delta = lax.dot_general(back[...], hidden, TN, preferred_element_type=jnp.float32)
+        out[:, lanes] = (a + mask[tile].astype(jnp.float32) * delta).astype(jnp.bfloat16)
+
+
+def far_weights(up, down, ocean_up, ocean_down):
+    chan = lax.axis_index("chan")
+    quarter = lax.axis_index("groups") * 2 + lax.axis_index("pair")
+    depth, shallow = up.shape[0] // 4, ocean_up.shape[0] // 4
+    width, narrow = up.shape[1] // 2, ocean_up.shape[1] // 2
+    first = lax.dynamic_slice(up, (quarter * depth, 0), (depth, 2 * width))
+    second = lax.dynamic_slice(down, (quarter * depth, (1 - chan) * width), (depth, width))
+    third = lax.dynamic_slice(ocean_up, (quarter * shallow, 0), (shallow, 2 * narrow))
+    fourth = lax.dynamic_slice(ocean_down, (quarter * shallow, (1 - chan) * narrow), (shallow, narrow))
+    low = jnp.concatenate([third, fourth], axis=1)
+    low = jnp.concatenate([low[: shallow // 2], low[shallow // 2 :]], axis=1)
+    packed = jnp.concatenate([jnp.concatenate([first, second], axis=1), low], axis=0)
+    one = lax.ppermute(packed, "chan", SWAP)
+    two = lax.ppermute(one, "groups", SWAP)
+    return one, two, lax.ppermute(one, "pair", SWAP), lax.ppermute(two, "pair", SWAP)
+
+
+def quick_shards(
+    atmosphere,
+    ocean_state,
+    conv_taps,
+    atmos_gain,
+    atmos_up,
+    atmos_down,
+    ocean_gain,
+    ocean_up,
+    ocean_down,
+    remap_blocks,
+    flux_sends,
+    flux_pattern,
+    sea_sends,
+    sea_pattern,
+    ocean_mask,
+):
+    bf16, f32 = jnp.bfloat16, jnp.float32
+    channels, lat_rows, lon_cells = atmosphere.shape
+    flux_depth, ocean_cells = ocean_state.shape
+    ocean_count = ocean_cells // 128
+    hidden = 2 * atmos_up.shape[0]
+    ocean_hidden = 2 * ocean_up.shape[0]
+    lat_bands = lax.axis_size("lat")
+    peers = ("lat", "pair")
+    chan = lax.axis_index("chan").reshape(1)
+    field = atmosphere.transpose(1, 2, 0)
+    taps = conv_taps.T
+    sea_rows = sea_pattern.transpose(2, 0, 1)
+    flux_rows = flux_pattern.transpose(2, 0, 1)
+
+    sides = jnp.stack([field[:, lon_cells - 1, :], field[:, 0, :]], axis=1).reshape(2 * lat_rows, channels)
+    sides = lax.ppermute(sides, "pair", SWAP)
+    pieces = far_weights(atmos_up, atmos_down, ocean_up, ocean_down)
+
+    sea_out = local_call(
+        sea_pick_body,
+        jax.ShapeDtypeStruct((sea_sends.size, 128, flux_depth), bf16),
+        (sea_sends.reshape(1, 1, -1), ocean_state),
+        [smem(), vmem()],
+        vmem(),
+        8,
+        moved=2**20,
+    )
+    sea_in = lax.all_to_all(sea_out, peers, split_axis=0, concat_axis=0, tiled=True)
+
+    fill = jnp.zeros((14, channels), bf16)
+    up_chain = [(i, i + 1) for i in range(lat_bands - 1)]
+    down_chain = [(i + 1, i) for i in range(lat_bands - 1)]
+    low = lax.ppermute(jnp.concatenate([field[lat_rows - 1], sides[-2:], fill], axis=0), "lat", up_chain)
+    high = lax.ppermute(jnp.concatenate([field[0], sides[:2], fill], axis=0), "lat", down_chain)
+
+    flux_out = local_call(
+        flux_pick_body,
+        jax.ShapeDtypeStruct((flux_sends.size, flux_depth, 128), bf16),
+        (flux_sends, field.reshape(lat_rows * lon_cells, channels)),
+        [smem(), vmem()],
+        vmem(),
+        24,
+        scratch=[pltpu.VMEM((lat_rows * lon_cells // 128, flux_depth, 128), bf16)],
+        flops=2 * lat_rows * lon_cells * channels * flux_depth,
+        moved=6 * 2**20,
+    )
+    flux_in = lax.all_to_all(flux_out, peers, split_axis=0, concat_axis=0, tiled=True)
+
+    entries = sea_pattern.shape[1]
+    sea = local_call(
+        sea_products_body,
+        jax.ShapeDtypeStruct((entries, 128, flux_depth), f32),
+        (sea_rows, sea_in, remap_blocks),
+        [smem(), vmem(), vmem()],
+        vmem(),
+        16,
+        flops=2 * entries * 128 * 128 * flux_depth,
+        moved=4 * 2**20,
+    )
+
+    def smooth_rows(odd, runs):
+        operands, specs, marked = [], [], []
+        for first, count in runs:
+            halos = []
+            for row in range(first - 1, first + count + 1):
+                if row < 0 or row >= lat_rows:
+                    operands.append((low if row < 0 else high)[None])
+                    specs.append(vmem())
+                    halos.append(row)
+                else:
+                    operands.append(field)
+                    specs.append(pl.BlockSpec((1, lon_cells, channels), lambda _, row=row: (row, 0, 0)))
+            marked.append((first, count, tuple(halos)))
+        places = len(operands)
+        operands += [sides, taps]
+        specs += [vmem(), vmem()]
+        scratch = [pltpu.VMEM((places, lon_cells + 16, channels // 2), f32)]
+        if odd:
+            operands += [sea_rows, sea]
+            specs += [smem(), vmem()]
+            longest = max(count for _, count in runs)
+            scratch.append(pltpu.VMEM((longest * lon_cells + 256, channels // 2), f32))
+        return local_call(
+            functools.partial(smooth_body, odd, tuple(marked), bool(odd)),
+            [jax.ShapeDtypeStruct((count * lon_cells, channels // 2), bf16) for _, count in runs],
+            operands,
+            specs,
+            [vmem() for _ in runs],
+            24,
+            scratch=scratch,
+            flops=18 * sum(count for _, count in runs) * lon_cells * channels // 2,
+            moved=4 * 2**20,
+        )
+
+    edge = lat_rows // 4
+    middle = [(edge, lat_rows - 2 * edge)]
+    ends = [(0, edge), (lat_rows - edge, edge)]
+    plan = []
+    for runs in (middle, ends):
+        evens = smooth_rows(0, runs)
+        others = [lax.ppermute(value, "chan", SWAP) for value in evens]
+        odds = smooth_rows(1, runs)
+        others_odd = [lax.ppermute(value, "chan", SWAP) for value in odds]
+        plan += list(zip(runs, evens, odds, others, others_odd))
+
+    across, back, ocean_across, ocean_back = local_call(
+        gather_weights_body,
+        [
+            jax.ShapeDtypeStruct((2 * channels, hidden), bf16),
+            jax.ShapeDtypeStruct((hidden, channels), bf16),
+            jax.ShapeDtypeStruct((ocean_hidden, 2 * flux_depth), bf16),
+            jax.ShapeDtypeStruct((ocean_hidden, flux_depth), bf16),
+        ],
+        (chan, atmos_up, atmos_down, ocean_up, ocean_down, *pieces),
+        [smem()] + [vmem()] * 8,
+        [vmem()] * 4,
+        32,
+        flops=8 * hidden * channels * channels,
+        moved=8 * 2**20,
+    )
+    gain = atmos_gain.reshape(2, channels // 2, 2)
+    gain = jnp.where(lax.axis_index("chan") == 0, gain, gain[::-1]).transpose(0, 2, 1).reshape(1, 2 * channels)
+    gain_ocean = ocean_gain.reshape(2, flux_depth)
+    gain_ocean = jnp.where(lax.axis_index("chan") == 0, gain_ocean, gain_ocean[::-1]).reshape(1, 2 * flux_depth)
+
+    entries = flux_pattern.shape[1]
+    ocean_input = local_call(
+        flux_remap_body,
+        jax.ShapeDtypeStruct((flux_depth, ocean_cells), bf16),
+        (flux_rows, flux_in, remap_blocks, ocean_state),
+        [smem(), vmem(), vmem(), vmem()],
+        vmem(),
+        16,
+        scratch=[pltpu.VMEM((ocean_count, flux_depth, 128), f32)],
+        flops=2 * entries * 128 * 128 * flux_depth,
+        moved=5 * 2**20,
+    )
+    ocean_other = lax.ppermute(ocean_input, "chan", SWAP)
+
+    result = None
+    for (first, count), *values in plan:
+        operands = [*values, gain, across, back]
+        specs = [pl.BlockSpec((lon_cells, channels // 2), lambda step: (step, 0))] * 4 + [vmem()] * 3
+        aliases = {}
+        if result is not None:
+            aliases = {len(operands): 0}
+            operands.append(result)
+            specs.append(anywhere())
+        result = local_call(
+            atmos_layer_body,
+            jax.ShapeDtypeStruct((lat_rows, lon_cells, channels), bf16),
+            operands,
+            specs,
+            pl.BlockSpec((1, lon_cells, channels), lambda step, first=first: (first + step, 0, 0)),
+            24,
+            grid=count,
+            flops=2 * count * lon_cells * 3 * channels * hidden,
+            moved=(4 + count) * 2**20,
+            exps=count * lon_cells * hidden,
+            aliases=aliases,
+        )
+    ocean_next = local_call(
+        ocean_layer_body,
+        jax.ShapeDtypeStruct((flux_depth, ocean_cells), bf16),
+        (ocean_mask, ocean_input, ocean_other, gain_ocean, ocean_across, ocean_back),
+        [smem()] + [vmem()] * 5,
+        vmem(),
+        16,
+        flops=2 * ocean_cells * 3 * flux_depth * ocean_hidden,
+        moved=4 * 2**20,
+        exps=ocean_cells * ocean_hidden,
+    )
+    return result.transpose(2, 0, 1), ocean_next
+
+
 def solution(mesh):
     in_specs = (
         P("chan", ("groups", "lat"), "pair"),
@@ -180,4 +635,6 @@
         P(("lat", "pair")),
     )
     out_specs = (P("chan", ("groups", "lat"), "pair"), P("chan", ("groups", "lat", "pair")))
-    return jax.shard_map(shards, mesh=mesh, in_specs=in_specs, out_specs=out_specs, check_vma=False)
+    paired = all(mesh.shape[axis] == 2 for axis in ("groups", "chan", "pair"))
+    body = quick_shards if paired else shards
+    return jax.shard_map(body, mesh=mesh, in_specs=in_specs, out_specs=out_specs, check_vma=False)

time: 404 us -> 150 us (0.37); the launches traced: 397 us -> 149 us
  local copies, waits for them, and re-layouts: 138 us -> 10.4 us
  other arithmetic: 84.4 us -> 2.63 us
  Pallas kernels: 0 us -> 62.9 us
  blocking collectives: 48.3 us -> 0 us
  matrix products: 35.5 us -> 0 us
  between operations: 14.4 us -> 0.97 us
  waiting for transfers between devices: 49.4 us -> 43.5 us
    slice x5 -> x2, local copies, waits for them, and re-layouts: 71.2 us -> 0.02 us  [the longest x1 0.02 us: quick_shards(): field[:, lon_cells - 1, :]]
    pallas_call x0 -> x13, Pallas kernels: none -> 62.9 us  [local_call(): pl.pallas_call(body, grid=(grid,), out_shape=out_shape, in_specs=in_specs...]
    all_gather x2 -> x0, blocking collectives: 48.3 us -> none  [the longest x1 39.8 us: shards(): ocean_up_rows = lax.all_gather(ocean_up, 'chan', axis=0, tiled=True)]
    all_to_all x6 -> x2, waiting for transfers between devices: 44.6 us -> 0.01 us  [the longest x1 0.01 us: quick_shards(): lax.all_to_all(sea_out, peers, split_axis=0, concat_axis=0, tiled=True)]
    add x2 -> x0, other arithmetic: 44.3 us -> none  [the longest x1 44.3 us: shards(): combined = atmosphere.astype(jnp.float32) + smooth]
    ppermute x4 -> x14, waiting for transfers between devices: 3.55 us -> 43.5 us  [the longest x1 21.8 us: quick_shards(): lax.ppermute(jnp.concatenate([field[lat_rows - 1], sides[-2:], fill], axi...]
    dot_general x8 -> x0, matrix products: 35.5 us -> none  [the longest x1 18.5 us: shards(): lax.dot_general(down_rows, hidden, (((0,), (0,)), ((), ())), preferred_el...]
    gather x9 -> x0, local copies, waits for them, and re-layouts: 24.6 us -> none  [the longest x3 10.5 us: add_group(): weights = jnp.take(blocks, entry_rows[:, 2], axis=0)]
  transfers between devices with their start and end apart: 12 -> 16, of which waited for: 3 -> 5; matrix products, arithmetic and copies ran while one was open for 56% -> 5% of each run, Pallas kernels for 0% -> 38%
where the time goes in v2:
time: 150 us; the launch traced here: 149 us
  Pallas kernels  62.9 us (42%)
  waiting for transfers between devices  43.5 us (29%)
  starting transfers between devices  28.6 us (19%)
  local copies, waits for them, and re-layouts  10.4 us (7%)
  other arithmetic  2.63 us (2%)
    pallas_call x13, Pallas kernels, local_call(): pl.pallas_call(body, grid=(grid,), out_shape=out_shape, in_specs=in_specs...  62.9 us
    ppermute x1, waiting for transfers between devices, quick_shards(): lax.ppermute(jnp.concatenate([field[lat_rows - 1], sides[-2:], fill], axi...  21.8 us
    ppermute x1, waiting for transfers between devices, far_weights(): one = lax.ppermute(packed, 'chan', SWAP)  10.8 us
    ppermute x1, waiting for transfers between devices, quick_shards(): lax.ppermute(jnp.concatenate([field[0], sides[:2], fill], axis=0), 'lat',...  9.47 us
    all_to_all x1, starting transfers between devices, quick_shards(): lax.all_to_all(flux_out, peers, split_axis=0, concat_axis=0, tiled=True)  6.58 us
    unnamed x58, local copies, waits for them, and re-layouts  5.58 us
    all_to_all x1, starting transfers between devices, quick_shards(): lax.all_to_all(sea_out, peers, split_axis=0, concat_axis=0, tiled=True)  5.21 us
    ppermute x3, starting transfers between devices, quick_shards(): others = [lax.ppermute(value, 'chan', SWAP) for value in evens]  3.75 us
  transfers between devices with their start and end apart: 16, of which 5 were waited for; matrix products, arithmetic and copies ran while one was open for 5% of the time, Pallas kernels for 38%

profile of v2, /device:TPU:16, one launch (start us, length us, event | category | flops | bytes accessed | tf_op | source)
XLA Modules:
  0.0 148.9 jit_solution(9774689341670600834)
XLA Ops:
  2.2 1.4 shard_map.159
  3.6 5.2 %all-to-all-start = ((bf16[8,128,128]{2,1,0:T(8,128)(2,1)}), bf16[8,128,128]{2,1,0:T(8,128)(2,1)S(1)}, u32[]{:S(2)}, u32[]{:S(2)}) async-start(bf16[8,128,128]{2,1,0:T(8,128)(2,1)} %shard_map.159), calls=%async_computation | async-start | bytes 524288 | tf_op jit(solution)/shard_map/all_to_all | solution.py:471
  8.8 1.8 %copy-done = bf16[256,8,720]{0,2,1:T(8,128)(2,1)S(1)} copy-done((bf16[256,8,720]{0,2,1:T(8,128)(2,1)S(1)}, bf16[256,8,720]{0,2,1:T(8,128)(2,1)}, u32[]{:S(2)}) %copy-start) | copy-done | bytes 2949144
  11.3 3.5 %shard_map.168 = bf16[64,128,128]{2,1,0:T(8,128)(2,1)S(1)} custom-call(s32[1,8,8]{2,1,0:T(8,128)S(1)} %copy-done.17, bf16[5760,256]{1,0:T(8,128)(2,1)S(1)} %bitcast.21), custom_call_target="tpu_custom_call" | custom-call | flops 377487360 | bytes 6291456 | tf_op jit(solution)/shard_map/pallas_call | solution.py:187
  14.9 1.3 copy-done.6
  16.2 6.6 %all-to-all-start.1 = ((bf16[64,128,128]{2,1,0:T(8,128)(2,1)}), bf16[64,128,128]{2,1,0:T(8,128)(2,1)}, u32[]{:S(2)}, u32[]{:S(2)}) async-start(bf16[64,128,128]{2,1,0:T(8,128)(2,1)} %copy-done.6), calls=%async_computation.1 | async-start | bytes 4194304 | tf_op jit(solution)/shard_map/all_to_all | solution.py:490
  25.4 1.0 constant_dynamic-slice_fusion.1
  27.2 1.5 %collective-permute-start.5 = (bf16[320,768]{1,0:T(8,128)(2,1)}, bf16[320,768]{1,0:T(8,128)(2,1)}, u32[]{:S(2)}, u32[]{:S(2)}) collective-permute-start(bf16[320,768]{1,0:T(8,128)(2,1)} %fusion.7), channel_id=1, source_target_pairs={{0,2},{2,0},{1,3},{3,1},{4,6},{6,4},{5,7},{7,5},{8,10},{10,8},{9,1... | collective-permute-start | bytes 1474568 | tf_op jit(solution)/shard_map/ppermute | solution.py:422
  28.9 1.0 collective-permute-done.refs_8_.refs_6_
  30.0 10.8 %collective-permute-done.5.refs_0_ = bf16[320,768]{1,0:T(8,128)(2,1)} collective-permute-done((bf16[320,768]{1,0:T(8,128)(2,1)}, bf16[320,768]{1,0:T(8,128)(2,1)}, u32[]{:S(2)}, u32[]{:S(2)}) %collective-permute-start.5) | collective-permute-done | bytes 491552 | tf_op jit(solution)/shard_map/ppermute | solution.py:422
  40.8 1.5 %collective-permute-start.6 = (bf16[320,768]{1,0:T(8,128)(2,1)}, bf16[320,768]{1,0:T(8,128)(2,1)}, u32[]{:S(2)}, u32[]{:S(2)}) collective-permute-start(bf16[320,768]{1,0:T(8,128)(2,1)} %collective-permute-done.5.refs_0_), channel_id=1, source_target_pairs={{0,16},{16,0},{1,17},{17,1},{2,18},{18,2},{3,19},{19,3},{4,20},{20... | collective-permute-start | bytes 1474568 | tf_op jit(solution)/shard_map/ppermute | solution.py:423
  42.3 1.1 maximum_maximum_fusion.1
  43.4 3.4 %collective-permute-start.1 = (bf16[736,256]{1,0:T(8,128)(2,1)}, bf16[736,256]{1,0:T(8,128)(2,1)S(1)}, u32[]{:S(2)}, u32[]{:S(2)}) collective-permute-start(bf16[736,256]{1,0:T(8,128)(2,1)} %get-tuple-element.25), channel_id=1, source_target_pairs={{0,4},{4,8},{8,12},{1,5},{5,9},{9,13},{2,6},{6,10},{10,14},{3,7},{... | collective-permute-start | bytes 1130504 | tf_op jit(solution)/shard_map/ppermute | solution.py:476
  46.8 2.1 %shard_map.163.own_even = bf16[2880,128]{1,0:T(8,128)(2,1)} custom-call(bf16[8,720,256]{2,1,0:T(8,128)(2,1)S(1)} %bitcast.24, bf16[8,720,256]{2,1,0:T(8,128)(2,1)S(1)} %bitcast.25, bf16[8,720,256]{2,1,0:T(8,128)(2,1)S(1)} %bitcast.26, bf16[8,720,256]{2,1,0:T(8,128)(2,1)S(1)} %bitcast.27, bf16[8,720,256]{2,1,0:T(8,128)(2,1)S(1)} %bitcast.28, ...), custom_call_target="tpu_custom_call" | custom-call | flops 6635520 | bytes 4194304 | tf_op jit(solution)/shard_map/pallas_call | solution.py:187
  48.9 1.5 %collective-permute-start.11 = (bf16[2880,128]{1,0:T(8,128)(2,1)}, bf16[2880,128]{1,0:T(8,128)(2,1)}, u32[]{:S(2)}, u32[]{:S(2)}) collective-permute-start(bf16[2880,128]{1,0:T(8,128)(2,1)} %shard_map.163.own_even), channel_id=1, source_target_pairs={{0,2},{2,0},{1,3},{3,1},{4,6},{6,4},{5,7},{7,5},{8,10},{10,8},{9,1... | collective-permute-start | bytes 2211848 | tf_op jit(solution)/shard_map/ppermute | solution.py:544
  50.4 1.1 shard_map.160.refs_11_.refs_9_
  51.5 2.9 %shard_map.164.own_odd = bf16[2880,128]{1,0:T(8,128)(2,1)} custom-call(bf16[8,720,256]{2,1,0:T(8,128)(2,1)S(1)} %bitcast.33, bf16[8,720,256]{2,1,0:T(8,128)(2,1)S(1)} %bitcast.31, bf16[8,720,256]{2,1,0:T(8,128)(2,1)S(1)} %bitcast.32, bf16[8,720,256]{2,1,0:T(8,128)(2,1)S(1)} %bitcast.30, bf16[8,720,256]{2,1,0:T(8,128)(2,1)S(1)} %bitcast.34, ...), custom_call_target="tpu_custom_call" | custom-call | flops 6635520 | bytes 4194304 | tf_op jit(solution)/shard_map/pallas_call | solution.py:187
  55.6 21.8 %collective-permute-done.1 = bf16[736,256]{1,0:T(8,128)(2,1)S(1)} collective-permute-done((bf16[736,256]{1,0:T(8,128)(2,1)}, bf16[736,256]{1,0:T(8,128)(2,1)S(1)}, u32[]{:S(2)}, u32[]{:S(2)}) %collective-permute-start.1) | collective-permute-done | bytes 376864 | tf_op jit(solution)/shard_map/ppermute | solution.py:476
  77.4 1.9 %collective-permute-start.2 = (bf16[736,256]{1,0:T(8,128)(2,1)}, bf16[736,256]{1,0:T(8,128)(2,1)}, u32[]{:S(2)}, u32[]{:S(2)}) collective-permute-start(bf16[736,256]{1,0:T(8,128)(2,1)} %get-tuple-element.24), channel_id=1, source_target_pairs={{4,0},{8,4},{12,8},{5,1},{9,5},{13,9},{6,2},{10,6},{14,10},{7,3},{... | collective-permute-start | bytes 1130504 | tf_op jit(solution)/shard_map/ppermute | solution.py:477
  80.0 1.0 copy.19
  80.9 9.5 %collective-permute-done.2 = bf16[736,256]{1,0:T(8,128)(2,1)} collective-permute-done((bf16[736,256]{1,0:T(8,128)(2,1)}, bf16[736,256]{1,0:T(8,128)(2,1)}, u32[]{:S(2)}, u32[]{:S(2)}) %collective-permute-start.2) | collective-permute-done | bytes 376864 | tf_op jit(solution)/shard_map/ppermute | solution.py:477
  90.4 3.0 %shard_map.158 = (bf16[1440,128]{1,0:T(8,128)(2,1)S(1)}, bf16[1440,128]{1,0:T(8,128)(2,1)}) custom-call(bf16[1,736,256]{2,1,0:T(8,128)(2,1)S(1)} %bitcast.48, bf16[8,720,256]{2,1,0:T(8,128)(2,1)S(1)} %bitcast.36, bf16[8,720,256]{2,1,0:T(8,128)(2,1)S(1)} %bitcast.37, bf16[8,720,256]{2,1,0:T(8,128)(2,1)S(1)} %bitcast.38, bf16[8,720,256]{2,1,0:T(8,128)(2,1)S(1)} %bitcast.39, ...), custom_call_target="tpu_custom_call" | custom-call | flops 6635520 | bytes 4194304 | tf_op jit(solution)/shard_map/pallas_call | solution.py:187
  93.4 1.6 %collective-permute-start.9 = (bf16[1440,128]{1,0:T(8,128)(2,1)S(1)}, bf16[1440,128]{1,0:T(8,128)(2,1)S(1)}, u32[]{:S(2)}, u32[]{:S(2)}) collective-permute-start(bf16[1440,128]{1,0:T(8,128)(2,1)S(1)} %get-tuple-element.14.own_even), channel_id=1, source_target_pairs={{0,2},{2,0},{1,3},{3,1},{4,6},{6,4},{5,7},{7,5},{8,10},{10,8},{9,1... | collective-permute-start | bytes 1105928 | tf_op jit(solution)/shard_map/ppermute | solution.py:544
  95.0 3.8 %shard_map.161 = (bf16[1440,128]{1,0:T(8,128)(2,1)S(1)}, bf16[1440,128]{1,0:T(8,128)(2,1)}) custom-call(bf16[1,736,256]{2,1,0:T(8,128)(2,1)S(1)} %bitcast.49, bf16[8,720,256]{2,1,0:T(8,128)(2,1)S(1)} %bitcast.42, bf16[8,720,256]{2,1,0:T(8,128)(2,1)S(1)} %bitcast.43, bf16[8,720,256]{2,1,0:T(8,128)(2,1)S(1)} %bitcast.44, bf16[8,720,256]{2,1,0:T(8,128)(2,1)S(1)} %bitcast.45, ...), custom_call_target="tpu_custom_call" | custom-call | flops 6635520 | bytes 4194304 | tf_op jit(solution)/shard_map/pallas_call | solution.py:187
  99.4 1.3 collective-permute-start.10
  100.8 2.9 %shard_map.162 = (bf16[512,2048]{1,0:T(8,128)(2,1)S(1)}, bf16[2048,256]{1,0:T(8,128)(2,1)S(1)}, bf16[1024,256]{1,0:T(8,128)(2,1)S(1)}, bf16[1024,128]{1,0:T(8,128)(2,1)S(1)}) custom-call(s32[1]{0:T(128)} %bitcast.10.chan, bf16[1024,512]{1,0:T(8,128)(2,1)S(1)} %copy-done.7, bf16[1024,512]{1,0:T(8,128)(2,1)S(1)} %copy-done.8, bf16[512,256]{1,0:T(8,128)(2,1)S(1)} %copy-done.13, ...), custom_call_target="tpu_custom_call" | custom-call | flops 1073741824 | bytes 8388608 | tf_op jit(solution)/shard_map/pallas_call | solution.py:187
  104.6 15.8 %shard_map.165.refs_0_ = bf16[8,720,256]{2,1,0:T(8,128)(2,1)} custom-call(bf16[2880,128]{1,0:T(8,128)(2,1)} %shard_map.163.own_even, bf16[2880,128]{1,0:T(8,128)(2,1)} %shard_map.164.own_odd, bf16[2880,128]{1,0:T(8,128)(2,1)} %collective-permute-done.11.other_even, bf16[2880,128]{1,0:T(8,128)(2,1)} %collective-permute-done.12.other_odd, ...), custom_call_target="tpu_custom_call" | custom-call | flops 9059696640 | bytes 8388608 | tf_op jit(solution)/shard_map/pallas_call | solution.py:187
  120.8 7.5 %shard_map.166.refs_0_ = bf16[8,720,256]{2,1,0:T(8,128)(2,1)} custom-call(bf16[1440,128]{1,0:T(8,128)(2,1)S(1)} %get-tuple-element.14.own_even, bf16[1440,128]{1,0:T(8,128)(2,1)S(1)} %get-tuple-element.15.own_odd, bf16[1440,128]{1,0:T(8,128)(2,1)S(1)} %collective-permute-done.9.other_even, ...), custom_call_target="tpu_custom_call", output_to_operand_aliasing={{}: (7, {})} | custom-call | flops 4529848320 | bytes 6291456 | tf_op jit(solution)/shard_map/pallas_call | solution.py:187
  128.3 5.5 %shard_map.169.own = bf16[128,1024]{1,0:T(8,128)(2,1)S(1)} custom-call(s32[3,1,128]{2,1,0:T(1,128)S(1)} %bitcast.60, bf16[64,128,128]{2,1,0:T(8,128)(2,1)} %all-to-all-done.1.slots, bf16[64,128,128]{2,1,0:T(8,128)(2,1)S(1)} %copy-done.5, bf16[128,1024]{1,0:T(8,128)(2,1)S(1)} %copy-done.10), custom_call_target="tpu_custom_call" | custom-call | flops 536870912 | bytes 5242880 | tf_op jit(solution)/shard_map/pallas_call | solution.py:187
  133.9 1.6 %collective-permute-start.13 = (bf16[128,1024]{1,0:T(8,128)(2,1)S(1)}, bf16[128,1024]{1,0:T(8,128)(2,1)S(1)}, u32[]{:S(2)}, u32[]{:S(2)}) collective-permute-start(bf16[128,1024]{1,0:T(8,128)(2,1)S(1)} %shard_map.169.own), channel_id=1, source_target_pairs={{0,2},{2,0},{1,3},{3,1},{4,6},{6,4},{5,7},{7,5},{8,10},{10,8},{9,1... | collective-permute-start | bytes 786440 | tf_op jit(solution)/shard_map/ppermute | solution.py:581
  135.5 8.6 %shard_map.167 = bf16[8,720,256]{2,1,0:T(8,128)(2,1)} custom-call(bf16[1440,128]{1,0:T(8,128)(2,1)} %get-tuple-element.10.own_even, bf16[1440,128]{1,0:T(8,128)(2,1)} %get-tuple-element.11.own_odd, bf16[1440,128]{1,0:T(8,128)(2,1)S(1)} %collective-permute-done.3.other_even, ...), custom_call_target="tpu_custom_call", output_to_operand_aliasing={{}: (7, {})} | custom-call | flops 4529848320 | bytes 6291456 | tf_op jit(solution)/shard_map/pallas_call | solution.py:187
  144.1 4.8 %shard_map.170 = bf16[128,1024]{1,0:T(8,128)(2,1)} custom-call(s32[8]{0:T(128)S(1)} %copy-done.26, bf16[128,1024]{1,0:T(8,128)(2,1)S(1)} %shard_map.169.own, bf16[128,1024]{1,0:T(8,128)(2,1)S(1)} %collective-permute-done.13.other, f32[1,256]{1,0:T(1,128)S(1)} %bitcast.61, bf16[1024,256]{1,0:T(8,128)(2,1)S(1)} %get-tuple-element.16.across, ...), custom_call_target="tpu_custom_call" | custom-call | flops 805306368 | bytes 4194304 | tf_op jit(solution)/shard_map/pallas_call | solution.py:187
  (90 shorter events, 9.8 us)
Async XLA Ops:
  3.6 12.6 %all-to-all-start = ((bf16[8,128,128]{2,1,0:T(8,128)(2,1)}), bf16[8,128,128]{2,1,0:T(8,128)(2,1)S(1)}, u32[]{:S(2)}, u32[]{:S(2)}) async-start(bf16[8,128,128]{2,1,0:T(8,128)(2,1)} %shard_map.159), calls=%async_computation | async-start | bytes 524288 | tf_op jit(solution)/shard_map/all_to_all | solution.py:471
  16.2 12.4 %copy-start.1 = (bf16[256,8,720]{0,2,1:T(8,128)(2,1)S(1)}, bf16[256,8,720]{0,2,1:T(8,128)(2,1)}, u32[]{:S(2)}) copy-start(bf16[256,8,720]{0,2,1:T(8,128)(2,1)} %param.15) | copy-start | bytes 8847364
  16.2 10.9 %copy-start.11 = (bf16[8,128,128]{2,1,0:T(8,128)(2,1)}, bf16[8,128,128]{2,1,0:T(8,128)(2,1)S(1)}, u32[]{:S(2)}) copy-start(bf16[8,128,128]{2,1,0:T(8,128)(2,1)S(1)} %all-to-all-done.slots) | copy-start | bytes 786436
  16.2 112.1 %all-to-all-start.1 = ((bf16[64,128,128]{2,1,0:T(8,128)(2,1)}), bf16[64,128,128]{2,1,0:T(8,128)(2,1)}, u32[]{:S(2)}, u32[]{:S(2)}) async-start(bf16[64,128,128]{2,1,0:T(8,128)(2,1)} %copy-done.6), calls=%async_computation.1 | async-start | bytes 4194304 | tf_op jit(solution)/shard_map/all_to_all | solution.py:490
  22.8 23.9 %copy-start.15 = (bf16[256,9]{0,1:T(8,128)(2,1)S(1)}, bf16[256,9]{0,1:T(8,128)(2,1)}, u32[]{:S(2)}) copy-start(bf16[256,9]{0,1:T(8,128)(2,1)} %param.17) | copy-start | bytes 13828
  27.2 13.6 %collective-permute-start.5 = (bf16[320,768]{1,0:T(8,128)(2,1)}, bf16[320,768]{1,0:T(8,128)(2,1)}, u32[]{:S(2)}, u32[]{:S(2)}) collective-permute-start(bf16[320,768]{1,0:T(8,128)(2,1)} %fusion.7), channel_id=1, source_target_pairs={{0,2},{2,0},{1,3},{3,1},{4,6},{6,4},{5,7},{7,5},{8,10},{10,8},{9,1... | collective-permute-start | bytes 1474568 | tf_op jit(solution)/shard_map/ppermute | solution.py:422
  28.7 1.2 collective-permute-start
  40.8 14.2 %collective-permute-start.6 = (bf16[320,768]{1,0:T(8,128)(2,1)}, bf16[320,768]{1,0:T(8,128)(2,1)}, u32[]{:S(2)}, u32[]{:S(2)}) collective-permute-start(bf16[320,768]{1,0:T(8,128)(2,1)} %collective-permute-done.5.refs_0_), channel_id=1, source_target_pairs={{0,16},{16,0},{1,17},{17,1},{2,18},{18,2},{3,19},{19,3},{4,20},{20... | collective-permute-start | bytes 1474568 | tf_op jit(solution)/shard_map/ppermute | solution.py:423
  43.4 34.0 %collective-permute-start.1 = (bf16[736,256]{1,0:T(8,128)(2,1)}, bf16[736,256]{1,0:T(8,128)(2,1)S(1)}, u32[]{:S(2)}, u32[]{:S(2)}) collective-permute-start(bf16[736,256]{1,0:T(8,128)(2,1)} %get-tuple-element.25), channel_id=1, source_target_pairs={{0,4},{4,8},{8,12},{1,5},{5,9},{9,13},{2,6},{6,10},{10,14},{3,7},{... | collective-permute-start | bytes 1130504 | tf_op jit(solution)/shard_map/ppermute | solution.py:476
  48.9 54.9 %collective-permute-start.11 = (bf16[2880,128]{1,0:T(8,128)(2,1)}, bf16[2880,128]{1,0:T(8,128)(2,1)}, u32[]{:S(2)}, u32[]{:S(2)}) collective-permute-start(bf16[2880,128]{1,0:T(8,128)(2,1)} %shard_map.163.own_even), channel_id=1, source_target_pairs={{0,2},{2,0},{1,3},{3,1},{4,6},{6,4},{5,7},{7,5},{8,10},{10,8},{9,1... | collective-permute-start | bytes 2211848 | tf_op jit(solution)/shard_map/ppermute | solution.py:544
  54.4 50.2 %collective-permute-start.12 = (bf16[2880,128]{1,0:T(8,128)(2,1)}, bf16[2880,128]{1,0:T(8,128)(2,1)}, u32[]{:S(2)}, u32[]{:S(2)}) collective-permute-start(bf16[2880,128]{1,0:T(8,128)(2,1)} %shard_map.164.own_odd), channel_id=1, source_target_pairs={{0,2},{2,0},{1,3},{3,1},{4,6},{6,4},{5,7},{7,5},{8,10},{10,8},{9,1... | collective-permute-start | bytes 2211848 | tf_op jit(solution)/shard_map/ppermute | solution.py:546
  54.9 43.8 %collective-permute-start.7 = (bf16[320,768]{1,0:T(8,128)(2,1)}, bf16[320,768]{1,0:T(8,128)(2,1)}, u32[]{:S(2)}, u32[]{:S(2)}) collective-permute-start(bf16[320,768]{1,0:T(8,128)(2,1)} %collective-permute-done.5.refs_0_), channel_id=1, source_target_pairs={{0,1},{1,0},{2,3},{3,2},{4,5},{5,4},{6,7},{7,6},{8,9},{9,8},{10,11... | collective-permute-start | bytes 1474568 | tf_op jit(solution)/shard_map/ppermute | solution.py:424
  54.9 44.5 %collective-permute-start.8 = (bf16[320,768]{1,0:T(8,128)(2,1)}, bf16[320,768]{1,0:T(8,128)(2,1)}, u32[]{:S(2)}, u32[]{:S(2)}) collective-permute-start(bf16[320,768]{1,0:T(8,128)(2,1)} %collective-permute-done.6.refs_1_), channel_id=1, source_target_pairs={{0,1},{1,0},{2,3},{3,2},{4,5},{5,4},{6,7},{7,6},{8,9},{9,8},{10,11... | collective-permute-start | bytes 1474568 | tf_op jit(solution)/shard_map/ppermute | solution.py:424
  77.4 13.0 %collective-permute-start.2 = (bf16[736,256]{1,0:T(8,128)(2,1)}, bf16[736,256]{1,0:T(8,128)(2,1)}, u32[]{:S(2)}, u32[]{:S(2)}) collective-permute-start(bf16[736,256]{1,0:T(8,128)(2,1)} %get-tuple-element.24), channel_id=1, source_target_pairs={{4,0},{8,4},{12,8},{5,1},{9,5},{13,9},{6,2},{10,6},{14,10},{7,3},{... | collective-permute-start | bytes 1130504 | tf_op jit(solution)/shard_map/ppermute | solution.py:477
  93.4 7.4 %copy-start.7 = (bf16[1024,512]{1,0:T(8,128)(2,1)S(1)}, bf16[1024,512]{1,0:T(8,128)(2,1)}, u32[]{:S(2)}) copy-start(bf16[1024,512]{1,0:T(8,128)(2,1)} %up.1) | copy-start | bytes 3145732
  93.4 7.4 %copy-start.8 = (bf16[1024,512]{1,0:T(8,128)(2,1)S(1)}, bf16[1024,512]{1,0:T(8,128)(2,1)}, u32[]{:S(2)}) copy-start(bf16[1024,512]{1,0:T(8,128)(2,1)} %down.1) | copy-start | bytes 3145732
  93.4 7.4 %copy-start.13 = (bf16[512,256]{1,0:T(8,128)(2,1)S(1)}, bf16[512,256]{1,0:T(8,128)(2,1)}, u32[]{:S(2)}) copy-start(bf16[512,256]{1,0:T(8,128)(2,1)} %ocean_up.1) | copy-start | bytes 786436
  93.4 7.4 %copy-start.14 = (bf16[512,256]{1,0:T(8,128)(2,1)S(1)}, bf16[512,256]{1,0:T(8,128)(2,1)}, u32[]{:S(2)}) copy-start(bf16[512,256]{1,0:T(8,128)(2,1)} %ocean_down.1) | copy-start | bytes 786436
  93.4 26.9 %collective-permute-start.9 = (bf16[1440,128]{1,0:T(8,128)(2,1)S(1)}, bf16[1440,128]{1,0:T(8,128)(2,1)S(1)}, u32[]{:S(2)}, u32[]{:S(2)}) collective-permute-start(bf16[1440,128]{1,0:T(8,128)(2,1)S(1)} %get-tuple-element.14.own_even), channel_id=1, source_target_pairs={{0,2},{2,0},{1,3},{3,1},{4,6},{6,4},{5,7},{7,5},{8,10},{10,8},{9,1... | collective-permute-start | bytes 1105928 | tf_op jit(solution)/shard_map/ppermute | solution.py:544
  98.7 36.7 %collective-permute-start.3 = (bf16[1440,128]{1,0:T(8,128)(2,1)}, bf16[1440,128]{1,0:T(8,128)(2,1)S(1)}, u32[]{:S(2)}, u32[]{:S(2)}) collective-permute-start(bf16[1440,128]{1,0:T(8,128)(2,1)} %get-tuple-element.10.own_even), channel_id=1, source_target_pairs={{0,2},{2,0},{1,3},{3,1},{4,6},{6,4},{5,7},{7,5},{8,10},{10,8},{9,1... | collective-permute-start | bytes 1105928 | tf_op jit(solution)/shard_map/ppermute | solution.py:544
  99.4 21.4 %collective-permute-start.10 = (bf16[1440,128]{1,0:T(8,128)(2,1)S(1)}, bf16[1440,128]{1,0:T(8,128)(2,1)S(1)}, u32[]{:S(2)}, u32[]{:S(2)}) collective-permute-start(bf16[1440,128]{1,0:T(8,128)(2,1)S(1)} %get-tuple-element.15.own_odd), channel_id=1, source_target_pairs={{0,2},{2,0},{1,3},{3,1},{4,6},{6,4},{5,7},{7,5},{8,10},{10,8},{9,1... | collective-permute-start | bytes 1105928 | tf_op jit(solution)/shard_map/ppermute | solution.py:546
  103.7 16.6 %copy-start.24 = (bf16[1024,128]{1,0:T(8,128)(2,1)}, bf16[1024,128]{1,0:T(8,128)(2,1)S(1)}, u32[]{:S(2)}) copy-start(bf16[1024,128]{1,0:T(8,128)(2,1)S(1)} %get-tuple-element.17.back) | copy-start | bytes 786436
  103.7 17.1 %copy-start.20 = (bf16[512,2048]{1,0:T(8,128)(2,1)}, bf16[512,2048]{1,0:T(8,128)(2,1)S(1)}, u32[]{:S(2)}) copy-start(bf16[512,2048]{1,0:T(8,128)(2,1)S(1)} %get-tuple-element.12.across) | copy-start | bytes 6291460
  103.8 17.1 %copy-start.22 = (bf16[2048,256]{1,0:T(8,128)(2,1)}, bf16[2048,256]{1,0:T(8,128)(2,1)S(1)}, u32[]{:S(2)}) copy-start(bf16[2048,256]{1,0:T(8,128)(2,1)S(1)} %get-tuple-element.13.back) | copy-start | bytes 3145732
  103.8 31.7 %collective-permute-start.4 = (bf16[1440,128]{1,0:T(8,128)(2,1)}, bf16[1440,128]{1,0:T(8,128)(2,1)}, u32[]{:S(2)}, u32[]{:S(2)}) collective-permute-start(bf16[1440,128]{1,0:T(8,128)(2,1)} %get-tuple-element.11.own_odd), channel_id=1, source_target_pairs={{0,2},{2,0},{1,3},{3,1},{4,6},{6,4},{5,7},{7,5},{8,10},{10,8},{9,1... | collective-permute-start | bytes 1105928 | tf_op jit(solution)/shard_map/ppermute | solution.py:546
  120.3 8.0 %copy-start.5 = (bf16[64,128,128]{2,1,0:T(8,128)(2,1)S(1)}, bf16[64,128,128]{2,1,0:T(8,128)(2,1)}, u32[]{:S(2)}) copy-start(bf16[64,128,128]{2,1,0:T(8,128)(2,1)} %blocks.3) | copy-start | bytes 6291460
  120.3 8.0 %copy-start.10 = (bf16[128,1024]{1,0:T(8,128)(2,1)S(1)}, bf16[128,1024]{1,0:T(8,128)(2,1)}, u32[]{:S(2)}) copy-start(bf16[128,1024]{1,0:T(8,128)(2,1)} %ocean.3) | copy-start | bytes 786436
  120.4 8.0 %copy-start.18 = (s32[1,128,3]{1,0,2:T(1,128)S(1)}, s32[1,128,3]{1,0,2:T(1,128)}, u32[]{:S(2)}) copy-start(s32[1,128,3]{1,0,2:T(1,128)} %param.26) | copy-start | bytes 4612
  128.3 7.1 %copy-start.23 = (bf16[2048,256]{1,0:T(8,128)(2,1)S(1)}, bf16[2048,256]{1,0:T(8,128)(2,1)}, u32[]{:S(2)}) copy-start(bf16[2048,256]{1,0:T(8,128)(2,1)} %copy-done.22) | copy-start | bytes 3145732
  133.9 10.2 %copy-start.25 = (bf16[1024,128]{1,0:T(8,128)(2,1)S(1)}, bf16[1024,128]{1,0:T(8,128)(2,1)}, u32[]{:S(2)}) copy-start(bf16[1024,128]{1,0:T(8,128)(2,1)} %copy-done.24) | copy-start | bytes 786436
  133.9 10.2 %copy-start.26 = (s32[8]{0:T(128)S(1)}, s32[8]{0:T(128)}, u32[]{:S(2)}) copy-start(s32[8]{0:T(128)} %mask.1) | copy-start | bytes 100
  133.9 10.2 %collective-permute-start.13 = (bf16[128,1024]{1,0:T(8,128)(2,1)S(1)}, bf16[128,1024]{1,0:T(8,128)(2,1)S(1)}, u32[]{:S(2)}, u32[]{:S(2)}) collective-permute-start(bf16[128,1024]{1,0:T(8,128)(2,1)S(1)} %shard_map.169.own), channel_id=1, source_target_pairs={{0,2},{2,0},{1,3},{3,1},{4,6},{6,4},{5,7},{7,5},{8,10},{10,8},{9,1... | collective-permute-start | bytes 786440 | tf_op jit(solution)/shard_map/ppermute | solution.py:581
  (13 other events, 38.8 us)

commit v3 on v2

--- a/solution.py
+++ b/solution.py
@@ -193,7 +193,7 @@
         scratch_shapes=list(scratch),
         input_output_aliases=aliases or {},
         compiler_params=pltpu.CompilerParams(vmem_limit_bytes=limit * 2**20),
-        cost_estimate=pl.CostEstimate(flops=flops, bytes_accessed=moved, transcendentals=exps),
+        cost_estimate=pl.CostEstimate(flops=1, bytes_accessed=1, transcendentals=0),
     )(*operands)
 
 
@@ -215,6 +215,20 @@
     for entry in range(out.shape[0]):
         at = pl.multiple_of(sends[0, 0, entry] * 128, 128)
         out[entry] = ocean[:, pl.ds(at, 128)].T
+
+
+def sides_body(right, left, sides):
+    for row in range(right.shape[0]):
+        sides[2 * row : 2 * row + 1, :] = right[row, right.shape[1] - 1 : right.shape[1], :]
+        sides[2 * row + 1 : 2 * row + 2, :] = left[row, 0:1, :]
+
+
+def edges_body(last, first, sides, *outs):
+    cells = last.shape[1]
+    for out, row, at in ((outs[0], last, sides.shape[0] - 2), (outs[1], first, 0)):
+        out[0:cells, :] = row[0]
+        out[cells : cells + 2, :] = sides[at : at + 2, :]
+        out[cells + 2 : cells + 16, :] = jnp.zeros((14, row.shape[2]), jnp.bfloat16)
 
 
 def flux_pick_body(sends, cells, out, even):
@@ -269,7 +283,8 @@
         span = count * cells
         for step in range(count + 2):
             row = first - 1 + step
-            values = jnp.dot(rows[place + step][0], take, preferred_element_type=jnp.float32)
+            values = rows[place + step][0, 0 : cells + 16] if row in halos else rows[place + step][0]
+            values = jnp.dot(values, take, preferred_element_type=jnp.float32)
             if row in halos:
                 left, right = values[cells : cells + 1], values[cells + 1 : cells + 2]
             else:
@@ -309,8 +324,8 @@
     return half + half * jnp.tanh(inner)
 
 
-def gather_weights_body(chan, up, down, ocean_up, ocean_down, *refs):
-    pieces, (across, back, ocean_across, ocean_back) = refs[:4], refs[4:]
+def gather_weights_body(chan, up, down, ocean_up, ocean_down, gain, ocean_gain, *refs):
+    pieces, (across, back, ocean_across, ocean_back, gains, ocean_gains) = refs[:4], refs[4:]
     hidden, channels = up.shape
     width = channels // 2
     depth, shallow = hidden // 4, ocean_up.shape[0] // 4
@@ -324,6 +339,13 @@
     target = jnp.where(inside < half, 2 * inside, 2 * (inside - half) + 1)
     target = target + jnp.where(rows < width, own, width - own)
     order = (target == lax.broadcasted_iota(jnp.int32, shape, 1)).astype(jnp.bfloat16)
+    gains[...] = lax.dot_general(
+        jnp.broadcast_to(gain[...].reshape(1, channels), (8, channels)),
+        order.astype(jnp.float32),
+        NT,
+        precision=lax.Precision.HIGHEST,
+        preferred_element_type=jnp.float32,
+    )[0:1]
     for part in range(8):
         at = slice(part * depth, (part + 1) * depth)
         block = up[at, :] if part < 4 else pieces[part - 4][0:depth, 0:channels]
@@ -334,6 +356,11 @@
     own = chan[0] * narrow
     mine = pl.ds(pl.multiple_of(own, 128), narrow)
     theirs = pl.ds(pl.multiple_of(narrow - own, 128), narrow)
+    wide = ocean_gain[...].reshape(1, 2 * narrow)
+    first, second = wide[:, 0:narrow], wide[:, narrow:]
+    low = jnp.full((1, narrow), chan[0], jnp.int32) == 0
+    ocean_gains[:, 0:narrow] = jnp.where(low, first, second)
+    ocean_gains[:, narrow:] = jnp.where(low, second, first)
     count = ocean_up.shape[0]
     ocean_across[0:count, 0:narrow] = ocean_up[:, mine]
     ocean_across[0:count, narrow : 2 * narrow] = ocean_up[:, theirs]
@@ -407,21 +434,43 @@
         out[:, lanes] = (a + mask[tile].astype(jnp.float32) * delta).astype(jnp.bfloat16)
 
 
-def far_weights(up, down, ocean_up, ocean_down):
-    chan = lax.axis_index("chan")
+def pack_body(place, up, down, ocean_up, ocean_down, out):
+    depth, channels = up.shape
+    half, narrow = ocean_up.shape[0] // 2, ocean_down.shape[1]
+    out[0:depth, 0:channels] = up[...]
+    out[0:depth, channels:] = down[...]
+    for side in range(2):
+        base, rows = side * 3 * narrow, slice(side * half, (side + 1) * half)
+        out[depth:, base : base + 2 * narrow] = ocean_up[rows, :]
+        out[depth:, base + 2 * narrow : base + 3 * narrow] = ocean_down[rows, :]
+
+
+def pack_weights(up, down, ocean_up, ocean_down):
     quarter = lax.axis_index("groups") * 2 + lax.axis_index("pair")
+    place = jnp.stack([quarter, 1 - lax.axis_index("chan")])
     depth, shallow = up.shape[0] // 4, ocean_up.shape[0] // 4
     width, narrow = up.shape[1] // 2, ocean_up.shape[1] // 2
-    first = lax.dynamic_slice(up, (quarter * depth, 0), (depth, 2 * width))
-    second = lax.dynamic_slice(down, (quarter * depth, (1 - chan) * width), (depth, width))
-    third = lax.dynamic_slice(ocean_up, (quarter * shallow, 0), (shallow, 2 * narrow))
-    fourth = lax.dynamic_slice(ocean_down, (quarter * shallow, (1 - chan) * narrow), (shallow, narrow))
-    low = jnp.concatenate([third, fourth], axis=1)
-    low = jnp.concatenate([low[: shallow // 2], low[shallow // 2 :]], axis=1)
-    packed = jnp.concatenate([jnp.concatenate([first, second], axis=1), low], axis=0)
-    one = lax.ppermute(packed, "chan", SWAP)
-    two = lax.ppermute(one, "groups", SWAP)
-    return one, two, lax.ppermute(one, "pair", SWAP), lax.ppermute(two, "pair", SWAP)
+    shape = (depth + shallow // 2, 3 * width)
+    return pl.pallas_call(
+        pack_body,
+        grid_spec=pltpu.PrefetchScalarGridSpec(
+            num_scalar_prefetch=1,
+            grid=(1,),
+            in_specs=[
+                pl.BlockSpec((depth, 2 * width), lambda _, place: (place[0], 0)),
+                pl.BlockSpec((depth, width), lambda _, place: (place[0], place[1])),
+                pl.BlockSpec((shallow, 2 * narrow), lambda _, place: (place[0], 0)),
+                pl.BlockSpec((shallow, narrow), lambda _, place: (place[0], place[1])),
+            ],
+            out_specs=pl.BlockSpec(shape, lambda _, place: (0, 0)),
+        ),
+        out_shape=jax.ShapeDtypeStruct(shape, up.dtype),
+        compiler_params=pltpu.CompilerParams(vmem_limit_bytes=60 * 2**20),
+    )(place, up, down, ocean_up, ocean_down)
+
+
+def after(value, *earlier):
+    return lax.optimization_barrier((value, *earlier))[0]
 
 
 def quick_shards(
@@ -455,53 +504,22 @@
     sea_rows = sea_pattern.transpose(2, 0, 1)
     flux_rows = flux_pattern.transpose(2, 0, 1)
 
-    sides = jnp.stack([field[:, lon_cells - 1, :], field[:, 0, :]], axis=1).reshape(2 * lat_rows, channels)
+    packed = pack_weights(atmos_up, atmos_down, ocean_up, ocean_down)
+    one = lax.ppermute(packed, "chan", SWAP)
+    sides = local_call(
+        sides_body,
+        jax.ShapeDtypeStruct((2 * lat_rows, channels), bf16),
+        (after(field, packed), field),
+        [
+            pl.BlockSpec((lat_rows, 16, channels), lambda _: (0, lon_cells // 16 - 1, 0)),
+            pl.BlockSpec((lat_rows, 16, channels), lambda _: (0, 0, 0)),
+        ],
+        vmem(),
+        60,
+        moved=2**18,
+    )
     sides = lax.ppermute(sides, "pair", SWAP)
-    pieces = far_weights(atmos_up, atmos_down, ocean_up, ocean_down)
-
-    sea_out = local_call(
-        sea_pick_body,
-        jax.ShapeDtypeStruct((sea_sends.size, 128, flux_depth), bf16),
-        (sea_sends.reshape(1, 1, -1), ocean_state),
-        [smem(), vmem()],
-        vmem(),
-        8,
-        moved=2**20,
-    )
-    sea_in = lax.all_to_all(sea_out, peers, split_axis=0, concat_axis=0, tiled=True)
-
-    fill = jnp.zeros((14, channels), bf16)
-    up_chain = [(i, i + 1) for i in range(lat_bands - 1)]
-    down_chain = [(i + 1, i) for i in range(lat_bands - 1)]
-    low = lax.ppermute(jnp.concatenate([field[lat_rows - 1], sides[-2:], fill], axis=0), "lat", up_chain)
-    high = lax.ppermute(jnp.concatenate([field[0], sides[:2], fill], axis=0), "lat", down_chain)
-
-    flux_out = local_call(
-        flux_pick_body,
-        jax.ShapeDtypeStruct((flux_sends.size, flux_depth, 128), bf16),
-        (flux_sends, field.reshape(lat_rows * lon_cells, channels)),
-        [smem(), vmem()],
-        vmem(),
-        24,
-        scratch=[pltpu.VMEM((lat_rows * lon_cells // 128, flux_depth, 128), bf16)],
-        flops=2 * lat_rows * lon_cells * channels * flux_depth,
-        moved=6 * 2**20,
-    )
-    flux_in = lax.all_to_all(flux_out, peers, split_axis=0, concat_axis=0, tiled=True)
-
-    entries = sea_pattern.shape[1]
-    sea = local_call(
-        sea_products_body,
-        jax.ShapeDtypeStruct((entries, 128, flux_depth), f32),
-        (sea_rows, sea_in, remap_blocks),
-        [smem(), vmem(), vmem()],
-        vmem(),
-        16,
-        flops=2 * entries * 128 * 128 * flux_depth,
-        moved=4 * 2**20,
-    )
-
-    def smooth_rows(odd, runs):
+    def smooth_rows(odd, runs, field):
         operands, specs, marked = [], [], []
         for first, count in runs:
             halos = []
@@ -537,51 +555,109 @@
 
     edge = lat_rows // 4
     middle = [(edge, lat_rows - 2 * edge)]
-    ends = [(0, edge), (lat_rows - edge, edge)]
-    plan = []
-    for runs in (middle, ends):
-        evens = smooth_rows(0, runs)
-        others = [lax.ppermute(value, "chan", SWAP) for value in evens]
-        odds = smooth_rows(1, runs)
-        others_odd = [lax.ppermute(value, "chan", SWAP) for value in odds]
-        plan += list(zip(runs, evens, odds, others, others_odd))
-
-    across, back, ocean_across, ocean_back = local_call(
+    ends_runs = [(0, edge), (lat_rows - edge, edge)]
+
+    def cross(values):
+        return [lax.ppermute(value, "chan", SWAP) for value in values]
+
+    evens = smooth_rows(0, middle, field)
+    others = cross(evens)
+    row = jax.ShapeDtypeStruct((lon_cells + 16, channels), bf16)
+    messages = local_call(
+        edges_body,
+        [row, row],
+        (after(field, *evens), field, sides),
+        [
+            pl.BlockSpec((1, lon_cells, channels), lambda _: (lat_rows - 1, 0, 0)),
+            pl.BlockSpec((1, lon_cells, channels), lambda _: (0, 0, 0)),
+            vmem(),
+        ],
+        [vmem()] * 2,
+        40,
+        moved=2**20,
+    )
+    low = lax.ppermute(messages[0], "lat", [(i, i + 1) for i in range(lat_bands - 1)])
+    high = lax.ppermute(messages[1], "lat", [(i + 1, i) for i in range(lat_bands - 1)])
+    sea_out = local_call(
+        sea_pick_body,
+        jax.ShapeDtypeStruct((sea_sends.size, 128, flux_depth), bf16),
+        (sea_sends.reshape(1, 1, -1), after(ocean_state, *messages)),
+        [smem(), vmem()],
+        vmem(),
+        60,
+        moved=2**20,
+    )
+    sea_in = lax.all_to_all(sea_out, peers, split_axis=0, concat_axis=0, tiled=True)
+    flux_out = local_call(
+        flux_pick_body,
+        jax.ShapeDtypeStruct((flux_sends.size, flux_depth, 128), bf16),
+        (flux_sends, after(field, sea_out).reshape(lat_rows * lon_cells, channels)),
+        [smem(), vmem()],
+        vmem(),
+        24,
+        scratch=[pltpu.VMEM((lat_rows * lon_cells // 128, flux_depth, 128), bf16)],
+        flops=2 * lat_rows * lon_cells * channels * flux_depth,
+        moved=6 * 2**20,
+    )
+
+    entries = sea_pattern.shape[1]
+    sea = local_call(
+        sea_products_body,
+        jax.ShapeDtypeStruct((entries, 128, flux_depth), f32),
+        (sea_rows, sea_in, after(remap_blocks, flux_out)),
+        [smem(), vmem(), vmem()],
+        vmem(),
+        16,
+        flops=2 * entries * 128 * 128 * flux_depth,
+        moved=4 * 2**20,
+    )
+    odds = smooth_rows(1, middle, field)
+    others_odd = cross(odds)
+    plan = list(zip(middle, evens, odds, others, others_odd))
+    flux_in = lax.all_to_all(after(flux_out, low, high, *others, one), peers, split_axis=0, concat_axis=0, tiled=True)
+    two = lax.ppermute(after(one, sea), "groups", SWAP)
+    ends_even = smooth_rows(0, ends_runs, after(field, *odds))
+    others_even = cross(ends_even)
+    odds = smooth_rows(1, ends_runs, after(field, *ends_even, one))
+    others_odd = cross(odds)
+    three, four = lax.ppermute(after(one, *odds), "pair", SWAP), lax.ppermute(after(two, *odds), "pair", SWAP)
+    pieces = one, two, three, four
+    plan += list(zip(ends_runs, ends_even, odds, others_even, others_odd))
+
+    across, back, ocean_across, ocean_back, gain, gain_ocean = local_call(
         gather_weights_body,
         [
             jax.ShapeDtypeStruct((2 * channels, hidden), bf16),
             jax.ShapeDtypeStruct((hidden, channels), bf16),
             jax.ShapeDtypeStruct((ocean_hidden, 2 * flux_depth), bf16),
             jax.ShapeDtypeStruct((ocean_hidden, flux_depth), bf16),
+            jax.ShapeDtypeStruct((1, 2 * channels), f32),
+            jax.ShapeDtypeStruct((1, 2 * flux_depth), f32),
         ],
-        (chan, atmos_up, atmos_down, ocean_up, ocean_down, *pieces),
-        [smem()] + [vmem()] * 8,
-        [vmem()] * 4,
+        (chan, after(atmos_up, *odds), atmos_down, ocean_up, ocean_down, atmos_gain, ocean_gain, *pieces),
+        [smem()] + [vmem()] * 10,
+        [vmem()] * 6,
         32,
         flops=8 * hidden * channels * channels,
         moved=8 * 2**20,
     )
-    gain = atmos_gain.reshape(2, channels // 2, 2)
-    gain = jnp.where(lax.axis_index("chan") == 0, gain, gain[::-1]).transpose(0, 2, 1).reshape(1, 2 * channels)
-    gain_ocean = ocean_gain.reshape(2, flux_depth)
-    gain_ocean = jnp.where(lax.axis_index("chan") == 0, gain_ocean, gain_ocean[::-1]).reshape(1, 2 * flux_depth)
-
-    entries = flux_pattern.shape[1]
-    ocean_input = local_call(
-        flux_remap_body,
-        jax.ShapeDtypeStruct((flux_depth, ocean_cells), bf16),
-        (flux_rows, flux_in, remap_blocks, ocean_state),
-        [smem(), vmem(), vmem(), vmem()],
-        vmem(),
-        16,
-        scratch=[pltpu.VMEM((ocean_count, flux_depth, 128), f32)],
-        flops=2 * entries * 128 * 128 * flux_depth,
-        moved=5 * 2**20,
-    )
-    ocean_other = lax.ppermute(ocean_input, "chan", SWAP)
-
     result = None
-    for (first, count), *values in plan:
+    for step, ((first, count), *values) in enumerate(plan):
+        if step == len(plan) - 1:
+            entries = flux_pattern.shape[1]
+            ocean_input = local_call(
+                flux_remap_body,
+                jax.ShapeDtypeStruct((flux_depth, ocean_cells), bf16),
+                (flux_rows, flux_in, after(remap_blocks, result), ocean_state),
+                [smem(), vmem(), vmem(), vmem()],
+                vmem(),
+                16,
+                scratch=[pltpu.VMEM((ocean_count, flux_depth, 128), f32)],
+                flops=2 * entries * 128 * 128 * flux_depth,
+                moved=5 * 2**20,
+            )
+            ocean_other = lax.ppermute(ocean_input, "chan", SWAP)
+            result = after(result, ocean_input)
         operands = [*values, gain, across, back]
         specs = [pl.BlockSpec((lon_cells, channels // 2), lambda step: (step, 0))] * 4 + [vmem()] * 3
         aliases = {}
@@ -605,7 +681,7 @@
     ocean_next = local_call(
         ocean_layer_body,
         jax.ShapeDtypeStruct((flux_depth, ocean_cells), bf16),
-        (ocean_mask, ocean_input, ocean_other, gain_ocean, ocean_across, ocean_back),
+        (ocean_mask, after(ocean_input, result), ocean_other, gain_ocean, ocean_across, ocean_back),
         [smem()] + [vmem()] * 5,
         vmem(),
         16,
@@ -635,6 +711,6 @@
         P(("lat", "pair")),
     )
     out_specs = (P("chan", ("groups", "lat"), "pair"), P("chan", ("groups", "lat", "pair")))
-    paired = all(mesh.shape[axis] == 2 for axis in ("groups", "chan", "pair"))
+    paired = all(mesh.shape[axis] == 2 for axis in ("groups", "chan", "pair")) and mesh.shape["lat"] > 2
     body = quick_shards if paired else shards
     return jax.shard_map(body, mesh=mesh, in_specs=in_specs, out_specs=out_specs, check_vma=False)

time: 150 us -> 117 us (0.78)
  waiting for transfers between devices: 43.5 us -> 14.3 us
  local copies, waits for them, and re-layouts: 10.4 us -> 6.86 us
  Pallas kernels: 62.9 us -> 65.3 us
  other arithmetic: 2.63 us -> 0.65 us
  starting transfers between devices: 28.6 us -> 27 us
    ppermute x12, waiting for transfers between devices: 42.5 us -> 12.9 us  [the longest x1 4.51 us: quick_shards(): lax.ppermute(messages[0], 'lat', [(i, i + 1) for i in range(lat_bands - 1)])]
    dynamic_slice x4 -> x0, local copies, waits for them, and re-layouts: 3.51 us -> none  [the longest x1 0.98 us: far_weights(): first = lax.dynamic_slice(up, (quarter * depth, 0), (depth, 2 * width))]
    pallas_call x0 -> x1, Pallas kernels: none -> 2.5 us  [pack_weights(): pl.pallas_call(pack_body, grid_spec=pltpu.PrefetchScalarGridSpec(num_scal...]
    concatenate x3 -> x0, other arithmetic: 1.93 us -> none  [the longest x1 1.11 us: quick_shards(): jnp.concatenate([field[0], sides[:2], fill], axis=0)]
    unnamed x58 -> x48, local copies, waits for them, and re-layouts: 5.58 us -> 6.86 us
    pallas_call x13 -> x15, Pallas kernels: 62.9 us -> 62.8 us  [local_call(): pl.pallas_call(body, grid=(grid,), out_shape=out_shape, in_specs=in_specs...]
  transfers between devices with their start and end apart: 16 -> 16, of which waited for: 5 -> 7; matrix products, arithmetic and copies ran while one was open for 5% -> 0% of each run, Pallas kernels for 38% -> 47%
where the time goes in v3:
time: 117 us; the launch traced here: 115 us
  Pallas kernels  65.3 us (56%)
  starting transfers between devices  27 us (23%)
  waiting for transfers between devices  14.3 us (12%)
  local copies, waits for them, and re-layouts  6.86 us (6%)
    pallas_call x15, Pallas kernels, local_call(): pl.pallas_call(body, grid=(grid,), out_shape=out_shape, in_specs=in_specs...  62.8 us
    ppermute x6, starting transfers between devices, cross(): return [lax.ppermute(value, 'chan', SWAP) for value in values]  7.1 us
    unnamed x48, local copies, waits for them, and re-layouts  6.86 us
    all_to_all x1, starting transfers between devices, quick_shards(): lax.all_to_all(after(flux_out, low, high, *others, one), peers, split_axi...  5.21 us
    all_to_all x1, starting transfers between devices, quick_shards(): lax.all_to_all(sea_out, peers, split_axis=0, concat_axis=0, tiled=True)  5.21 us
    ppermute x1, waiting for transfers between devices, quick_shards(): lax.ppermute(messages[0], 'lat', [(i, i + 1) for i in range(lat_bands - 1)])  4.51 us
    ppermute x1, waiting for transfers between devices, quick_shards(): two = lax.ppermute(after(one, sea), 'groups', SWAP)  3.38 us
    ppermute x1, starting transfers between devices, quick_shards(): lax.ppermute(messages[0], 'lat', [(i, i + 1) for i in range(lat_bands - 1)])  3.36 us
  transfers between devices with their start and end apart: 16, of which 7 were waited for; matrix products, arithmetic and copies ran while one was open for 0% of the time, Pallas kernels for 47%

profile of v3, /device:TPU:16, one launch (start us, length us, event | category | flops | bytes accessed | tf_op | source)
XLA Modules:
  0.0 115.1 jit_solution(13709810507578450690)
XLA Ops:
  1.3 2.5 %shard_map.158 = bf16[320,768]{1,0:T(8,128)(2,1)} custom-call(s32[2]{0:T(128)} %pad_add_fusion.place, bf16[1024,512]{1,0:T(8,128)(2,1)} %up.2, bf16[1024,512]{1,0:T(8,128)(2,1)} %down.3, bf16[512,256]{1,0:T(8,128)(2,1)} %ocean_up.3, bf16[512,256]{1,0:T(8,128)(2,1)} %ocean_down.3), custom_call_target="tpu_custom_call" | custom-call | tf_op jit(solution)/shard_map/pallas_call | solution.py:454
  3.8 1.6 %shard_map.159 = bf16[16,256]{1,0:T(8,128)(2,1)} custom-call(bf16[8,720,256]{2,1,0:T(8,128)(2,1)} %bitcast.12, bf16[8,720,256]{2,1,0:T(8,128)(2,1)} %bitcast.13), custom_call_target="tpu_custom_call" | custom-call | flops 1 | bytes 1 | tf_op jit(solution)/shard_map/pallas_call | solution.py:187
  5.4 1.4 %collective-permute-done.refs_6_.sides.refs_8_ = bf16[16,256]{1,0:T(8,128)(2,1)S(1)} collective-permute-done((bf16[16,256]{1,0:T(8,128)(2,1)}, bf16[16,256]{1,0:T(8,128)(2,1)S(1)}, u32[]{:S(2)}, u32[]{:S(2)}) %collective-permute-start) | collective-permute-done | bytes 8224 | tf_op jit(solution)/shard_map/ppermute | solution.py:521
  6.8 2.1 %shard_map.160.own_even = bf16[2880,128]{1,0:T(8,128)(2,1)} custom-call(bf16[8,720,256]{2,1,0:T(8,128)(2,1)S(1)} %bitcast.14, bf16[8,720,256]{2,1,0:T(8,128)(2,1)S(1)} %bitcast.15, bf16[8,720,256]{2,1,0:T(8,128)(2,1)S(1)} %bitcast.16, bf16[8,720,256]{2,1,0:T(8,128)(2,1)S(1)} %bitcast.17, bf16[8,720,256]{2,1,0:T(8,128)(2,1)S(1)} %bitcast.18, ...), custom_call_target="tpu_custom_call" | custom-call | flops 1 | bytes 1 | tf_op jit(solution)/shard_map/pallas_call | solution.py:187
  8.9 1.5 %collective-permute-start.11 = (bf16[2880,128]{1,0:T(8,128)(2,1)}, bf16[2880,128]{1,0:T(8,128)(2,1)}, u32[]{:S(2)}, u32[]{:S(2)}) collective-permute-start(bf16[2880,128]{1,0:T(8,128)(2,1)} %shard_map.160.own_even), channel_id=1, source_target_pairs={{0,2},{2,0},{1,3},{3,1},{4,6},{6,4},{5,7},{7,5},{8,10},{10,8},{9,1... | collective-permute-start | bytes 2211848 | tf_op jit(solution)/shard_map/ppermute | solution.py:561
  12.5 1.8 %shard_map.162 = bf16[8,128,128]{2,1,0:T(8,128)(2,1)} custom-call(s32[1,1,8]{2,1,0:T(1,128)} %bitcast.54, bf16[128,1024]{1,0:T(8,128)(2,1)} %ocean.2), custom_call_target="tpu_custom_call" | custom-call | flops 1 | bytes 1 | tf_op jit(solution)/shard_map/pallas_call | solution.py:187
  14.3 5.2 %all-to-all-start = ((bf16[8,128,128]{2,1,0:T(8,128)(2,1)}), bf16[8,128,128]{2,1,0:T(8,128)(2,1)}, u32[]{:S(2)}, u32[]{:S(2)}) async-start(bf16[8,128,128]{2,1,0:T(8,128)(2,1)} %shard_map.162), calls=%async_computation | async-start | bytes 524288 | tf_op jit(solution)/shard_map/all_to_all | solution.py:590
  19.5 3.4 %collective-permute-start.1 = (bf16[736,256]{1,0:T(8,128)(2,1)}, bf16[736,256]{1,0:T(8,128)(2,1)S(1)}, u32[]{:S(2)}, u32[]{:S(2)}) collective-permute-start(bf16[736,256]{1,0:T(8,128)(2,1)} %copy-done.23), channel_id=1, source_target_pairs={{0,4},{4,8},{8,12},{1,5},{5,9},{9,13},{2,6},{6,10},{10,14},{3,7},{... | collective-permute-start | bytes 1130504 | tf_op jit(solution)/shard_map/ppermute | solution.py:579
  22.8 2.5 %collective-permute-start.2 = (bf16[736,256]{1,0:T(8,128)(2,1)}, bf16[736,256]{1,0:T(8,128)(2,1)S(1)}, u32[]{:S(2)}, u32[]{:S(2)}) collective-permute-start(bf16[736,256]{1,0:T(8,128)(2,1)} %copy-done.22), channel_id=1, source_target_pairs={{4,0},{8,4},{12,8},{5,1},{9,5},{13,9},{6,2},{10,6},{14,10},{7,3},{... | collective-permute-start | bytes 1130504 | tf_op jit(solution)/shard_map/ppermute | solution.py:580
  25.3 3.5 %shard_map.163 = bf16[64,128,128]{2,1,0:T(8,128)(2,1)S(1)} custom-call(s32[1,8,8]{2,1,0:T(8,128)S(1)} %copy-done.17, bf16[5760,256]{1,0:T(8,128)(2,1)S(1)} %bitcast.22), custom_call_target="tpu_custom_call" | custom-call | flops 1 | bytes 1 | tf_op jit(solution)/shard_map/pallas_call | solution.py:187
  30.2 4.5 %collective-permute-done.1 = bf16[736,256]{1,0:T(8,128)(2,1)S(1)} collective-permute-done((bf16[736,256]{1,0:T(8,128)(2,1)}, bf16[736,256]{1,0:T(8,128)(2,1)S(1)}, u32[]{:S(2)}, u32[]{:S(2)}) %collective-permute-start.1) | collective-permute-done | bytes 376864 | tf_op jit(solution)/shard_map/ppermute | solution.py:579
  36.2 2.0 %collective-permute-done.3.refs_0_ = bf16[320,768]{1,0:T(8,128)(2,1)} collective-permute-done((bf16[320,768]{1,0:T(8,128)(2,1)}, bf16[320,768]{1,0:T(8,128)(2,1)}, u32[]{:S(2)}, u32[]{:S(2)}) %collective-permute-start.3) | collective-permute-done | bytes 491552 | tf_op jit(solution)/shard_map/ppermute | solution.py:508
  38.3 5.2 %all-to-all-start.1 = ((bf16[64,128,128]{2,1,0:T(8,128)(2,1)}), bf16[64,128,128]{2,1,0:T(8,128)(2,1)}, u32[]{:S(2)}, u32[]{:S(2)}) async-start(bf16[64,128,128]{2,1,0:T(8,128)(2,1)} %copy-done.3), calls=%async_computation.1 | async-start | bytes 4194304 | tf_op jit(solution)/shard_map/all_to_all | solution.py:617
  43.5 1.6 %copy-done.1 = bf16[64,128,128]{2,1,0:T(8,128)(2,1)S(1)} copy-done((bf16[64,128,128]{2,1,0:T(8,128)(2,1)S(1)}, bf16[64,128,128]{2,1,0:T(8,128)(2,1)}, u32[]{:S(2)}) %copy-start.1) | copy-done | bytes 2097176
  45.1 1.5 %shard_map.164.refs_9_.refs_11_ = f32[16,128,128]{2,1,0:T(8,128)S(1)} custom-call(s32[3,1,16]{2,1,0:T(1,128)S(1)} %bitcast.49, bf16[8,128,128]{2,1,0:T(8,128)(2,1)} %all-to-all-done.slots, bf16[64,128,128]{2,1,0:T(8,128)(2,1)S(1)} %copy-done.1), custom_call_target="tpu_custom_call" | custom-call | flops 1 | bytes 1 | tf_op jit(solution)/shard_map/pallas_call | solution.py:187
  46.6 1.6 %collective-permute-start.6 = (bf16[320,768]{1,0:T(8,128)(2,1)}, bf16[320,768]{1,0:T(8,128)(2,1)S(1)}, u32[]{:S(2)}, u32[]{:S(2)}) collective-permute-start(bf16[320,768]{1,0:T(8,128)(2,1)} %collective-permute-done.3.refs_0_), channel_id=1, source_target_pairs={{0,16},{16,0},{1,17},{17,1},{2,18},{18,2},{3,19},{19,3},{4,20},{20... | collective-permute-start | bytes 1474568 | tf_op jit(solution)/shard_map/ppermute | solution.py:618
  48.2 1.9 %shard_map.165.own_odd = bf16[2880,128]{1,0:T(8,128)(2,1)S(1)} custom-call(bf16[8,720,256]{2,1,0:T(8,128)(2,1)S(1)} %bitcast.25, bf16[8,720,256]{2,1,0:T(8,128)(2,1)S(1)} %bitcast.24, bf16[8,720,256]{2,1,0:T(8,128)(2,1)S(1)} %bitcast.23, bf16[8,720,256]{2,1,0:T(8,128)(2,1)S(1)} %bitcast.26, bf16[8,720,256]{2,1,0:T(8,128)(2,1)S(1)} %bitcast.27, ...), custom_call_target="tpu_custom_call" | custom-call | flops 1 | bytes 1 | tf_op jit(solution)/shard_map/pallas_call | solution.py:187
  50.1 1.6 %collective-permute-start.12 = (bf16[2880,128]{1,0:T(8,128)(2,1)S(1)}, bf16[2880,128]{1,0:T(8,128)(2,1)S(1)}, u32[]{:S(2)}, u32[]{:S(2)}) collective-permute-start(bf16[2880,128]{1,0:T(8,128)(2,1)S(1)} %shard_map.165.own_odd), channel_id=1, source_target_pairs={{0,2},{2,0},{1,3},{3,1},{4,6},{6,4},{5,7},{7,5},{8,10},{10,8},{9,1... | collective-permute-start | bytes 2211848 | tf_op jit(solution)/shard_map/ppermute | solution.py:561
  51.7 1.9 %shard_map.166 = (bf16[1440,128]{1,0:T(8,128)(2,1)S(1)}, bf16[1440,128]{1,0:T(8,128)(2,1)}) custom-call(bf16[1,736,256]{2,1,0:T(8,128)(2,1)S(1)} %bitcast.41, bf16[8,720,256]{2,1,0:T(8,128)(2,1)S(1)} %bitcast.29, bf16[8,720,256]{2,1,0:T(8,128)(2,1)S(1)} %bitcast.30, bf16[8,720,256]{2,1,0:T(8,128)(2,1)S(1)} %bitcast.31, bf16[8,720,256]{2,1,0:T(8,128)(2,1)S(1)} %bitcast.32, ...), custom_call_target="tpu_custom_call" | custom-call | flops 1 | bytes 1 | tf_op jit(solution)/shard_map/pallas_call | solution.py:187
  53.7 3.1 %shard_map.167 = (bf16[1440,128]{1,0:T(8,128)(2,1)S(1)}, bf16[1440,128]{1,0:T(8,128)(2,1)}) custom-call(bf16[1,736,256]{2,1,0:T(8,128)(2,1)S(1)} %bitcast.42, bf16[8,720,256]{2,1,0:T(8,128)(2,1)S(1)} %bitcast.35, bf16[8,720,256]{2,1,0:T(8,128)(2,1)S(1)} %bitcast.36, bf16[8,720,256]{2,1,0:T(8,128)(2,1)S(1)} %bitcast.37, bf16[8,720,256]{2,1,0:T(8,128)(2,1)S(1)} %bitcast.38, ...), custom_call_target="tpu_custom_call" | custom-call | flops 1 | bytes 1 | tf_op jit(solution)/shard_map/pallas_call | solution.py:187
  56.8 3.4 %collective-permute-done.6.refs_1_ = bf16[320,768]{1,0:T(8,128)(2,1)S(1)} collective-permute-done((bf16[320,768]{1,0:T(8,128)(2,1)}, bf16[320,768]{1,0:T(8,128)(2,1)S(1)}, u32[]{:S(2)}, u32[]{:S(2)}) %collective-permute-start.6) | collective-permute-done | bytes 491552 | tf_op jit(solution)/shard_map/ppermute | solution.py:618
  60.2 1.5 %collective-permute-start.9 = (bf16[1440,128]{1,0:T(8,128)(2,1)S(1)}, bf16[1440,128]{1,0:T(8,128)(2,1)S(1)}, u32[]{:S(2)}, u32[]{:S(2)}) collective-permute-start(bf16[1440,128]{1,0:T(8,128)(2,1)S(1)} %get-tuple-element.38.own_even), channel_id=1, source_target_pairs={{0,2},{2,0},{1,3},{3,1},{4,6},{6,4},{5,7},{7,5},{8,10},{10,8},{9,1... | collective-permute-start | bytes 1105928 | tf_op jit(solution)/shard_map/ppermute | solution.py:561
  62.2 1.5 %collective-permute-start.4 = (bf16[1440,128]{1,0:T(8,128)(2,1)}, bf16[1440,128]{1,0:T(8,128)(2,1)}, u32[]{:S(2)}, u32[]{:S(2)}) collective-permute-start(bf16[1440,128]{1,0:T(8,128)(2,1)} %get-tuple-element.37.own_even), channel_id=1, source_target_pairs={{0,2},{2,0},{1,3},{3,1},{4,6},{6,4},{5,7},{7,5},{8,10},{10,8},{9,1... | collective-permute-start | bytes 1105928 | tf_op jit(solution)/shard_map/ppermute | solution.py:561
  64.3 3.4 %shard_map.168 = (bf16[512,2048]{1,0:T(8,128)(2,1)S(1)}, bf16[2048,256]{1,0:T(8,128)(2,1)S(1)}, bf16[1024,256]{1,0:T(8,128)(2,1)S(1)}, bf16[1024,128]{1,0:T(8,12...) custom-call(s32[1]{0:T(128)} %bitcast.9.chan, bf16[1024,512]{1,0:T(8,128)(2,1)S(1)} %copy-done.4, ...), custom_call_target="tpu_custom_call" | custom-call | flops 1 | bytes 1 | tf_op jit(solution)/shard_map/pallas_call | solution.py:187
  67.7 1.9 %collective-permute-done.12.other_odd = bf16[2880,128]{1,0:T(8,128)(2,1)S(1)} collective-permute-done((bf16[2880,128]{1,0:T(8,128)(2,1)S(1)}, bf16[2880,128]{1,0:T(8,128)(2,1)S(1)}, u32[]{:S(2)}, u32[]{:S(2)}) %collective-permute-start.12) | collective-permute-done | bytes 737312 | tf_op jit(solution)/shard_map/ppermute | solution.py:561
  69.6 15.4 %shard_map.169.refs_0_ = bf16[8,720,256]{2,1,0:T(8,128)(2,1)} custom-call(bf16[2880,128]{1,0:T(8,128)(2,1)} %shard_map.160.own_even, bf16[2880,128]{1,0:T(8,128)(2,1)S(1)} %shard_map.165.own_odd, bf16[2880,128]{1,0:T(8,128)(2,1)} %collective-permute-done.11.other_even, bf16[2880,128]{1,0:T(8,128)(2,1)S(1)} %collective-permute-done.12.other_odd, ...), custom_call_target="tpu_custom_call" | custom-call | flops 1 | bytes 1 | tf_op jit(solution)/shard_map/pallas_call | solution.py:187
  85.4 7.5 %shard_map.170.refs_0_ = bf16[8,720,256]{2,1,0:T(8,128)(2,1)} custom-call(bf16[1440,128]{1,0:T(8,128)(2,1)S(1)} %get-tuple-element.38.own_even, bf16[1440,128]{1,0:T(8,128)(2,1)S(1)} %get-tuple-element.41.own_odd, bf16[1440,128]{1,0:T(8,128)(2,1)S(1)} %collective-permute-done.9.other_even, ...), custom_call_target="tpu_custom_call", output_to_operand_aliasing={{}: (7, {})} | custom-call | flops 1 | bytes 1 | tf_op jit(solution)/shard_map/pallas_call | solution.py:187
  92.9 1.6 %copy-done.2 = bf16[64,128,128]{2,1,0:T(8,128)(2,1)S(1)} copy-done((bf16[64,128,128]{2,1,0:T(8,128)(2,1)S(1)}, bf16[64,128,128]{2,1,0:T(8,128)(2,1)}, u32[]{:S(2)}) %copy-start.2) | copy-done | bytes 2097176
  94.5 5.4 %shard_map.171.own = bf16[128,1024]{1,0:T(8,128)(2,1)S(1)} custom-call(s32[3,1,128]{2,1,0:T(1,128)S(1)} %bitcast.52, bf16[64,128,128]{2,1,0:T(8,128)(2,1)} %all-to-all-done.1.slots, bf16[64,128,128]{2,1,0:T(8,128)(2,1)S(1)} %copy-done.2, bf16[128,1024]{1,0:T(8,128)(2,1)S(1)} %copy-done.10), custom_call_target="tpu_custom_call" | custom-call | flops 1 | bytes 1 | tf_op jit(solution)/shard_map/pallas_call | solution.py:187
  99.9 1.6 %collective-permute-start.13 = (bf16[128,1024]{1,0:T(8,128)(2,1)S(1)}, bf16[128,1024]{1,0:T(8,128)(2,1)S(1)}, u32[]{:S(2)}, u32[]{:S(2)}) collective-permute-start(bf16[128,1024]{1,0:T(8,128)(2,1)S(1)} %shard_map.171.own), channel_id=1, source_target_pairs={{0,2},{2,0},{1,3},{3,1},{4,6},{6,4},{5,7},{7,5},{8,10},{10,8},{9,1... | collective-permute-start | bytes 786440 | tf_op jit(solution)/shard_map/ppermute | solution.py:659
  101.5 8.7 %shard_map.172 = bf16[8,720,256]{2,1,0:T(8,128)(2,1)} custom-call(bf16[1440,128]{1,0:T(8,128)(2,1)} %get-tuple-element.37.own_even, bf16[1440,128]{1,0:T(8,128)(2,1)} %get-tuple-element.40.own_odd, bf16[1440,128]{1,0:T(8,128)(2,1)} %collective-permute-done.4.other_even, ...), custom_call_target="tpu_custom_call", output_to_operand_aliasing={{}: (7, {})} | custom-call | flops 1 | bytes 1 | tf_op jit(solution)/shard_map/pallas_call | solution.py:187
  110.3 4.8 %shard_map.173 = bf16[128,1024]{1,0:T(8,128)(2,1)} custom-call(s32[8]{0:T(128)S(1)} %copy-done.21, bf16[128,1024]{1,0:T(8,128)(2,1)S(1)} %shard_map.171.own, bf16[128,1024]{1,0:T(8,128)(2,1)S(1)} %collective-permute-done.13.other, f32[1,256]{1,0:T(1,128)S(1)} %get-tuple-element.53.gain, bf16[1024,256]{1,0:T(8,128)(2,1)S(1)} %copy-done.12, ...), custom_call_target="tpu_custom_call" | custom-call | flops 1 | bytes 1 | tf_op jit(solution)/shard_map/pallas_call | solution.py:187
  (65 shorter events, 7.2 us)
Async XLA Ops:
  5.4 1.4 %collective-permute-start = (bf16[16,256]{1,0:T(8,128)(2,1)}, bf16[16,256]{1,0:T(8,128)(2,1)S(1)}, u32[]{:S(2)}, u32[]{:S(2)}) collective-permute-start(bf16[16,256]{1,0:T(8,128)(2,1)} %shard_map.159), channel_id=1, source_target_pairs={{0,1},{1,0},{2,3},{3,2},{4,5},{5,4},{6,7},{7,6},{8,9},{9,8},{10,11... | collective-permute-start | bytes 24584 | tf_op jit(solution)/shard_map/ppermute | solution.py:521
  8.9 16.4 %copy-start.17 = (s32[1,8,8]{2,1,0:T(8,128)S(1)}, s32[1,8,8]{2,1,0:T(8,128)}, u32[]{:S(2)}) copy-start(s32[1,8,8]{2,1,0:T(8,128)} %sends.1) | copy-start | bytes 772
  8.9 29.4 %collective-permute-start.11 = (bf16[2880,128]{1,0:T(8,128)(2,1)}, bf16[2880,128]{1,0:T(8,128)(2,1)}, u32[]{:S(2)}, u32[]{:S(2)}) collective-permute-start(bf16[2880,128]{1,0:T(8,128)(2,1)} %shard_map.160.own_even), channel_id=1, source_target_pairs={{0,2},{2,0},{1,3},{3,1},{4,6},{6,4},{5,7},{7,5},{8,10},{10,8},{9,1... | collective-permute-start | bytes 2211848 | tf_op jit(solution)/shard_map/ppermute | solution.py:561
  10.4 27.9 %collective-permute-start.3 = (bf16[320,768]{1,0:T(8,128)(2,1)}, bf16[320,768]{1,0:T(8,128)(2,1)}, u32[]{:S(2)}, u32[]{:S(2)}) collective-permute-start(bf16[320,768]{1,0:T(8,128)(2,1)} %shard_map.158), channel_id=1, source_target_pairs={{0,2},{2,0},{1,3},{3,1},{4,6},{6,4},{5,7},{7,5},{8,10},{10,8},{9,1... | collective-permute-start | bytes 1474568 | tf_op jit(solution)/shard_map/ppermute | solution.py:508
  14.3 24.0 %all-to-all-start = ((bf16[8,128,128]{2,1,0:T(8,128)(2,1)}), bf16[8,128,128]{2,1,0:T(8,128)(2,1)}, u32[]{:S(2)}, u32[]{:S(2)}) async-start(bf16[8,128,128]{2,1,0:T(8,128)(2,1)} %shard_map.162), calls=%async_computation | async-start | bytes 524288 | tf_op jit(solution)/shard_map/all_to_all | solution.py:590
  19.5 15.3 %collective-permute-start.1 = (bf16[736,256]{1,0:T(8,128)(2,1)}, bf16[736,256]{1,0:T(8,128)(2,1)S(1)}, u32[]{:S(2)}, u32[]{:S(2)}) collective-permute-start(bf16[736,256]{1,0:T(8,128)(2,1)} %copy-done.23), channel_id=1, source_target_pairs={{0,4},{4,8},{8,12},{1,5},{5,9},{9,13},{2,6},{6,10},{10,14},{3,7},{... | collective-permute-start | bytes 1130504 | tf_op jit(solution)/shard_map/ppermute | solution.py:579
  22.8 12.6 %collective-permute-start.2 = (bf16[736,256]{1,0:T(8,128)(2,1)}, bf16[736,256]{1,0:T(8,128)(2,1)S(1)}, u32[]{:S(2)}, u32[]{:S(2)}) collective-permute-start(bf16[736,256]{1,0:T(8,128)(2,1)} %copy-done.22), channel_id=1, source_target_pairs={{4,0},{8,4},{12,8},{5,1},{9,5},{13,9},{6,2},{10,6},{14,10},{7,3},{... | collective-permute-start | bytes 1130504 | tf_op jit(solution)/shard_map/ppermute | solution.py:580
  30.2 13.3 %copy-start.16 = (s32[1,16,3]{1,0,2:T(1,128)S(1)}, s32[1,16,3]{1,0,2:T(1,128)}, u32[]{:S(2)}) copy-start(s32[1,16,3]{1,0,2:T(1,128)} %param.28) | copy-start | bytes 580
  38.3 54.6 %all-to-all-start.1 = ((bf16[64,128,128]{2,1,0:T(8,128)(2,1)}), bf16[64,128,128]{2,1,0:T(8,128)(2,1)}, u32[]{:S(2)}, u32[]{:S(2)}) async-start(bf16[64,128,128]{2,1,0:T(8,128)(2,1)} %copy-done.3), calls=%async_computation.1 | async-start | bytes 4194304 | tf_op jit(solution)/shard_map/all_to_all | solution.py:617
  46.6 5.1 %copy-start.7 = (bf16[736,256]{1,0:T(8,128)(2,1)S(1)}, bf16[736,256]{1,0:T(8,128)(2,1)}, u32[]{:S(2)}) copy-start(bf16[736,256]{1,0:T(8,128)(2,1)} %copy-done.6) | copy-start | bytes 1130500
  46.6 13.6 %collective-permute-start.6 = (bf16[320,768]{1,0:T(8,128)(2,1)}, bf16[320,768]{1,0:T(8,128)(2,1)S(1)}, u32[]{:S(2)}, u32[]{:S(2)}) collective-permute-start(bf16[320,768]{1,0:T(8,128)(2,1)} %collective-permute-done.3.refs_0_), channel_id=1, source_target_pairs={{0,16},{16,0},{1,17},{17,1},{2,18},{18,2},{3,19},{19,3},{4,20},{20... | collective-permute-start | bytes 1474568 | tf_op jit(solution)/shard_map/ppermute | solution.py:618
  50.1 19.4 %collective-permute-start.12 = (bf16[2880,128]{1,0:T(8,128)(2,1)S(1)}, bf16[2880,128]{1,0:T(8,128)(2,1)S(1)}, u32[]{:S(2)}, u32[]{:S(2)}) collective-permute-start(bf16[2880,128]{1,0:T(8,128)(2,1)S(1)} %shard_map.165.own_odd), channel_id=1, source_target_pairs={{0,2},{2,0},{1,3},{3,1},{4,6},{6,4},{5,7},{7,5},{8,10},{10,8},{9,1... | collective-permute-start | bytes 2211848 | tf_op jit(solution)/shard_map/ppermute | solution.py:561
  53.6 10.6 %copy-start.4 = (bf16[1024,512]{1,0:T(8,128)(2,1)S(1)}, bf16[1024,512]{1,0:T(8,128)(2,1)}, u32[]{:S(2)}) copy-start(bf16[1024,512]{1,0:T(8,128)(2,1)} %up.2) | copy-start | bytes 3145732
  53.6 10.6 %copy-start.5 = (bf16[1024,512]{1,0:T(8,128)(2,1)S(1)}, bf16[1024,512]{1,0:T(8,128)(2,1)}, u32[]{:S(2)}) copy-start(bf16[1024,512]{1,0:T(8,128)(2,1)} %down.3) | copy-start | bytes 3145732
  53.6 10.6 %copy-start.8 = (bf16[512,256]{1,0:T(8,128)(2,1)S(1)}, bf16[512,256]{1,0:T(8,128)(2,1)}, u32[]{:S(2)}) copy-start(bf16[512,256]{1,0:T(8,128)(2,1)} %ocean_up.3) | copy-start | bytes 786436
  53.6 10.6 %copy-start.9 = (bf16[512,256]{1,0:T(8,128)(2,1)S(1)}, bf16[512,256]{1,0:T(8,128)(2,1)}, u32[]{:S(2)}) copy-start(bf16[512,256]{1,0:T(8,128)(2,1)} %ocean_down.3) | copy-start | bytes 786436
  53.6 10.6 %copy-start.18 = (f32[512]{0:T(512)S(1)}, f32[512]{0:T(512)}, u32[]{:S(2)}) copy-start(f32[512]{0:T(512)} %gain.1) | copy-start | bytes 6148
  53.7 10.6 %copy-start.20 = (f32[256]{0:T(256)S(1)}, f32[256]{0:T(256)}, u32[]{:S(2)}) copy-start(f32[256]{0:T(256)} %ocean_gain.1) | copy-start | bytes 3076
  56.8 5.4 %collective-permute-start.7 = (bf16[320,768]{1,0:T(8,128)(2,1)}, bf16[320,768]{1,0:T(8,128)(2,1)S(1)}, u32[]{:S(2)}, u32[]{:S(2)}) collective-permute-start(bf16[320,768]{1,0:T(8,128)(2,1)} %collective-permute-done.3.refs_0_), channel_id=1, source_target_pairs={{0,1},{1,0},{2,3},{3,2},{4,5},{5,4},{6,7},{7,6},{8,9},{9,8},{10,11... | collective-permute-start | bytes 1474568 | tf_op jit(solution)/shard_map/ppermute | solution.py:623
  60.2 3.5 %collective-permute-start.8 = (bf16[320,768]{1,0:T(8,128)(2,1)S(1)}, bf16[320,768]{1,0:T(8,128)(2,1)S(1)}, u32[]{:S(2)}, u32[]{:S(2)}) collective-permute-start(bf16[320,768]{1,0:T(8,128)(2,1)S(1)} %collective-permute-done.6.refs_1_), channel_id=1, source_target_pairs={{0,1},{1,0},{2,3},{3,2},{4,5},{5,4},{6,7},{7,6},{8,9},{9,8},{10,11... | collective-permute-start | bytes 1474568 | tf_op jit(solution)/shard_map/ppermute | solution.py:623
  60.2 24.8 %collective-permute-start.9 = (bf16[1440,128]{1,0:T(8,128)(2,1)S(1)}, bf16[1440,128]{1,0:T(8,128)(2,1)S(1)}, u32[]{:S(2)}, u32[]{:S(2)}) collective-permute-start(bf16[1440,128]{1,0:T(8,128)(2,1)S(1)} %get-tuple-element.38.own_even), channel_id=1, source_target_pairs={{0,2},{2,0},{1,3},{3,1},{4,6},{6,4},{5,7},{7,5},{8,10},{10,8},{9,1... | collective-permute-start | bytes 1105928 | tf_op jit(solution)/shard_map/ppermute | solution.py:561
  61.7 23.7 %collective-permute-start.10 = (bf16[1440,128]{1,0:T(8,128)(2,1)S(1)}, bf16[1440,128]{1,0:T(8,128)(2,1)S(1)}, u32[]{:S(2)}, u32[]{:S(2)}) collective-permute-start(bf16[1440,128]{1,0:T(8,128)(2,1)S(1)} %get-tuple-element.41.own_odd), channel_id=1, source_target_pairs={{0,2},{2,0},{1,3},{3,1},{4,6},{6,4},{5,7},{7,5},{8,10},{10,8},{9,1... | collective-permute-start | bytes 1105928 | tf_op jit(solution)/shard_map/ppermute | solution.py:561
  62.2 39.3 %collective-permute-start.4 = (bf16[1440,128]{1,0:T(8,128)(2,1)}, bf16[1440,128]{1,0:T(8,128)(2,1)}, u32[]{:S(2)}, u32[]{:S(2)}) collective-permute-start(bf16[1440,128]{1,0:T(8,128)(2,1)} %get-tuple-element.37.own_even), channel_id=1, source_target_pairs={{0,2},{2,0},{1,3},{3,1},{4,6},{6,4},{5,7},{7,5},{8,10},{10,8},{9,1... | collective-permute-start | bytes 1105928 | tf_op jit(solution)/shard_map/ppermute | solution.py:561
  63.7 37.8 %collective-permute-start.5 = (bf16[1440,128]{1,0:T(8,128)(2,1)}, bf16[1440,128]{1,0:T(8,128)(2,1)}, u32[]{:S(2)}, u32[]{:S(2)}) collective-permute-start(bf16[1440,128]{1,0:T(8,128)(2,1)} %get-tuple-element.40.own_odd), channel_id=1, source_target_pairs={{0,2},{2,0},{1,3},{3,1},{4,6},{6,4},{5,7},{7,5},{8,10},{10,8},{9,1... | collective-permute-start | bytes 1105928 | tf_op jit(solution)/shard_map/ppermute | solution.py:561
  67.7 17.3 %copy-start.11 = (bf16[1024,256]{1,0:T(8,128)(2,1)}, bf16[1024,256]{1,0:T(8,128)(2,1)S(1)}, u32[]{:S(2)}) copy-start(bf16[1024,256]{1,0:T(8,128)(2,1)S(1)} %get-tuple-element.54.across) | copy-start | bytes 1572868
  67.7 17.3 %copy-start.13 = (bf16[1024,128]{1,0:T(8,128)(2,1)}, bf16[1024,128]{1,0:T(8,128)(2,1)S(1)}, u32[]{:S(2)}) copy-start(bf16[1024,128]{1,0:T(8,128)(2,1)S(1)} %get-tuple-element.55.back) | copy-start | bytes 786436
  85.0 7.9 %copy-start.10 = (bf16[128,1024]{1,0:T(8,128)(2,1)S(1)}, bf16[128,1024]{1,0:T(8,128)(2,1)}, u32[]{:S(2)}) copy-start(bf16[128,1024]{1,0:T(8,128)(2,1)} %ocean.2) | copy-start | bytes 786436
  85.0 7.9 %copy-start.19 = (s32[1,128,3]{1,0,2:T(1,128)S(1)}, s32[1,128,3]{1,0,2:T(1,128)}, u32[]{:S(2)}) copy-start(s32[1,128,3]{1,0,2:T(1,128)} %param.26) | copy-start | bytes 4612
  99.9 10.3 %copy-start.12 = (bf16[1024,256]{1,0:T(8,128)(2,1)S(1)}, bf16[1024,256]{1,0:T(8,128)(2,1)}, u32[]{:S(2)}) copy-start(bf16[1024,256]{1,0:T(8,128)(2,1)} %copy-done.11) | copy-start | bytes 1572868
  99.9 10.3 %copy-start.14 = (bf16[1024,128]{1,0:T(8,128)(2,1)S(1)}, bf16[1024,128]{1,0:T(8,128)(2,1)}, u32[]{:S(2)}) copy-start(bf16[1024,128]{1,0:T(8,128)(2,1)} %copy-done.13) | copy-start | bytes 786436
  99.9 10.3 %copy-start.21 = (s32[8]{0:T(128)S(1)}, s32[8]{0:T(128)}, u32[]{:S(2)}) copy-start(s32[8]{0:T(128)} %mask.1) | copy-start | bytes 100
  99.9 10.3 %collective-permute-start.13 = (bf16[128,1024]{1,0:T(8,128)(2,1)S(1)}, bf16[128,1024]{1,0:T(8,128)(2,1)S(1)}, u32[]{:S(2)}, u32[]{:S(2)}) collective-permute-start(bf16[128,1024]{1,0:T(8,128)(2,1)S(1)} %shard_map.171.own), channel_id=1, source_target_pairs={{0,2},{2,0},{1,3},{3,1},{4,6},{6,4},{5,7},{7,5},{8,10},{10,8},{9,1... | collective-permute-start | bytes 786440 | tf_op jit(solution)/shard_map/ppermute | solution.py:659
  (8 other events, 12.9 us)

commit v4 on v3

--- a/solution.py
+++ b/solution.py
@@ -182,7 +182,7 @@
 
 
 def local_call(
-    body, out_shape, operands, in_specs, out_specs, limit, grid=1, scratch=(), flops=0, moved=0, exps=0, aliases=None
+    body, out_shape, operands, in_specs, out_specs, limit, grid=1, scratch=(), aliases=None
 ):
     return pl.pallas_call(
         body,
@@ -364,7 +364,8 @@
     count = ocean_up.shape[0]
     ocean_across[0:count, 0:narrow] = ocean_up[:, mine]
     ocean_across[0:count, narrow : 2 * narrow] = ocean_up[:, theirs]
-    ocean_back[0:count, :] = ocean_down[:, mine]
+    ocean_back[:, 0:count] = ocean_down[:, mine].T
+    parts = []
     for part in range(4):
         for side in range(2):
             start = count + part * shallow + side * (shallow // 2)
@@ -375,7 +376,8 @@
             right = pl.multiple_of(base + narrow - own, 128)
             ocean_across[at, 0:narrow] = pieces[part][low, pl.ds(left, narrow)]
             ocean_across[at, narrow : 2 * narrow] = pieces[part][low, pl.ds(right, narrow)]
-            ocean_back[at, :] = pieces[part][low, base + 2 * narrow : base + 3 * narrow]
+            parts.append(pieces[part][low, base + 2 * narrow : base + 3 * narrow])
+    ocean_back[:, count:] = jnp.concatenate(parts, axis=0).T
 
 
 def atmos_layer_body(own_even, own_odd, other_even, other_odd, gain, across, back, *refs):
@@ -387,7 +389,7 @@
     inverse = lax.rsqrt(squares * (1.0 / (2 * width)) + 1e-06)
     normed = (wide * inverse * gain[...]).astype(jnp.bfloat16)
     total = jnp.dot(values[:, 0:width], weaver(width), preferred_element_type=jnp.float32)
-    step = 256
+    step = 512
     for base in range(0, across.shape[1], step):
         at = slice(base, base + step)
         v = jnp.dot(normed, across[:, at], preferred_element_type=jnp.float32)
@@ -420,18 +422,23 @@
 def ocean_layer_body(mask, own, other, gain, across, back, out):
     width = own.shape[0]
     square = (width, width)
-    tall = [jnp.broadcast_to(gain[:, k * width : (k + 1) * width], square).T for k in range(2)]
-    for tile in range(mask.shape[0]):
-        lanes = slice(tile * 128, tile * 128 + 128)
+    tall = [jnp.broadcast_to(gain[:, k * width : (k + 1) * width], square).T[:, 0:1] for k in range(2)]
+    group = math.gcd(mask.shape[0], 4)
+    for base in range(0, mask.shape[0], group):
+        lanes = slice(base * 128, (base + group) * 128)
         a = own[:, lanes].astype(jnp.float32)
         b = other[:, lanes].astype(jnp.float32)
         squares = jnp.sum(a * a + b * b, axis=0, keepdims=True)
         inverse = lax.rsqrt(squares * (1.0 / (2 * width)) + 1e-06)
-        normed = jnp.concatenate([a * inverse * tall[0][:, 0:128], b * inverse * tall[1][:, 0:128]], axis=0)
-        v = jnp.dot(across[...], normed.astype(jnp.bfloat16), preferred_element_type=jnp.float32)
+        normed = jnp.concatenate([a * inverse * tall[0], b * inverse * tall[1]], axis=0).astype(jnp.bfloat16)
+        v = jnp.dot(across[...], normed, preferred_element_type=jnp.float32)
         hidden = gelu(v).astype(jnp.bfloat16)
-        delta = lax.dot_general(back[...], hidden, TN, preferred_element_type=jnp.float32)
-        out[:, lanes] = (a + mask[tile].astype(jnp.float32) * delta).astype(jnp.bfloat16)
+        delta = jnp.dot(back[...], hidden, preferred_element_type=jnp.float32)
+        for tile in range(group):
+            inside = slice(tile * 128, tile * 128 + 128)
+            keep = mask[base + tile].astype(jnp.float32)
+            at = slice((base + tile) * 128, (base + tile + 1) * 128)
+            out[:, at] = (a[:, inside] + keep * delta[:, inside]).astype(jnp.bfloat16)
 
 
 def pack_body(place, up, down, ocean_up, ocean_down, out):
@@ -504,19 +511,16 @@
     sea_rows = sea_pattern.transpose(2, 0, 1)
     flux_rows = flux_pattern.transpose(2, 0, 1)
 
-    packed = pack_weights(atmos_up, atmos_down, ocean_up, ocean_down)
-    one = lax.ppermute(packed, "chan", SWAP)
     sides = local_call(
         sides_body,
         jax.ShapeDtypeStruct((2 * lat_rows, channels), bf16),
-        (after(field, packed), field),
+        (field, field),
         [
             pl.BlockSpec((lat_rows, 16, channels), lambda _: (0, lon_cells // 16 - 1, 0)),
             pl.BlockSpec((lat_rows, 16, channels), lambda _: (0, 0, 0)),
         ],
         vmem(),
         60,
-        moved=2**18,
     )
     sides = lax.ppermute(sides, "pair", SWAP)
     def smooth_rows(odd, runs, field):
@@ -549,8 +553,6 @@
             [vmem() for _ in runs],
             24,
             scratch=scratch,
-            flops=18 * sum(count for _, count in runs) * lon_cells * channels // 2,
-            moved=4 * 2**20,
         )
 
     edge = lat_rows // 4
@@ -562,11 +564,20 @@
 
     evens = smooth_rows(0, middle, field)
     others = cross(evens)
+    sea_out = local_call(
+        sea_pick_body,
+        jax.ShapeDtypeStruct((sea_sends.size, 128, flux_depth), bf16),
+        (sea_sends.reshape(1, 1, -1), after(ocean_state, *evens)),
+        [smem(), vmem()],
+        vmem(),
+        60,
+    )
+    sea_in = lax.all_to_all(sea_out, peers, split_axis=0, concat_axis=0, tiled=True)
     row = jax.ShapeDtypeStruct((lon_cells + 16, channels), bf16)
     messages = local_call(
         edges_body,
         [row, row],
-        (after(field, *evens), field, sides),
+        (after(field, sea_out), field, sides),
         [
             pl.BlockSpec((1, lon_cells, channels), lambda _: (lat_rows - 1, 0, 0)),
             pl.BlockSpec((1, lon_cells, channels), lambda _: (0, 0, 0)),
@@ -574,30 +585,19 @@
         ],
         [vmem()] * 2,
         40,
-        moved=2**20,
     )
     low = lax.ppermute(messages[0], "lat", [(i, i + 1) for i in range(lat_bands - 1)])
     high = lax.ppermute(messages[1], "lat", [(i + 1, i) for i in range(lat_bands - 1)])
-    sea_out = local_call(
-        sea_pick_body,
-        jax.ShapeDtypeStruct((sea_sends.size, 128, flux_depth), bf16),
-        (sea_sends.reshape(1, 1, -1), after(ocean_state, *messages)),
-        [smem(), vmem()],
-        vmem(),
-        60,
-        moved=2**20,
-    )
-    sea_in = lax.all_to_all(sea_out, peers, split_axis=0, concat_axis=0, tiled=True)
+    packed = pack_weights(after(atmos_up, *messages), atmos_down, ocean_up, ocean_down)
+    one = lax.ppermute(packed, "chan", SWAP)
     flux_out = local_call(
         flux_pick_body,
         jax.ShapeDtypeStruct((flux_sends.size, flux_depth, 128), bf16),
-        (flux_sends, after(field, sea_out).reshape(lat_rows * lon_cells, channels)),
+        (flux_sends, after(field, packed).reshape(lat_rows * lon_cells, channels)),
         [smem(), vmem()],
         vmem(),
         24,
         scratch=[pltpu.VMEM((lat_rows * lon_cells // 128, flux_depth, 128), bf16)],
-        flops=2 * lat_rows * lon_cells * channels * flux_depth,
-        moved=6 * 2**20,
     )
 
     entries = sea_pattern.shape[1]
@@ -608,8 +608,6 @@
         [smem(), vmem(), vmem()],
         vmem(),
         16,
-        flops=2 * entries * 128 * 128 * flux_depth,
-        moved=4 * 2**20,
     )
     odds = smooth_rows(1, middle, field)
     others_odd = cross(odds)
@@ -630,7 +628,7 @@
             jax.ShapeDtypeStruct((2 * channels, hidden), bf16),
             jax.ShapeDtypeStruct((hidden, channels), bf16),
             jax.ShapeDtypeStruct((ocean_hidden, 2 * flux_depth), bf16),
-            jax.ShapeDtypeStruct((ocean_hidden, flux_depth), bf16),
+            jax.ShapeDtypeStruct((flux_depth, ocean_hidden), bf16),
             jax.ShapeDtypeStruct((1, 2 * channels), f32),
             jax.ShapeDtypeStruct((1, 2 * flux_depth), f32),
         ],
@@ -638,8 +636,6 @@
         [smem()] + [vmem()] * 10,
         [vmem()] * 6,
         32,
-        flops=8 * hidden * channels * channels,
-        moved=8 * 2**20,
     )
     result = None
     for step, ((first, count), *values) in enumerate(plan):
@@ -651,10 +647,8 @@
                 (flux_rows, flux_in, after(remap_blocks, result), ocean_state),
                 [smem(), vmem(), vmem(), vmem()],
                 vmem(),
-                16,
+                60,
                 scratch=[pltpu.VMEM((ocean_count, flux_depth, 128), f32)],
-                flops=2 * entries * 128 * 128 * flux_depth,
-                moved=5 * 2**20,
             )
             ocean_other = lax.ppermute(ocean_input, "chan", SWAP)
             result = after(result, ocean_input)
@@ -673,9 +667,6 @@
             pl.BlockSpec((1, lon_cells, channels), lambda step, first=first: (first + step, 0, 0)),
             24,
             grid=count,
-            flops=2 * count * lon_cells * 3 * channels * hidden,
-            moved=(4 + count) * 2**20,
-            exps=count * lon_cells * hidden,
             aliases=aliases,
         )
     ocean_next = local_call(
@@ -685,9 +676,6 @@
         [smem()] + [vmem()] * 5,
         vmem(),
         16,
-        flops=2 * ocean_cells * 3 * flux_depth * ocean_hidden,
-        moved=4 * 2**20,
-        exps=ocean_cells * ocean_hidden,
     )
     return result.transpose(2, 0, 1), ocean_next
 

time: 117 us -> 111 us (0.949)
  Pallas kernels: 65.3 us -> 61.3 us
  local copies, waits for them, and re-layouts: 6.86 us -> 4.51 us
    pallas_call x15, Pallas kernels: 62.8 us -> 58.7 us  [local_call(): pl.pallas_call(body, grid=(grid,), out_shape=out_shape, in_specs=in_specs...]
    unnamed x48 -> x44, local copies, waits for them, and re-layouts: 6.86 us -> 4.51 us
    ppermute x6, waiting for transfers between devices: 2.24 us -> 4.54 us  [cross(): return [lax.ppermute(value, 'chan', SWAP) for value in values]]
    ppermute x1, waiting for transfers between devices: 2.05 us -> 0.01 us  [quick_shards(): one = lax.ppermute(packed, 'chan', SWAP)]
  transfers between devices with their start and end apart: 16 -> 16, of which waited for: 7 -> 7; matrix products, arithmetic and copies ran while one was open for 0% -> 1% of each run, Pallas kernels for 47% -> 50%
where the time goes in v4:
time: 111 us; the launch traced here: 109 us
  Pallas kernels  61.3 us (55%)
  starting transfers between devices  27.1 us (24%)
  waiting for transfers between devices  14.6 us (13%)
  local copies, waits for them, and re-layouts  4.51 us (4%)
    pallas_call x15, Pallas kernels, local_call(): pl.pallas_call(body, grid=(grid,), out_shape=out_shape, in_specs=in_specs...  58.7 us
    ppermute x6, starting transfers between devices, cross(): return [lax.ppermute(value, 'chan', SWAP) for value in values]  7.1 us
    all_to_all x1, starting transfers between devices, quick_shards(): lax.all_to_all(after(flux_out, low, high, *others, one), peers, split_axi...  5.24 us
    all_to_all x1, starting transfers between devices, quick_shards(): lax.all_to_all(sea_out, peers, split_axis=0, concat_axis=0, tiled=True)  5.21 us
    ppermute x6, waiting for transfers between devices, cross(): return [lax.ppermute(value, 'chan', SWAP) for value in values]  4.54 us
    unnamed x44, local copies, waits for them, and re-layouts  4.51 us
    ppermute x1, waiting for transfers between devices, quick_shards(): lax.ppermute(messages[0], 'lat', [(i, i + 1) for i in range(lat_bands - 1)])  4.5 us
    ppermute x1, waiting for transfers between devices, quick_shards(): two = lax.ppermute(after(one, sea), 'groups', SWAP)  3.41 us
  transfers between devices with their start and end apart: 16, of which 7 were waited for; matrix products, arithmetic and copies ran while one was open for 1% of the time, Pallas kernels for 50%

profile of v4, /device:TPU:16, one launch (start us, length us, event | category | flops | bytes accessed | tf_op | source)
XLA Modules:
  0.0 108.9 jit_solution(4483540252823467385)
XLA Ops:
  0.6 1.6 %shard_map.158 = bf16[16,256]{1,0:T(8,128)(2,1)} custom-call(bf16[8,720,256]{2,1,0:T(8,128)(2,1)} %bitcast.12, bf16[8,720,256]{2,1,0:T(8,128)(2,1)} %bitcast.13), custom_call_target="tpu_custom_call" | custom-call | flops 1 | bytes 1 | tf_op jit(solution)/shard_map/pallas_call | solution.py:187
  2.3 1.4 %collective-permute-done.refs_6_.sides.refs_8_ = bf16[16,256]{1,0:T(8,128)(2,1)S(1)} collective-permute-done((bf16[16,256]{1,0:T(8,128)(2,1)}, bf16[16,256]{1,0:T(8,128)(2,1)S(1)}, u32[]{:S(2)}, u32[]{:S(2)}) %collective-permute-start) | collective-permute-done | bytes 8224 | tf_op jit(solution)/shard_map/ppermute | solution.py:525
  3.7 2.1 %shard_map.159.own_even = bf16[2880,128]{1,0:T(8,128)(2,1)} custom-call(bf16[8,720,256]{2,1,0:T(8,128)(2,1)S(1)} %bitcast.14, bf16[8,720,256]{2,1,0:T(8,128)(2,1)S(1)} %bitcast.15, bf16[8,720,256]{2,1,0:T(8,128)(2,1)S(1)} %bitcast.16, bf16[8,720,256]{2,1,0:T(8,128)(2,1)S(1)} %bitcast.17, bf16[8,720,256]{2,1,0:T(8,128)(2,1)S(1)} %bitcast.18, ...), custom_call_target="tpu_custom_call" | custom-call | flops 1 | bytes 1 | tf_op jit(solution)/shard_map/pallas_call | solution.py:187
  5.8 1.5 %collective-permute-start.11 = (bf16[2880,128]{1,0:T(8,128)(2,1)}, bf16[2880,128]{1,0:T(8,128)(2,1)}, u32[]{:S(2)}, u32[]{:S(2)}) collective-permute-start(bf16[2880,128]{1,0:T(8,128)(2,1)} %shard_map.159.own_even), channel_id=1, source_target_pairs={{0,2},{2,0},{1,3},{3,1},{4,6},{6,4},{5,7},{7,5},{8,10},{10,8},{9,1... | collective-permute-start | bytes 2211848 | tf_op jit(solution)/shard_map/ppermute | solution.py:563
  7.8 1.8 %shard_map.160 = bf16[8,128,128]{2,1,0:T(8,128)(2,1)} custom-call(s32[1,1,8]{2,1,0:T(1,128)} %bitcast.54, bf16[128,1024]{1,0:T(8,128)(2,1)} %ocean.2), custom_call_target="tpu_custom_call" | custom-call | flops 1 | bytes 1 | tf_op jit(solution)/shard_map/pallas_call | solution.py:187
  10.4 2.6 %shard_map.162 = bf16[320,768]{1,0:T(8,128)(2,1)} custom-call(s32[2]{0:T(128)} %pad_add_fusion.place, bf16[1024,512]{1,0:T(8,128)(2,1)} %up.1, bf16[1024,512]{1,0:T(8,128)(2,1)} %down.3, bf16[512,256]{1,0:T(8,128)(2,1)} %ocean_up.3, bf16[512,256]{1,0:T(8,128)(2,1)} %ocean_down.3), custom_call_target="tpu_custom_call" | custom-call | tf_op jit(solution)/shard_map/pallas_call | solution.py:461
  13.6 5.2 %all-to-all-start = ((bf16[8,128,128]{2,1,0:T(8,128)(2,1)}), bf16[8,128,128]{2,1,0:T(8,128)(2,1)}, u32[]{:S(2)}, u32[]{:S(2)}) async-start(bf16[8,128,128]{2,1,0:T(8,128)(2,1)} %shard_map.160), calls=%async_computation | async-start | bytes 524288 | tf_op jit(solution)/shard_map/all_to_all | solution.py:575
  18.8 3.4 %collective-permute-start.1 = (bf16[736,256]{1,0:T(8,128)(2,1)}, bf16[736,256]{1,0:T(8,128)(2,1)S(1)}, u32[]{:S(2)}, u32[]{:S(2)}) collective-permute-start(bf16[736,256]{1,0:T(8,128)(2,1)} %copy-done.21), channel_id=1, source_target_pairs={{0,4},{4,8},{8,12},{1,5},{5,9},{9,13},{2,6},{6,10},{10,14},{3,7},{... | collective-permute-start | bytes 1130504 | tf_op jit(solution)/shard_map/ppermute | solution.py:589
  22.2 2.5 %collective-permute-start.2 = (bf16[736,256]{1,0:T(8,128)(2,1)}, bf16[736,256]{1,0:T(8,128)(2,1)S(1)}, u32[]{:S(2)}, u32[]{:S(2)}) collective-permute-start(bf16[736,256]{1,0:T(8,128)(2,1)} %copy-done.20), channel_id=1, source_target_pairs={{4,0},{8,4},{12,8},{5,1},{9,5},{13,9},{6,2},{10,6},{14,10},{7,3},{... | collective-permute-start | bytes 1130504 | tf_op jit(solution)/shard_map/ppermute | solution.py:590
  24.6 3.5 %shard_map.163 = bf16[64,128,128]{2,1,0:T(8,128)(2,1)S(1)} custom-call(s32[1,8,8]{2,1,0:T(8,128)S(1)} %copy-done.16, bf16[5760,256]{1,0:T(8,128)(2,1)S(1)} %bitcast.22), custom_call_target="tpu_custom_call" | custom-call | flops 1 | bytes 1 | tf_op jit(solution)/shard_map/pallas_call | solution.py:187
  28.2 1.4 %copy-done.2 = bf16[64,128,128]{2,1,0:T(8,128)(2,1)} copy-done((bf16[64,128,128]{2,1,0:T(8,128)(2,1)}, bf16[64,128,128]{2,1,0:T(8,128)(2,1)S(1)}, u32[]{:S(2)}) %copy-start.2) | copy-done | bytes 2097176
  29.5 4.5 %collective-permute-done.1 = bf16[736,256]{1,0:T(8,128)(2,1)S(1)} collective-permute-done((bf16[736,256]{1,0:T(8,128)(2,1)}, bf16[736,256]{1,0:T(8,128)(2,1)S(1)}, u32[]{:S(2)}, u32[]{:S(2)}) %collective-permute-start.1) | collective-permute-done | bytes 376864 | tf_op jit(solution)/shard_map/ppermute | solution.py:589
  35.6 5.2 %all-to-all-start.1 = ((bf16[64,128,128]{2,1,0:T(8,128)(2,1)}), bf16[64,128,128]{2,1,0:T(8,128)(2,1)}, u32[]{:S(2)}, u32[]{:S(2)}) async-start(bf16[64,128,128]{2,1,0:T(8,128)(2,1)} %copy-done.2), calls=%async_computation.1 | async-start | bytes 4194304 | tf_op jit(solution)/shard_map/all_to_all | solution.py:615
  40.8 1.6 %copy-done.1 = bf16[64,128,128]{2,1,0:T(8,128)(2,1)S(1)} copy-done((bf16[64,128,128]{2,1,0:T(8,128)(2,1)S(1)}, bf16[64,128,128]{2,1,0:T(8,128)(2,1)}, u32[]{:S(2)}) %copy-start.1) | copy-done | bytes 2097176
  42.4 1.5 %shard_map.164.refs_9_.refs_11_ = f32[16,128,128]{2,1,0:T(8,128)S(1)} custom-call(s32[3,1,16]{2,1,0:T(1,128)S(1)} %bitcast.49, bf16[8,128,128]{2,1,0:T(8,128)(2,1)} %all-to-all-done.slots, bf16[64,128,128]{2,1,0:T(8,128)(2,1)S(1)} %copy-done.1), custom_call_target="tpu_custom_call" | custom-call | flops 1 | bytes 1 | tf_op jit(solution)/shard_map/pallas_call | solution.py:187
  43.9 1.6 %collective-permute-start.6 = (bf16[320,768]{1,0:T(8,128)(2,1)}, bf16[320,768]{1,0:T(8,128)(2,1)S(1)}, u32[]{:S(2)}, u32[]{:S(2)}) collective-permute-start(bf16[320,768]{1,0:T(8,128)(2,1)} %collective-permute-done.3.refs_0_), channel_id=1, source_target_pairs={{0,16},{16,0},{1,17},{17,1},{2,18},{18,2},{3,19},{19,3},{4,20},{20... | collective-permute-start | bytes 1474568 | tf_op jit(solution)/shard_map/ppermute | solution.py:616
  45.5 1.9 %shard_map.165.own_odd = bf16[2880,128]{1,0:T(8,128)(2,1)S(1)} custom-call(bf16[8,720,256]{2,1,0:T(8,128)(2,1)S(1)} %bitcast.25, bf16[8,720,256]{2,1,0:T(8,128)(2,1)S(1)} %bitcast.24, bf16[8,720,256]{2,1,0:T(8,128)(2,1)S(1)} %bitcast.23, bf16[8,720,256]{2,1,0:T(8,128)(2,1)S(1)} %bitcast.26, bf16[8,720,256]{2,1,0:T(8,128)(2,1)S(1)} %bitcast.27, ...), custom_call_target="tpu_custom_call" | custom-call | flops 1 | bytes 1 | tf_op jit(solution)/shard_map/pallas_call | solution.py:187
  47.4 1.6 %collective-permute-start.12 = (bf16[2880,128]{1,0:T(8,128)(2,1)S(1)}, bf16[2880,128]{1,0:T(8,128)(2,1)S(1)}, u32[]{:S(2)}, u32[]{:S(2)}) collective-permute-start(bf16[2880,128]{1,0:T(8,128)(2,1)S(1)} %shard_map.165.own_odd), channel_id=1, source_target_pairs={{0,2},{2,0},{1,3},{3,1},{4,6},{6,4},{5,7},{7,5},{8,10},{10,8},{9,1... | collective-permute-start | bytes 2211848 | tf_op jit(solution)/shard_map/ppermute | solution.py:563
  49.0 1.9 %shard_map.166 = (bf16[1440,128]{1,0:T(8,128)(2,1)S(1)}, bf16[1440,128]{1,0:T(8,128)(2,1)}) custom-call(bf16[1,736,256]{2,1,0:T(8,128)(2,1)S(1)} %bitcast.41, bf16[8,720,256]{2,1,0:T(8,128)(2,1)S(1)} %bitcast.29, bf16[8,720,256]{2,1,0:T(8,128)(2,1)S(1)} %bitcast.30, bf16[8,720,256]{2,1,0:T(8,128)(2,1)S(1)} %bitcast.31, bf16[8,720,256]{2,1,0:T(8,128)(2,1)S(1)} %bitcast.32, ...), custom_call_target="tpu_custom_call" | custom-call | flops 1 | bytes 1 | tf_op jit(solution)/shard_map/pallas_call | solution.py:187
  50.9 3.1 %shard_map.167 = (bf16[1440,128]{1,0:T(8,128)(2,1)S(1)}, bf16[1440,128]{1,0:T(8,128)(2,1)}) custom-call(bf16[1,736,256]{2,1,0:T(8,128)(2,1)S(1)} %bitcast.42, bf16[8,720,256]{2,1,0:T(8,128)(2,1)S(1)} %bitcast.35, bf16[8,720,256]{2,1,0:T(8,128)(2,1)S(1)} %bitcast.36, bf16[8,720,256]{2,1,0:T(8,128)(2,1)S(1)} %bitcast.37, bf16[8,720,256]{2,1,0:T(8,128)(2,1)S(1)} %bitcast.38, ...), custom_call_target="tpu_custom_call" | custom-call | flops 1 | bytes 1 | tf_op jit(solution)/shard_map/pallas_call | solution.py:187
  54.0 3.4 %collective-permute-done.6.refs_1_ = bf16[320,768]{1,0:T(8,128)(2,1)S(1)} collective-permute-done((bf16[320,768]{1,0:T(8,128)(2,1)}, bf16[320,768]{1,0:T(8,128)(2,1)S(1)}, u32[]{:S(2)}, u32[]{:S(2)}) %collective-permute-start.6) | collective-permute-done | bytes 491552 | tf_op jit(solution)/shard_map/ppermute | solution.py:616
  57.4 1.5 %collective-permute-start.9 = (bf16[1440,128]{1,0:T(8,128)(2,1)S(1)}, bf16[1440,128]{1,0:T(8,128)(2,1)S(1)}, u32[]{:S(2)}, u32[]{:S(2)}) collective-permute-start(bf16[1440,128]{1,0:T(8,128)(2,1)S(1)} %get-tuple-element.38.own_even), channel_id=1, source_target_pairs={{0,2},{2,0},{1,3},{3,1},{4,6},{6,4},{5,7},{7,5},{8,10},{10,8},{9,1... | collective-permute-start | bytes 1105928 | tf_op jit(solution)/shard_map/ppermute | solution.py:563
  59.5 1.5 %collective-permute-start.4 = (bf16[1440,128]{1,0:T(8,128)(2,1)}, bf16[1440,128]{1,0:T(8,128)(2,1)S(1)}, u32[]{:S(2)}, u32[]{:S(2)}) collective-permute-start(bf16[1440,128]{1,0:T(8,128)(2,1)} %get-tuple-element.37.own_even), channel_id=1, source_target_pairs={{0,2},{2,0},{1,3},{3,1},{4,6},{6,4},{5,7},{7,5},{8,10},{10,8},{9,1... | collective-permute-start | bytes 1105928 | tf_op jit(solution)/shard_map/ppermute | solution.py:563
  61.5 3.3 %shard_map.168 = (bf16[512,2048]{1,0:T(8,128)(2,1)S(1)}, bf16[2048,256]{1,0:T(8,128)(2,1)S(1)}, bf16[1024,256]{1,0:T(8,128)(2,1)S(1)}, bf16[128,1024]{1,0:T(8,12...) custom-call(s32[1]{0:T(128)} %bitcast.9.chan, bf16[1024,512]{1,0:T(8,128)(2,1)S(1)} %copy-done.3, ...), custom_call_target="tpu_custom_call" | custom-call | flops 1 | bytes 1 | tf_op jit(solution)/shard_map/pallas_call | solution.py:187
  64.9 2.0 %collective-permute-done.12.other_odd = bf16[2880,128]{1,0:T(8,128)(2,1)S(1)} collective-permute-done((bf16[2880,128]{1,0:T(8,128)(2,1)S(1)}, bf16[2880,128]{1,0:T(8,128)(2,1)S(1)}, u32[]{:S(2)}, u32[]{:S(2)}) %collective-permute-start.12) | collective-permute-done | bytes 737312 | tf_op jit(solution)/shard_map/ppermute | solution.py:563
  66.9 13.5 %shard_map.169.refs_0_ = bf16[8,720,256]{2,1,0:T(8,128)(2,1)} custom-call(bf16[2880,128]{1,0:T(8,128)(2,1)} %shard_map.159.own_even, bf16[2880,128]{1,0:T(8,128)(2,1)S(1)} %shard_map.165.own_odd, bf16[2880,128]{1,0:T(8,128)(2,1)} %collective-permute-done.11.other_even, bf16[2880,128]{1,0:T(8,128)(2,1)S(1)} %collective-permute-done.12.other_odd, ...), custom_call_target="tpu_custom_call" | custom-call | flops 1 | bytes 1 | tf_op jit(solution)/shard_map/pallas_call | solution.py:187
  80.4 2.2 %collective-permute-done.10.other_odd = bf16[1440,128]{1,0:T(8,128)(2,1)S(1)} collective-permute-done((bf16[1440,128]{1,0:T(8,128)(2,1)S(1)}, bf16[1440,128]{1,0:T(8,128)(2,1)S(1)}, u32[]{:S(2)}, u32[]{:S(2)}) %collective-permute-start.10) | collective-permute-done | bytes 368672 | tf_op jit(solution)/shard_map/ppermute | solution.py:563
  82.7 6.6 %shard_map.170.refs_0_ = bf16[8,720,256]{2,1,0:T(8,128)(2,1)} custom-call(bf16[1440,128]{1,0:T(8,128)(2,1)S(1)} %get-tuple-element.38.own_even, bf16[1440,128]{1,0:T(8,128)(2,1)S(1)} %get-tuple-element.41.own_odd, bf16[1440,128]{1,0:T(8,128)(2,1)S(1)} %collective-permute-done.9.other_even, ...), custom_call_target="tpu_custom_call", output_to_operand_aliasing={{}: (7, {})} | custom-call | flops 1 | bytes 1 | tf_op jit(solution)/shard_map/pallas_call | solution.py:187
  89.3 6.7 %shard_map.171.own = bf16[128,1024]{1,0:T(8,128)(2,1)} custom-call(s32[3,1,128]{2,1,0:T(1,128)} %bitcast.53, bf16[64,128,128]{2,1,0:T(8,128)(2,1)} %all-to-all-done.1.slots, bf16[64,128,128]{2,1,0:T(8,128)(2,1)} %blocks.1, bf16[128,1024]{1,0:T(8,128)(2,1)} %ocean.2), custom_call_target="tpu_custom_call" | custom-call | flops 1 | bytes 1 | tf_op jit(solution)/shard_map/pallas_call | solution.py:187
  96.0 1.6 %collective-permute-start.13 = (bf16[128,1024]{1,0:T(8,128)(2,1)}, bf16[128,1024]{1,0:T(8,128)(2,1)S(1)}, u32[]{:S(2)}, u32[]{:S(2)}) collective-permute-start(bf16[128,1024]{1,0:T(8,128)(2,1)} %shard_map.171.own), channel_id=1, source_target_pairs={{0,2},{2,0},{1,3},{3,1},{4,6},{6,4},{5,7},{7,5},{8,10},{10,8},{9,1... | collective-permute-start | bytes 786440 | tf_op jit(solution)/shard_map/ppermute | solution.py:653
  97.9 7.7 %shard_map.172 = bf16[8,720,256]{2,1,0:T(8,128)(2,1)} custom-call(bf16[1440,128]{1,0:T(8,128)(2,1)} %get-tuple-element.37.own_even, bf16[1440,128]{1,0:T(8,128)(2,1)} %get-tuple-element.40.own_odd, bf16[1440,128]{1,0:T(8,128)(2,1)S(1)} %collective-permute-done.4.other_even, ...), custom_call_target="tpu_custom_call", output_to_operand_aliasing={{}: (7, {})} | custom-call | flops 1 | bytes 1 | tf_op jit(solution)/shard_map/pallas_call | solution.py:187
  105.6 3.3 %shard_map.173 = bf16[128,1024]{1,0:T(8,128)(2,1)} custom-call(s32[8]{0:T(128)S(1)} %copy-done.19, bf16[128,1024]{1,0:T(8,128)(2,1)S(1)} %copy-done.9, bf16[128,1024]{1,0:T(8,128)(2,1)S(1)} %collective-permute-done.13.other, f32[1,256]{1,0:T(1,128)S(1)} %get-tuple-element.53.gain, bf16[1024,256]{1,0:T(8,128)(2,1)S(1)} %copy-done.11, ...), custom_call_target="tpu_custom_call" | custom-call | flops 1 | bytes 1 | tf_op jit(solution)/shard_map/pallas_call | solution.py:187
  (61 shorter events, 4.9 us)
Async XLA Ops:
  2.3 1.4 %collective-permute-start = (bf16[16,256]{1,0:T(8,128)(2,1)}, bf16[16,256]{1,0:T(8,128)(2,1)S(1)}, u32[]{:S(2)}, u32[]{:S(2)}) collective-permute-start(bf16[16,256]{1,0:T(8,128)(2,1)} %shard_map.158), channel_id=1, source_target_pairs={{0,1},{1,0},{2,3},{3,2},{4,5},{5,4},{6,7},{7,6},{8,9},{9,8},{10,11... | collective-permute-start | bytes 24584 | tf_op jit(solution)/shard_map/ppermute | solution.py:525
  5.8 29.8 %collective-permute-start.11 = (bf16[2880,128]{1,0:T(8,128)(2,1)}, bf16[2880,128]{1,0:T(8,128)(2,1)}, u32[]{:S(2)}, u32[]{:S(2)}) collective-permute-start(bf16[2880,128]{1,0:T(8,128)(2,1)} %shard_map.159.own_even), channel_id=1, source_target_pairs={{0,2},{2,0},{1,3},{3,1},{4,6},{6,4},{5,7},{7,5},{8,10},{10,8},{9,1... | collective-permute-start | bytes 2211848 | tf_op jit(solution)/shard_map/ppermute | solution.py:563
  10.4 3.2 %copy-start.20 = (bf16[736,256]{1,0:T(8,128)(2,1)}, bf16[736,256]{1,0:T(8,128)(2,1)S(1)}, u32[]{:S(2)}) copy-start(bf16[736,256]{1,0:T(8,128)(2,1)S(1)} %get-tuple-element.32) | copy-start | bytes 1130500
  10.4 14.2 %copy-start.16 = (s32[1,8,8]{2,1,0:T(8,128)S(1)}, s32[1,8,8]{2,1,0:T(8,128)}, u32[]{:S(2)}) copy-start(s32[1,8,8]{2,1,0:T(8,128)} %sends.1) | copy-start | bytes 772
  13.0 22.5 %collective-permute-start.3 = (bf16[320,768]{1,0:T(8,128)(2,1)}, bf16[320,768]{1,0:T(8,128)(2,1)}, u32[]{:S(2)}, u32[]{:S(2)}) collective-permute-start(bf16[320,768]{1,0:T(8,128)(2,1)} %shard_map.162), channel_id=1, source_target_pairs={{0,2},{2,0},{1,3},{3,1},{4,6},{6,4},{5,7},{7,5},{8,10},{10,8},{9,1... | collective-permute-start | bytes 1474568 | tf_op jit(solution)/shard_map/ppermute | solution.py:592
  13.6 22.0 %all-to-all-start = ((bf16[8,128,128]{2,1,0:T(8,128)(2,1)}), bf16[8,128,128]{2,1,0:T(8,128)(2,1)}, u32[]{:S(2)}, u32[]{:S(2)}) async-start(bf16[8,128,128]{2,1,0:T(8,128)(2,1)} %shard_map.160), calls=%async_computation | async-start | bytes 524288 | tf_op jit(solution)/shard_map/all_to_all | solution.py:575
  18.8 15.3 %collective-permute-start.1 = (bf16[736,256]{1,0:T(8,128)(2,1)}, bf16[736,256]{1,0:T(8,128)(2,1)S(1)}, u32[]{:S(2)}, u32[]{:S(2)}) collective-permute-start(bf16[736,256]{1,0:T(8,128)(2,1)} %copy-done.21), channel_id=1, source_target_pairs={{0,4},{4,8},{8,12},{1,5},{5,9},{9,13},{2,6},{6,10},{10,14},{3,7},{... | collective-permute-start | bytes 1130504 | tf_op jit(solution)/shard_map/ppermute | solution.py:589
  22.2 12.6 %collective-permute-start.2 = (bf16[736,256]{1,0:T(8,128)(2,1)}, bf16[736,256]{1,0:T(8,128)(2,1)S(1)}, u32[]{:S(2)}, u32[]{:S(2)}) collective-permute-start(bf16[736,256]{1,0:T(8,128)(2,1)} %copy-done.20), channel_id=1, source_target_pairs={{4,0},{8,4},{12,8},{5,1},{9,5},{13,9},{6,2},{10,6},{14,10},{7,3},{... | collective-permute-start | bytes 1130504 | tf_op jit(solution)/shard_map/ppermute | solution.py:590
  29.5 11.3 %copy-start.15 = (s32[1,16,3]{1,0,2:T(1,128)S(1)}, s32[1,16,3]{1,0,2:T(1,128)}, u32[]{:S(2)}) copy-start(s32[1,16,3]{1,0,2:T(1,128)} %param.28) | copy-start | bytes 580
  35.6 53.7 %all-to-all-start.1 = ((bf16[64,128,128]{2,1,0:T(8,128)(2,1)}), bf16[64,128,128]{2,1,0:T(8,128)(2,1)}, u32[]{:S(2)}, u32[]{:S(2)}) async-start(bf16[64,128,128]{2,1,0:T(8,128)(2,1)} %copy-done.2), calls=%async_computation.1 | async-start | bytes 4194304 | tf_op jit(solution)/shard_map/all_to_all | solution.py:615
  43.9 5.1 %copy-start.6 = (bf16[736,256]{1,0:T(8,128)(2,1)S(1)}, bf16[736,256]{1,0:T(8,128)(2,1)}, u32[]{:S(2)}) copy-start(bf16[736,256]{1,0:T(8,128)(2,1)} %copy-done.5) | copy-start | bytes 1130500
  43.9 13.6 %collective-permute-start.6 = (bf16[320,768]{1,0:T(8,128)(2,1)}, bf16[320,768]{1,0:T(8,128)(2,1)S(1)}, u32[]{:S(2)}, u32[]{:S(2)}) collective-permute-start(bf16[320,768]{1,0:T(8,128)(2,1)} %collective-permute-done.3.refs_0_), channel_id=1, source_target_pairs={{0,16},{16,0},{1,17},{17,1},{2,18},{18,2},{3,19},{19,3},{4,20},{20... | collective-permute-start | bytes 1474568 | tf_op jit(solution)/shard_map/ppermute | solution.py:616
  47.4 19.4 %collective-permute-start.12 = (bf16[2880,128]{1,0:T(8,128)(2,1)S(1)}, bf16[2880,128]{1,0:T(8,128)(2,1)S(1)}, u32[]{:S(2)}, u32[]{:S(2)}) collective-permute-start(bf16[2880,128]{1,0:T(8,128)(2,1)S(1)} %shard_map.165.own_odd), channel_id=1, source_target_pairs={{0,2},{2,0},{1,3},{3,1},{4,6},{6,4},{5,7},{7,5},{8,10},{10,8},{9,1... | collective-permute-start | bytes 2211848 | tf_op jit(solution)/shard_map/ppermute | solution.py:563
  50.9 10.6 %copy-start.3 = (bf16[1024,512]{1,0:T(8,128)(2,1)S(1)}, bf16[1024,512]{1,0:T(8,128)(2,1)}, u32[]{:S(2)}) copy-start(bf16[1024,512]{1,0:T(8,128)(2,1)} %up.1) | copy-start | bytes 3145732
  50.9 10.6 %copy-start.4 = (bf16[1024,512]{1,0:T(8,128)(2,1)S(1)}, bf16[1024,512]{1,0:T(8,128)(2,1)}, u32[]{:S(2)}) copy-start(bf16[1024,512]{1,0:T(8,128)(2,1)} %down.3) | copy-start | bytes 3145732
  50.9 10.6 %copy-start.7 = (bf16[512,256]{1,0:T(8,128)(2,1)S(1)}, bf16[512,256]{1,0:T(8,128)(2,1)}, u32[]{:S(2)}) copy-start(bf16[512,256]{1,0:T(8,128)(2,1)} %ocean_up.3) | copy-start | bytes 786436
  50.9 10.6 %copy-start.8 = (bf16[512,256]{1,0:T(8,128)(2,1)S(1)}, bf16[512,256]{1,0:T(8,128)(2,1)}, u32[]{:S(2)}) copy-start(bf16[512,256]{1,0:T(8,128)(2,1)} %ocean_down.3) | copy-start | bytes 786436
  50.9 10.6 %copy-start.17 = (f32[512]{0:T(512)S(1)}, f32[512]{0:T(512)}, u32[]{:S(2)}) copy-start(f32[512]{0:T(512)} %gain.1) | copy-start | bytes 6148
  50.9 10.6 %copy-start.18 = (f32[256]{0:T(256)S(1)}, f32[256]{0:T(256)}, u32[]{:S(2)}) copy-start(f32[256]{0:T(256)} %ocean_gain.1) | copy-start | bytes 3076
  54.0 5.4 %collective-permute-start.7 = (bf16[320,768]{1,0:T(8,128)(2,1)}, bf16[320,768]{1,0:T(8,128)(2,1)S(1)}, u32[]{:S(2)}, u32[]{:S(2)}) collective-permute-start(bf16[320,768]{1,0:T(8,128)(2,1)} %collective-permute-done.3.refs_0_), channel_id=1, source_target_pairs={{0,1},{1,0},{2,3},{3,2},{4,5},{5,4},{6,7},{7,6},{8,9},{9,8},{10,11... | collective-permute-start | bytes 1474568 | tf_op jit(solution)/shard_map/ppermute | solution.py:621
  57.4 3.5 %collective-permute-start.8 = (bf16[320,768]{1,0:T(8,128)(2,1)S(1)}, bf16[320,768]{1,0:T(8,128)(2,1)S(1)}, u32[]{:S(2)}, u32[]{:S(2)}) collective-permute-start(bf16[320,768]{1,0:T(8,128)(2,1)S(1)} %collective-permute-done.6.refs_1_), channel_id=1, source_target_pairs={{0,1},{1,0},{2,3},{3,2},{4,5},{5,4},{6,7},{7,6},{8,9},{9,8},{10,11... | collective-permute-start | bytes 1474568 | tf_op jit(solution)/shard_map/ppermute | solution.py:621
  57.4 23.0 %collective-permute-start.9 = (bf16[1440,128]{1,0:T(8,128)(2,1)S(1)}, bf16[1440,128]{1,0:T(8,128)(2,1)S(1)}, u32[]{:S(2)}, u32[]{:S(2)}) collective-permute-start(bf16[1440,128]{1,0:T(8,128)(2,1)S(1)} %get-tuple-element.38.own_even), channel_id=1, source_target_pairs={{0,2},{2,0},{1,3},{3,1},{4,6},{6,4},{5,7},{7,5},{8,10},{10,8},{9,1... | collective-permute-start | bytes 1105928 | tf_op jit(solution)/shard_map/ppermute | solution.py:563
  58.9 23.7 %collective-permute-start.10 = (bf16[1440,128]{1,0:T(8,128)(2,1)S(1)}, bf16[1440,128]{1,0:T(8,128)(2,1)S(1)}, u32[]{:S(2)}, u32[]{:S(2)}) collective-permute-start(bf16[1440,128]{1,0:T(8,128)(2,1)S(1)} %get-tuple-element.41.own_odd), channel_id=1, source_target_pairs={{0,2},{2,0},{1,3},{3,1},{4,6},{6,4},{5,7},{7,5},{8,10},{10,8},{9,1... | collective-permute-start | bytes 1105928 | tf_op jit(solution)/shard_map/ppermute | solution.py:563
  59.5 38.1 %collective-permute-start.4 = (bf16[1440,128]{1,0:T(8,128)(2,1)}, bf16[1440,128]{1,0:T(8,128)(2,1)S(1)}, u32[]{:S(2)}, u32[]{:S(2)}) collective-permute-start(bf16[1440,128]{1,0:T(8,128)(2,1)} %get-tuple-element.37.own_even), channel_id=1, source_target_pairs={{0,2},{2,0},{1,3},{3,1},{4,6},{6,4},{5,7},{7,5},{8,10},{10,8},{9,1... | collective-permute-start | bytes 1105928 | tf_op jit(solution)/shard_map/ppermute | solution.py:563
  61.0 36.9 %collective-permute-start.5 = (bf16[1440,128]{1,0:T(8,128)(2,1)}, bf16[1440,128]{1,0:T(8,128)(2,1)}, u32[]{:S(2)}, u32[]{:S(2)}) collective-permute-start(bf16[1440,128]{1,0:T(8,128)(2,1)} %get-tuple-element.40.own_odd), channel_id=1, source_target_pairs={{0,2},{2,0},{1,3},{3,1},{4,6},{6,4},{5,7},{7,5},{8,10},{10,8},{9,1... | collective-permute-start | bytes 1105928 | tf_op jit(solution)/shard_map/ppermute | solution.py:563
  64.8 15.5 %copy-start.10 = (bf16[1024,256]{1,0:T(8,128)(2,1)}, bf16[1024,256]{1,0:T(8,128)(2,1)S(1)}, u32[]{:S(2)}) copy-start(bf16[1024,256]{1,0:T(8,128)(2,1)S(1)} %get-tuple-element.54.across) | copy-start | bytes 1572868
  64.9 15.5 %copy-start.12 = (bf16[128,1024]{1,0:T(8,128)(2,1)}, bf16[128,1024]{1,0:T(8,128)(2,1)S(1)}, u32[]{:S(2)}) copy-start(bf16[128,1024]{1,0:T(8,128)(2,1)S(1)} %get-tuple-element.55.back) | copy-start | bytes 786436
  96.0 9.6 %copy-start.9 = (bf16[128,1024]{1,0:T(8,128)(2,1)S(1)}, bf16[128,1024]{1,0:T(8,128)(2,1)}, u32[]{:S(2)}) copy-start(bf16[128,1024]{1,0:T(8,128)(2,1)} %shard_map.171.own) | copy-start | bytes 786436
  96.0 9.6 %copy-start.11 = (bf16[1024,256]{1,0:T(8,128)(2,1)S(1)}, bf16[1024,256]{1,0:T(8,128)(2,1)}, u32[]{:S(2)}) copy-start(bf16[1024,256]{1,0:T(8,128)(2,1)} %copy-done.10) | copy-start | bytes 1572868
  96.0 9.6 %copy-start.13 = (bf16[128,1024]{1,0:T(8,128)(2,1)S(1)}, bf16[128,1024]{1,0:T(8,128)(2,1)}, u32[]{:S(2)}) copy-start(bf16[128,1024]{1,0:T(8,128)(2,1)} %copy-done.12) | copy-start | bytes 786436
  96.0 9.6 %copy-start.19 = (s32[8]{0:T(128)S(1)}, s32[8]{0:T(128)}, u32[]{:S(2)}) copy-start(s32[8]{0:T(128)} %mask.1) | copy-start | bytes 100
  96.0 9.6 %collective-permute-start.13 = (bf16[128,1024]{1,0:T(8,128)(2,1)}, bf16[128,1024]{1,0:T(8,128)(2,1)S(1)}, u32[]{:S(2)}, u32[]{:S(2)}) collective-permute-start(bf16[128,1024]{1,0:T(8,128)(2,1)} %shard_map.171.own), channel_id=1, source_target_pairs={{0,2},{2,0},{1,3},{3,1},{4,6},{6,4},{5,7},{7,5},{8,10},{10,8},{9,1... | collective-permute-start | bytes 786440 | tf_op jit(solution)/shard_map/ppermute | solution.py:653
  (6 other events, 10.6 us)

commit v5 on v4

--- a/solution.py
+++ b/solution.py
@@ -397,23 +397,39 @@
     out[0] = total.astype(jnp.bfloat16)
 
 
-def flux_remap_body(pattern, slots, blocks, ocean, out, total):
+def slot_uses_body(pattern, uses):
+    def clear(slot, carry):
+        uses[0, slot] = -1
+        return carry
+
+    def note(entry, carry):
+        slot = pattern[0, 0, entry]
+        uses[jnp.where(uses[0, slot] >= 0, 1, 0), slot] = entry
+        return carry
+
+    lax.fori_loop(0, uses.shape[1], clear, 0, unroll=8)
+    lax.fori_loop(0, pattern.shape[2], note, 0, unroll=8)
+
+
+def flux_remap_body(pattern, uses, slots, blocks, ocean, out, total):
     total[...] = jnp.zeros_like(total)
-    group = math.gcd(pattern.shape[2], 8)
-
-    def entries(step, carry):
+    group = math.gcd(slots.shape[0], 8)
+
+    def some_slots(step, carry):
         found = []
         for index in range(group):
-            at = step * group + index
-            found.append(
-                jnp.dot(slots[pattern[0, 0, at]], blocks[pattern[2, 0, at]], preferred_element_type=jnp.float32)
+            slot = step * group + index
+            wide = jnp.concatenate(
+                [blocks[pattern[2, 0, uses[0, slot]]], blocks[pattern[2, 0, uses[1, slot]]]], axis=1
             )
+            found.append(jnp.dot(slots[slot], wide, preferred_element_type=jnp.float32))
         for index in range(group):
-            tile = pattern[1, 0, step * group + index]
-            total[tile] = total[tile] + found[index]
+            for use in range(2):
+                tile = pattern[1, 0, uses[use, step * group + index]]
+                total[tile] = total[tile] + found[index][:, use * 128 : use * 128 + 128]
         return carry
 
-    lax.fori_loop(0, pattern.shape[2] // group, entries, 0)
+    lax.fori_loop(0, slots.shape[0] // group, some_slots, 0)
     for tile in range(total.shape[0]):
         lanes = slice(tile * 128, tile * 128 + 128)
         out[:, lanes] = (ocean[:, lanes].astype(jnp.float32) + 0.125 * total[tile]).astype(jnp.bfloat16)
@@ -441,7 +457,7 @@
             out[:, at] = (a[:, inside] + keep * delta[:, inside]).astype(jnp.bfloat16)
 
 
-def pack_body(place, up, down, ocean_up, ocean_down, out):
+def pack_body(quarter, other, up, down, ocean_up, ocean_down, out):
     depth, channels = up.shape
     half, narrow = ocean_up.shape[0] // 2, ocean_down.shape[1]
     out[0:depth, 0:channels] = up[...]
@@ -453,27 +469,27 @@
 
 
 def pack_weights(up, down, ocean_up, ocean_down):
-    quarter = lax.axis_index("groups") * 2 + lax.axis_index("pair")
-    place = jnp.stack([quarter, 1 - lax.axis_index("chan")])
+    quarter = (lax.axis_index("groups") * 2 + lax.axis_index("pair")).reshape(1)
+    other = (1 - lax.axis_index("chan")).reshape(1)
     depth, shallow = up.shape[0] // 4, ocean_up.shape[0] // 4
     width, narrow = up.shape[1] // 2, ocean_up.shape[1] // 2
     shape = (depth + shallow // 2, 3 * width)
     return pl.pallas_call(
         pack_body,
         grid_spec=pltpu.PrefetchScalarGridSpec(
-            num_scalar_prefetch=1,
+            num_scalar_prefetch=2,
             grid=(1,),
             in_specs=[
-                pl.BlockSpec((depth, 2 * width), lambda _, place: (place[0], 0)),
-                pl.BlockSpec((depth, width), lambda _, place: (place[0], place[1])),
-                pl.BlockSpec((shallow, 2 * narrow), lambda _, place: (place[0], 0)),
-                pl.BlockSpec((shallow, narrow), lambda _, place: (place[0], place[1])),
+                pl.BlockSpec((depth, 2 * width), lambda _, quarter, other: (quarter[0], 0)),
+                pl.BlockSpec((depth, width), lambda _, quarter, other: (quarter[0], other[0])),
+                pl.BlockSpec((shallow, 2 * narrow), lambda _, quarter, other: (quarter[0], 0)),
+                pl.BlockSpec((shallow, narrow), lambda _, quarter, other: (quarter[0], other[0])),
             ],
-            out_specs=pl.BlockSpec(shape, lambda _, place: (0, 0)),
+            out_specs=pl.BlockSpec(shape, lambda _, quarter, other: (0, 0)),
         ),
         out_shape=jax.ShapeDtypeStruct(shape, up.dtype),
         compiler_params=pltpu.CompilerParams(vmem_limit_bytes=60 * 2**20),
-    )(place, up, down, ocean_up, ocean_down)
+    )(quarter, other, up, down, ocean_up, ocean_down)
 
 
 def after(value, *earlier):
@@ -639,13 +655,23 @@
     )
     result = None
     for step, ((first, count), *values) in enumerate(plan):
+        if step == 1:
+            uses = local_call(
+                slot_uses_body,
+                jax.ShapeDtypeStruct((2, flux_sends.shape[1] * flux_sends.shape[2]), jnp.int32),
+                (after(flux_rows, result),),
+                [smem()],
+                smem(),
+                8,
+            )
+            result = after(result, uses)
         if step == len(plan) - 1:
             entries = flux_pattern.shape[1]
             ocean_input = local_call(
                 flux_remap_body,
                 jax.ShapeDtypeStruct((flux_depth, ocean_cells), bf16),
-                (flux_rows, flux_in, after(remap_blocks, result), ocean_state),
-                [smem(), vmem(), vmem(), vmem()],
+                (flux_rows, uses, flux_in, after(remap_blocks, result), ocean_state),
+                [smem(), smem(), vmem(), vmem(), vmem()],
                 vmem(),
                 60,
                 scratch=[pltpu.VMEM((ocean_count, flux_depth, 128), f32)],

time: 111 us -> 110 us (level); the launches traced: 109 us -> 109 us
    pallas_call x15 -> x16, Pallas kernels: 58.7 us -> 59.8 us  [local_call(): pl.pallas_call(body, grid=(grid,), out_shape=out_shape, in_specs=in_specs...]
    ppermute x6, waiting for transfers between devices: 4.54 us -> 3.41 us  [cross(): return [lax.ppermute(value, 'chan', SWAP) for value in values]]
    unnamed x44 -> x48, local copies, waits for them, and re-layouts: 4.51 us -> 5.06 us
  transfers between devices with their start and end apart: 16 -> 16, of which waited for: 7 -> 7; matrix products, arithmetic and copies ran while one was open for 1% -> 0% of each run, Pallas kernels for 50% -> 50%
where the time goes in v5:
time: 110 us; the launch traced here: 109 us
  Pallas kernels  61.8 us (56%)
  starting transfers between devices  27 us (25%)
  waiting for transfers between devices  14.2 us (13%)
  local copies, waits for them, and re-layouts  5.06 us (5%)
    pallas_call x16, Pallas kernels, local_call(): pl.pallas_call(body, grid=(grid,), out_shape=out_shape, in_specs=in_specs...  59.8 us
    ppermute x6, starting transfers between devices, cross(): return [lax.ppermute(value, 'chan', SWAP) for value in values]  7.1 us
    all_to_all x1, starting transfers between devices, quick_shards(): lax.all_to_all(after(flux_out, low, high, *others, one), peers, split_axi...  5.21 us
    all_to_all x1, starting transfers between devices, quick_shards(): lax.all_to_all(sea_out, peers, split_axis=0, concat_axis=0, tiled=True)  5.21 us
    unnamed x48, local copies, waits for them, and re-layouts  5.06 us
    ppermute x1, waiting for transfers between devices, quick_shards(): lax.ppermute(messages[0], 'lat', [(i, i + 1) for i in range(lat_bands - 1)])  4.51 us
    ppermute x6, waiting for transfers between devices, cross(): return [lax.ppermute(value, 'chan', SWAP) for value in values]  3.41 us
    ppermute x1, starting transfers between devices, quick_shards(): lax.ppermute(messages[0], 'lat', [(i, i + 1) for i in range(lat_bands - 1)])  3.36 us
  transfers between devices with their start and end apart: 16, of which 7 were waited for; matrix products, arithmetic and copies ran while one was open for 0% of the time, Pallas kernels for 50%

profile of v5, /device:TPU:16, one launch (start us, length us, event | category | flops | bytes accessed | tf_op | source)
XLA Modules:
  0.0 109.0 jit_solution(14242449676913242046)
XLA Ops:
  0.6 1.6 %shard_map.158 = bf16[16,256]{1,0:T(8,128)(2,1)} custom-call(bf16[8,720,256]{2,1,0:T(8,128)(2,1)} %bitcast.12, bf16[8,720,256]{2,1,0:T(8,128)(2,1)} %bitcast.13), custom_call_target="tpu_custom_call" | custom-call | flops 1 | bytes 1 | tf_op jit(solution)/shard_map/pallas_call | solution.py:187
  2.3 1.4 %collective-permute-done.refs_6_.sides.refs_8_ = bf16[16,256]{1,0:T(8,128)(2,1)S(1)} collective-permute-done((bf16[16,256]{1,0:T(8,128)(2,1)}, bf16[16,256]{1,0:T(8,128)(2,1)S(1)}, u32[]{:S(2)}, u32[]{:S(2)}) %collective-permute-start) | collective-permute-done | bytes 8224 | tf_op jit(solution)/shard_map/ppermute | solution.py:541
  3.7 2.1 %shard_map.159.own_even = bf16[2880,128]{1,0:T(8,128)(2,1)} custom-call(bf16[8,720,256]{2,1,0:T(8,128)(2,1)S(1)} %bitcast.14, bf16[8,720,256]{2,1,0:T(8,128)(2,1)S(1)} %bitcast.15, bf16[8,720,256]{2,1,0:T(8,128)(2,1)S(1)} %bitcast.16, bf16[8,720,256]{2,1,0:T(8,128)(2,1)S(1)} %bitcast.17, bf16[8,720,256]{2,1,0:T(8,128)(2,1)S(1)} %bitcast.18, ...), custom_call_target="tpu_custom_call" | custom-call | flops 1 | bytes 1 | tf_op jit(solution)/shard_map/pallas_call | solution.py:187
  5.7 1.5 %collective-permute-start.11 = (bf16[2880,128]{1,0:T(8,128)(2,1)}, bf16[2880,128]{1,0:T(8,128)(2,1)}, u32[]{:S(2)}, u32[]{:S(2)}) collective-permute-start(bf16[2880,128]{1,0:T(8,128)(2,1)} %shard_map.159.own_even), channel_id=1, source_target_pairs={{0,2},{2,0},{1,3},{3,1},{4,6},{6,4},{5,7},{7,5},{8,10},{10,8},{9,1... | collective-permute-start | bytes 2211848 | tf_op jit(solution)/shard_map/ppermute | solution.py:579
  7.2 1.8 %shard_map.160 = bf16[8,128,128]{2,1,0:T(8,128)(2,1)} custom-call(s32[1,1,8]{2,1,0:T(1,128)} %bitcast.55, bf16[128,1024]{1,0:T(8,128)(2,1)} %ocean.2), custom_call_target="tpu_custom_call" | custom-call | flops 1 | bytes 1 | tf_op jit(solution)/shard_map/pallas_call | solution.py:187
  9.8 2.0 %shard_map.162 = bf16[320,768]{1,0:T(8,128)(2,1)} custom-call(s32[1]{0:T(128)} %bitcast.5.quarter, s32[1]{0:T(128)} %bitcast.6.other, bf16[1024,512]{1,0:T(8,128)(2,1)} %up.1, bf16[1024,512]{1,0:T(8,128)(2,1)} %down.3, bf16[512,256]{1,0:T(8,128)(2,1)} %ocean_up.3, bf16[512,256]{1,0:T(8,128)(2,1)} %ocean_down.3), custom_call_target="tpu_custom_call" | custom-call | tf_op jit(solution)/shard_map/pallas_call | solution.py:477
  12.4 5.2 %all-to-all-start = ((bf16[8,128,128]{2,1,0:T(8,128)(2,1)}), bf16[8,128,128]{2,1,0:T(8,128)(2,1)}, u32[]{:S(2)}, u32[]{:S(2)}) async-start(bf16[8,128,128]{2,1,0:T(8,128)(2,1)} %shard_map.160), calls=%async_computation | async-start | bytes 524288 | tf_op jit(solution)/shard_map/all_to_all | solution.py:591
  17.6 3.4 %collective-permute-start.1 = (bf16[736,256]{1,0:T(8,128)(2,1)}, bf16[736,256]{1,0:T(8,128)(2,1)S(1)}, u32[]{:S(2)}, u32[]{:S(2)}) collective-permute-start(bf16[736,256]{1,0:T(8,128)(2,1)} %copy-done.23), channel_id=1, source_target_pairs={{0,4},{4,8},{8,12},{1,5},{5,9},{9,13},{2,6},{6,10},{10,14},{3,7},{... | collective-permute-start | bytes 1130504 | tf_op jit(solution)/shard_map/ppermute | solution.py:605
  20.9 2.5 %collective-permute-start.2 = (bf16[736,256]{1,0:T(8,128)(2,1)}, bf16[736,256]{1,0:T(8,128)(2,1)S(1)}, u32[]{:S(2)}, u32[]{:S(2)}) collective-permute-start(bf16[736,256]{1,0:T(8,128)(2,1)} %copy-done.22), channel_id=1, source_target_pairs={{4,0},{8,4},{12,8},{5,1},{9,5},{13,9},{6,2},{10,6},{14,10},{7,3},{... | collective-permute-start | bytes 1130504 | tf_op jit(solution)/shard_map/ppermute | solution.py:606
  23.4 3.5 %shard_map.163 = bf16[64,128,128]{2,1,0:T(8,128)(2,1)S(1)} custom-call(s32[1,8,8]{2,1,0:T(8,128)S(1)} %copy-done.18, bf16[5760,256]{1,0:T(8,128)(2,1)S(1)} %bitcast.22), custom_call_target="tpu_custom_call" | custom-call | flops 1 | bytes 1 | tf_op jit(solution)/shard_map/pallas_call | solution.py:187
  28.3 4.5 %collective-permute-done.1 = bf16[736,256]{1,0:T(8,128)(2,1)S(1)} collective-permute-done((bf16[736,256]{1,0:T(8,128)(2,1)}, bf16[736,256]{1,0:T(8,128)(2,1)S(1)}, u32[]{:S(2)}, u32[]{:S(2)}) %collective-permute-start.1) | collective-permute-done | bytes 376864 | tf_op jit(solution)/shard_map/ppermute | solution.py:605
  35.2 5.2 %all-to-all-start.1 = ((bf16[64,128,128]{2,1,0:T(8,128)(2,1)}), bf16[64,128,128]{2,1,0:T(8,128)(2,1)}, u32[]{:S(2)}, u32[]{:S(2)}) async-start(bf16[64,128,128]{2,1,0:T(8,128)(2,1)} %copy-done.2), calls=%async_computation.1 | async-start | bytes 4194304 | tf_op jit(solution)/shard_map/all_to_all | solution.py:631
  40.4 1.6 %copy-done.1 = bf16[64,128,128]{2,1,0:T(8,128)(2,1)S(1)} copy-done((bf16[64,128,128]{2,1,0:T(8,128)(2,1)S(1)}, bf16[64,128,128]{2,1,0:T(8,128)(2,1)}, u32[]{:S(2)}) %copy-start.1) | copy-done | bytes 2097176
  42.0 1.5 %shard_map.164.refs_9_.refs_11_ = f32[16,128,128]{2,1,0:T(8,128)S(1)} custom-call(s32[3,1,16]{2,1,0:T(1,128)S(1)} %bitcast.49, bf16[8,128,128]{2,1,0:T(8,128)(2,1)} %all-to-all-done.slots, bf16[64,128,128]{2,1,0:T(8,128)(2,1)S(1)} %copy-done.1), custom_call_target="tpu_custom_call" | custom-call | flops 1 | bytes 1 | tf_op jit(solution)/shard_map/pallas_call | solution.py:187
  43.5 1.6 %collective-permute-start.6 = (bf16[320,768]{1,0:T(8,128)(2,1)}, bf16[320,768]{1,0:T(8,128)(2,1)S(1)}, u32[]{:S(2)}, u32[]{:S(2)}) collective-permute-start(bf16[320,768]{1,0:T(8,128)(2,1)} %collective-permute-done.3.refs_0_), channel_id=1, source_target_pairs={{0,16},{16,0},{1,17},{17,1},{2,18},{18,2},{3,19},{19,3},{4,20},{20... | collective-permute-start | bytes 1474568 | tf_op jit(solution)/shard_map/ppermute | solution.py:632
  45.1 1.9 %shard_map.165.own_odd = bf16[2880,128]{1,0:T(8,128)(2,1)S(1)} custom-call(bf16[8,720,256]{2,1,0:T(8,128)(2,1)S(1)} %bitcast.25, bf16[8,720,256]{2,1,0:T(8,128)(2,1)S(1)} %bitcast.24, bf16[8,720,256]{2,1,0:T(8,128)(2,1)S(1)} %bitcast.23, bf16[8,720,256]{2,1,0:T(8,128)(2,1)S(1)} %bitcast.26, bf16[8,720,256]{2,1,0:T(8,128)(2,1)S(1)} %bitcast.27, ...), custom_call_target="tpu_custom_call" | custom-call | flops 1 | bytes 1 | tf_op jit(solution)/shard_map/pallas_call | solution.py:187
  47.0 1.6 %collective-permute-start.12 = (bf16[2880,128]{1,0:T(8,128)(2,1)S(1)}, bf16[2880,128]{1,0:T(8,128)(2,1)S(1)}, u32[]{:S(2)}, u32[]{:S(2)}) collective-permute-start(bf16[2880,128]{1,0:T(8,128)(2,1)S(1)} %shard_map.165.own_odd), channel_id=1, source_target_pairs={{0,2},{2,0},{1,3},{3,1},{4,6},{6,4},{5,7},{7,5},{8,10},{10,8},{9,1... | collective-permute-start | bytes 2211848 | tf_op jit(solution)/shard_map/ppermute | solution.py:579
  48.6 1.9 %shard_map.166 = (bf16[1440,128]{1,0:T(8,128)(2,1)S(1)}, bf16[1440,128]{1,0:T(8,128)(2,1)}) custom-call(bf16[1,736,256]{2,1,0:T(8,128)(2,1)S(1)} %bitcast.41, bf16[8,720,256]{2,1,0:T(8,128)(2,1)S(1)} %bitcast.29, bf16[8,720,256]{2,1,0:T(8,128)(2,1)S(1)} %bitcast.30, bf16[8,720,256]{2,1,0:T(8,128)(2,1)S(1)} %bitcast.31, bf16[8,720,256]{2,1,0:T(8,128)(2,1)S(1)} %bitcast.32, ...), custom_call_target="tpu_custom_call" | custom-call | flops 1 | bytes 1 | tf_op jit(solution)/shard_map/pallas_call | solution.py:187
  50.5 3.1 %shard_map.167 = (bf16[1440,128]{1,0:T(8,128)(2,1)S(1)}, bf16[1440,128]{1,0:T(8,128)(2,1)}) custom-call(bf16[1,736,256]{2,1,0:T(8,128)(2,1)S(1)} %bitcast.42, bf16[8,720,256]{2,1,0:T(8,128)(2,1)S(1)} %bitcast.35, bf16[8,720,256]{2,1,0:T(8,128)(2,1)S(1)} %bitcast.36, bf16[8,720,256]{2,1,0:T(8,128)(2,1)S(1)} %bitcast.37, bf16[8,720,256]{2,1,0:T(8,128)(2,1)S(1)} %bitcast.38, ...), custom_call_target="tpu_custom_call" | custom-call | flops 1 | bytes 1 | tf_op jit(solution)/shard_map/pallas_call | solution.py:187
  53.7 3.4 %collective-permute-done.6.refs_1_ = bf16[320,768]{1,0:T(8,128)(2,1)S(1)} collective-permute-done((bf16[320,768]{1,0:T(8,128)(2,1)}, bf16[320,768]{1,0:T(8,128)(2,1)S(1)}, u32[]{:S(2)}, u32[]{:S(2)}) %collective-permute-start.6) | collective-permute-done | bytes 491552 | tf_op jit(solution)/shard_map/ppermute | solution.py:632
  57.0 1.5 %collective-permute-start.9 = (bf16[1440,128]{1,0:T(8,128)(2,1)S(1)}, bf16[1440,128]{1,0:T(8,128)(2,1)S(1)}, u32[]{:S(2)}, u32[]{:S(2)}) collective-permute-start(bf16[1440,128]{1,0:T(8,128)(2,1)S(1)} %get-tuple-element.40.own_even), channel_id=1, source_target_pairs={{0,2},{2,0},{1,3},{3,1},{4,6},{6,4},{5,7},{7,5},{8,10},{10,8},{9,1... | collective-permute-start | bytes 1105928 | tf_op jit(solution)/shard_map/ppermute | solution.py:579
  59.1 1.5 %collective-permute-start.4 = (bf16[1440,128]{1,0:T(8,128)(2,1)}, bf16[1440,128]{1,0:T(8,128)(2,1)S(1)}, u32[]{:S(2)}, u32[]{:S(2)}) collective-permute-start(bf16[1440,128]{1,0:T(8,128)(2,1)} %get-tuple-element.39.own_even), channel_id=1, source_target_pairs={{0,2},{2,0},{1,3},{3,1},{4,6},{6,4},{5,7},{7,5},{8,10},{10,8},{9,1... | collective-permute-start | bytes 1105928 | tf_op jit(solution)/shard_map/ppermute | solution.py:579
  61.1 3.3 %shard_map.168 = (bf16[512,2048]{1,0:T(8,128)(2,1)S(1)}, bf16[2048,256]{1,0:T(8,128)(2,1)S(1)}, bf16[1024,256]{1,0:T(8,128)(2,1)S(1)}, bf16[128,1024]{1,0:T(8,12...) custom-call(s32[1]{0:T(128)} %bitcast.9.chan, bf16[1024,512]{1,0:T(8,128)(2,1)S(1)} %copy-done.3, ...), custom_call_target="tpu_custom_call" | custom-call | flops 1 | bytes 1 | tf_op jit(solution)/shard_map/pallas_call | solution.py:187
  64.4 2.0 %collective-permute-done.12.other_odd = bf16[2880,128]{1,0:T(8,128)(2,1)S(1)} collective-permute-done((bf16[2880,128]{1,0:T(8,128)(2,1)S(1)}, bf16[2880,128]{1,0:T(8,128)(2,1)S(1)}, u32[]{:S(2)}, u32[]{:S(2)}) %collective-permute-start.12) | collective-permute-done | bytes 737312 | tf_op jit(solution)/shard_map/ppermute | solution.py:579
  66.4 13.6 %shard_map.169.refs_0_ = bf16[8,720,256]{2,1,0:T(8,128)(2,1)} custom-call(bf16[2880,128]{1,0:T(8,128)(2,1)} %shard_map.159.own_even, bf16[2880,128]{1,0:T(8,128)(2,1)S(1)} %shard_map.165.own_odd, bf16[2880,128]{1,0:T(8,128)(2,1)} %collective-permute-done.11.other_even, bf16[2880,128]{1,0:T(8,128)(2,1)S(1)} %collective-permute-done.12.other_odd, ...), custom_call_target="tpu_custom_call" | custom-call | flops 1 | bytes 1 | tf_op jit(solution)/shard_map/pallas_call | solution.py:187
  80.0 2.2 %shard_map.170.uses = s32[2,64]{1,0:T(2,128)S(1)} custom-call(s32[3,1,128]{2,1,0:T(1,128)S(1)} %bitcast.53), custom_call_target="tpu_custom_call" | custom-call | flops 1 | bytes 1 | tf_op jit(solution)/shard_map/pallas_call | solution.py:187
  82.8 6.6 %shard_map.171.refs_0_ = bf16[8,720,256]{2,1,0:T(8,128)(2,1)} custom-call(bf16[1440,128]{1,0:T(8,128)(2,1)S(1)} %get-tuple-element.40.own_even, bf16[1440,128]{1,0:T(8,128)(2,1)S(1)} %get-tuple-element.43.own_odd, bf16[1440,128]{1,0:T(8,128)(2,1)S(1)} %collective-permute-done.9.other_even, ...), custom_call_target="tpu_custom_call", output_to_operand_aliasing={{}: (7, {})} | custom-call | flops 1 | bytes 1 | tf_op jit(solution)/shard_map/pallas_call | solution.py:187
  89.4 5.6 %shard_map.172.own = bf16[128,1024]{1,0:T(8,128)(2,1)} custom-call(s32[3,1,128]{2,1,0:T(1,128)} %bitcast.52, s32[2,64]{1,0:T(2,128)} %copy-done.17, bf16[64,128,128]{2,1,0:T(8,128)(2,1)} %all-to-all-done.1.slots, bf16[64,128,128]{2,1,0:T(8,128)(2,1)} %blocks.1, bf16[128,1024]{1,0:T(8,128)(2,1)} %ocean.2), custom_call_target="tpu_custom_call" | custom-call | flops 1 | bytes 1 | tf_op jit(solution)/shard_map/pallas_call | solution.py:187
  95.0 1.6 %collective-permute-start.13 = (bf16[128,1024]{1,0:T(8,128)(2,1)}, bf16[128,1024]{1,0:T(8,128)(2,1)S(1)}, u32[]{:S(2)}, u32[]{:S(2)}) collective-permute-start(bf16[128,1024]{1,0:T(8,128)(2,1)} %shard_map.172.own), channel_id=1, source_target_pairs={{0,2},{2,0},{1,3},{3,1},{4,6},{6,4},{5,7},{7,5},{8,10},{10,8},{9,1... | collective-permute-start | bytes 786440 | tf_op jit(solution)/shard_map/ppermute | solution.py:679
  96.6 1.4 %collective-permute-done.5.other_odd = bf16[1440,128]{1,0:T(8,128)(2,1)} collective-permute-done((bf16[1440,128]{1,0:T(8,128)(2,1)}, bf16[1440,128]{1,0:T(8,128)(2,1)}, u32[]{:S(2)}, u32[]{:S(2)}) %collective-permute-start.5) | collective-permute-done | bytes 368672 | tf_op jit(solution)/shard_map/ppermute | solution.py:579
  98.0 7.7 %shard_map.173 = bf16[8,720,256]{2,1,0:T(8,128)(2,1)} custom-call(bf16[1440,128]{1,0:T(8,128)(2,1)} %get-tuple-element.39.own_even, bf16[1440,128]{1,0:T(8,128)(2,1)} %get-tuple-element.42.own_odd, bf16[1440,128]{1,0:T(8,128)(2,1)S(1)} %collective-permute-done.4.other_even, ...), custom_call_target="tpu_custom_call", output_to_operand_aliasing={{}: (7, {})} | custom-call | flops 1 | bytes 1 | tf_op jit(solution)/shard_map/pallas_call | solution.py:187
  105.8 3.3 %shard_map.174 = bf16[128,1024]{1,0:T(8,128)(2,1)} custom-call(s32[8]{0:T(128)S(1)} %copy-done.21, bf16[128,1024]{1,0:T(8,128)(2,1)S(1)} %copy-done.9, bf16[128,1024]{1,0:T(8,128)(2,1)S(1)} %collective-permute-done.13.other, f32[1,256]{1,0:T(1,128)S(1)} %get-tuple-element.57.gain, bf16[1024,256]{1,0:T(8,128)(2,1)S(1)} %copy-done.11, ...), custom_call_target="tpu_custom_call" | custom-call | flops 1 | bytes 1 | tf_op jit(solution)/shard_map/pallas_call | solution.py:187
  (65 shorter events, 6.7 us)
Async XLA Ops:
  2.3 1.4 %collective-permute-start = (bf16[16,256]{1,0:T(8,128)(2,1)}, bf16[16,256]{1,0:T(8,128)(2,1)S(1)}, u32[]{:S(2)}, u32[]{:S(2)}) collective-permute-start(bf16[16,256]{1,0:T(8,128)(2,1)} %shard_map.158), channel_id=1, source_target_pairs={{0,1},{1,0},{2,3},{3,2},{4,5},{5,4},{6,7},{7,6},{8,9},{9,8},{10,11... | collective-permute-start | bytes 24584 | tf_op jit(solution)/shard_map/ppermute | solution.py:541
  5.7 29.4 %collective-permute-start.11 = (bf16[2880,128]{1,0:T(8,128)(2,1)}, bf16[2880,128]{1,0:T(8,128)(2,1)}, u32[]{:S(2)}, u32[]{:S(2)}) collective-permute-start(bf16[2880,128]{1,0:T(8,128)(2,1)} %shard_map.159.own_even), channel_id=1, source_target_pairs={{0,2},{2,0},{1,3},{3,1},{4,6},{6,4},{5,7},{7,5},{8,10},{10,8},{9,1... | collective-permute-start | bytes 2211848 | tf_op jit(solution)/shard_map/ppermute | solution.py:579
  9.8 13.6 %copy-start.18 = (s32[1,8,8]{2,1,0:T(8,128)S(1)}, s32[1,8,8]{2,1,0:T(8,128)}, u32[]{:S(2)}) copy-start(s32[1,8,8]{2,1,0:T(8,128)} %sends.1) | copy-start | bytes 772
  11.8 23.3 %collective-permute-start.3 = (bf16[320,768]{1,0:T(8,128)(2,1)}, bf16[320,768]{1,0:T(8,128)(2,1)}, u32[]{:S(2)}, u32[]{:S(2)}) collective-permute-start(bf16[320,768]{1,0:T(8,128)(2,1)} %shard_map.162), channel_id=1, source_target_pairs={{0,2},{2,0},{1,3},{3,1},{4,6},{6,4},{5,7},{7,5},{8,10},{10,8},{9,1... | collective-permute-start | bytes 1474568 | tf_op jit(solution)/shard_map/ppermute | solution.py:608
  12.4 22.8 %all-to-all-start = ((bf16[8,128,128]{2,1,0:T(8,128)(2,1)}), bf16[8,128,128]{2,1,0:T(8,128)(2,1)}, u32[]{:S(2)}, u32[]{:S(2)}) async-start(bf16[8,128,128]{2,1,0:T(8,128)(2,1)} %shard_map.160), calls=%async_computation | async-start | bytes 524288 | tf_op jit(solution)/shard_map/all_to_all | solution.py:591
  17.6 15.3 %collective-permute-start.1 = (bf16[736,256]{1,0:T(8,128)(2,1)}, bf16[736,256]{1,0:T(8,128)(2,1)S(1)}, u32[]{:S(2)}, u32[]{:S(2)}) collective-permute-start(bf16[736,256]{1,0:T(8,128)(2,1)} %copy-done.23), channel_id=1, source_target_pairs={{0,4},{4,8},{8,12},{1,5},{5,9},{9,13},{2,6},{6,10},{10,14},{3,7},{... | collective-permute-start | bytes 1130504 | tf_op jit(solution)/shard_map/ppermute | solution.py:605
  20.9 12.6 %collective-permute-start.2 = (bf16[736,256]{1,0:T(8,128)(2,1)}, bf16[736,256]{1,0:T(8,128)(2,1)S(1)}, u32[]{:S(2)}, u32[]{:S(2)}) collective-permute-start(bf16[736,256]{1,0:T(8,128)(2,1)} %copy-done.22), channel_id=1, source_target_pairs={{4,0},{8,4},{12,8},{5,1},{9,5},{13,9},{6,2},{10,6},{14,10},{7,3},{... | collective-permute-start | bytes 1130504 | tf_op jit(solution)/shard_map/ppermute | solution.py:606
  28.3 12.1 %copy-start.15 = (s32[1,16,3]{1,0,2:T(1,128)S(1)}, s32[1,16,3]{1,0,2:T(1,128)}, u32[]{:S(2)}) copy-start(s32[1,16,3]{1,0,2:T(1,128)} %param.28) | copy-start | bytes 580
  35.2 54.3 %all-to-all-start.1 = ((bf16[64,128,128]{2,1,0:T(8,128)(2,1)}), bf16[64,128,128]{2,1,0:T(8,128)(2,1)}, u32[]{:S(2)}, u32[]{:S(2)}) async-start(bf16[64,128,128]{2,1,0:T(8,128)(2,1)} %copy-done.2), calls=%async_computation.1 | async-start | bytes 4194304 | tf_op jit(solution)/shard_map/all_to_all | solution.py:631
  43.5 5.1 %copy-start.6 = (bf16[736,256]{1,0:T(8,128)(2,1)S(1)}, bf16[736,256]{1,0:T(8,128)(2,1)}, u32[]{:S(2)}) copy-start(bf16[736,256]{1,0:T(8,128)(2,1)} %copy-done.5) | copy-start | bytes 1130500
  43.5 13.6 %collective-permute-start.6 = (bf16[320,768]{1,0:T(8,128)(2,1)}, bf16[320,768]{1,0:T(8,128)(2,1)S(1)}, u32[]{:S(2)}, u32[]{:S(2)}) collective-permute-start(bf16[320,768]{1,0:T(8,128)(2,1)} %collective-permute-done.3.refs_0_), channel_id=1, source_target_pairs={{0,16},{16,0},{1,17},{17,1},{2,18},{18,2},{3,19},{19,3},{4,20},{20... | collective-permute-start | bytes 1474568 | tf_op jit(solution)/shard_map/ppermute | solution.py:632
  47.0 19.4 %collective-permute-start.12 = (bf16[2880,128]{1,0:T(8,128)(2,1)S(1)}, bf16[2880,128]{1,0:T(8,128)(2,1)S(1)}, u32[]{:S(2)}, u32[]{:S(2)}) collective-permute-start(bf16[2880,128]{1,0:T(8,128)(2,1)S(1)} %shard_map.165.own_odd), channel_id=1, source_target_pairs={{0,2},{2,0},{1,3},{3,1},{4,6},{6,4},{5,7},{7,5},{8,10},{10,8},{9,1... | collective-permute-start | bytes 2211848 | tf_op jit(solution)/shard_map/ppermute | solution.py:579
  50.5 10.6 %copy-start.3 = (bf16[1024,512]{1,0:T(8,128)(2,1)S(1)}, bf16[1024,512]{1,0:T(8,128)(2,1)}, u32[]{:S(2)}) copy-start(bf16[1024,512]{1,0:T(8,128)(2,1)} %up.1) | copy-start | bytes 3145732
  50.5 10.6 %copy-start.4 = (bf16[1024,512]{1,0:T(8,128)(2,1)S(1)}, bf16[1024,512]{1,0:T(8,128)(2,1)}, u32[]{:S(2)}) copy-start(bf16[1024,512]{1,0:T(8,128)(2,1)} %down.3) | copy-start | bytes 3145732
  50.5 10.6 %copy-start.7 = (bf16[512,256]{1,0:T(8,128)(2,1)S(1)}, bf16[512,256]{1,0:T(8,128)(2,1)}, u32[]{:S(2)}) copy-start(bf16[512,256]{1,0:T(8,128)(2,1)} %ocean_up.3) | copy-start | bytes 786436
  50.5 10.6 %copy-start.8 = (bf16[512,256]{1,0:T(8,128)(2,1)S(1)}, bf16[512,256]{1,0:T(8,128)(2,1)}, u32[]{:S(2)}) copy-start(bf16[512,256]{1,0:T(8,128)(2,1)} %ocean_down.3) | copy-start | bytes 786436
  50.5 10.6 %copy-start.19 = (f32[512]{0:T(512)S(1)}, f32[512]{0:T(512)}, u32[]{:S(2)}) copy-start(f32[512]{0:T(512)} %gain.1) | copy-start | bytes 6148
  50.5 10.6 %copy-start.20 = (f32[256]{0:T(256)S(1)}, f32[256]{0:T(256)}, u32[]{:S(2)}) copy-start(f32[256]{0:T(256)} %ocean_gain.1) | copy-start | bytes 3076
  53.7 5.4 %collective-permute-start.7 = (bf16[320,768]{1,0:T(8,128)(2,1)}, bf16[320,768]{1,0:T(8,128)(2,1)S(1)}, u32[]{:S(2)}, u32[]{:S(2)}) collective-permute-start(bf16[320,768]{1,0:T(8,128)(2,1)} %collective-permute-done.3.refs_0_), channel_id=1, source_target_pairs={{0,1},{1,0},{2,3},{3,2},{4,5},{5,4},{6,7},{7,6},{8,9},{9,8},{10,11... | collective-permute-start | bytes 1474568 | tf_op jit(solution)/shard_map/ppermute | solution.py:637
  57.0 3.5 %collective-permute-start.8 = (bf16[320,768]{1,0:T(8,128)(2,1)S(1)}, bf16[320,768]{1,0:T(8,128)(2,1)S(1)}, u32[]{:S(2)}, u32[]{:S(2)}) collective-permute-start(bf16[320,768]{1,0:T(8,128)(2,1)S(1)} %collective-permute-done.6.refs_1_), channel_id=1, source_target_pairs={{0,1},{1,0},{2,3},{3,2},{4,5},{5,4},{6,7},{7,6},{8,9},{9,8},{10,11... | collective-permute-start | bytes 1474568 | tf_op jit(solution)/shard_map/ppermute | solution.py:637
  57.0 25.8 %collective-permute-start.9 = (bf16[1440,128]{1,0:T(8,128)(2,1)S(1)}, bf16[1440,128]{1,0:T(8,128)(2,1)S(1)}, u32[]{:S(2)}, u32[]{:S(2)}) collective-permute-start(bf16[1440,128]{1,0:T(8,128)(2,1)S(1)} %get-tuple-element.40.own_even), channel_id=1, source_target_pairs={{0,2},{2,0},{1,3},{3,1},{4,6},{6,4},{5,7},{7,5},{8,10},{10,8},{9,1... | collective-permute-start | bytes 1105928 | tf_op jit(solution)/shard_map/ppermute | solution.py:579
  58.5 24.3 %collective-permute-start.10 = (bf16[1440,128]{1,0:T(8,128)(2,1)S(1)}, bf16[1440,128]{1,0:T(8,128)(2,1)S(1)}, u32[]{:S(2)}, u32[]{:S(2)}) collective-permute-start(bf16[1440,128]{1,0:T(8,128)(2,1)S(1)} %get-tuple-element.43.own_odd), channel_id=1, source_target_pairs={{0,2},{2,0},{1,3},{3,1},{4,6},{6,4},{5,7},{7,5},{8,10},{10,8},{9,1... | collective-permute-start | bytes 1105928 | tf_op jit(solution)/shard_map/ppermute | solution.py:579
  59.1 37.5 %collective-permute-start.4 = (bf16[1440,128]{1,0:T(8,128)(2,1)}, bf16[1440,128]{1,0:T(8,128)(2,1)S(1)}, u32[]{:S(2)}, u32[]{:S(2)}) collective-permute-start(bf16[1440,128]{1,0:T(8,128)(2,1)} %get-tuple-element.39.own_even), channel_id=1, source_target_pairs={{0,2},{2,0},{1,3},{3,1},{4,6},{6,4},{5,7},{7,5},{8,10},{10,8},{9,1... | collective-permute-start | bytes 1105928 | tf_op jit(solution)/shard_map/ppermute | solution.py:579
  60.5 37.5 %collective-permute-start.5 = (bf16[1440,128]{1,0:T(8,128)(2,1)}, bf16[1440,128]{1,0:T(8,128)(2,1)}, u32[]{:S(2)}, u32[]{:S(2)}) collective-permute-start(bf16[1440,128]{1,0:T(8,128)(2,1)} %get-tuple-element.42.own_odd), channel_id=1, source_target_pairs={{0,2},{2,0},{1,3},{3,1},{4,6},{6,4},{5,7},{7,5},{8,10},{10,8},{9,1... | collective-permute-start | bytes 1105928 | tf_op jit(solution)/shard_map/ppermute | solution.py:579
  64.4 15.6 %copy-start.10 = (bf16[1024,256]{1,0:T(8,128)(2,1)}, bf16[1024,256]{1,0:T(8,128)(2,1)S(1)}, u32[]{:S(2)}) copy-start(bf16[1024,256]{1,0:T(8,128)(2,1)S(1)} %get-tuple-element.58.across) | copy-start | bytes 1572868
  64.4 15.6 %copy-start.12 = (bf16[128,1024]{1,0:T(8,128)(2,1)}, bf16[128,1024]{1,0:T(8,128)(2,1)S(1)}, u32[]{:S(2)}) copy-start(bf16[128,1024]{1,0:T(8,128)(2,1)S(1)} %get-tuple-element.59.back) | copy-start | bytes 786436
  66.4 13.6 %copy-start.16 = (s32[1,128,3]{1,0,2:T(1,128)S(1)}, s32[1,128,3]{1,0,2:T(1,128)}, u32[]{:S(2)}) copy-start(s32[1,128,3]{1,0,2:T(1,128)} %param.26) | copy-start | bytes 4612
  95.0 10.7 %copy-start.9 = (bf16[128,1024]{1,0:T(8,128)(2,1)S(1)}, bf16[128,1024]{1,0:T(8,128)(2,1)}, u32[]{:S(2)}) copy-start(bf16[128,1024]{1,0:T(8,128)(2,1)} %shard_map.172.own) | copy-start | bytes 786436
  95.0 10.7 %copy-start.11 = (bf16[1024,256]{1,0:T(8,128)(2,1)S(1)}, bf16[1024,256]{1,0:T(8,128)(2,1)}, u32[]{:S(2)}) copy-start(bf16[1024,256]{1,0:T(8,128)(2,1)} %copy-done.10) | copy-start | bytes 1572868
  95.0 10.7 %copy-start.13 = (bf16[128,1024]{1,0:T(8,128)(2,1)S(1)}, bf16[128,1024]{1,0:T(8,128)(2,1)}, u32[]{:S(2)}) copy-start(bf16[128,1024]{1,0:T(8,128)(2,1)} %copy-done.12) | copy-start | bytes 786436
  95.0 10.7 %copy-start.21 = (s32[8]{0:T(128)S(1)}, s32[8]{0:T(128)}, u32[]{:S(2)}) copy-start(s32[8]{0:T(128)} %mask.1) | copy-start | bytes 100
  95.0 10.7 %collective-permute-start.13 = (bf16[128,1024]{1,0:T(8,128)(2,1)}, bf16[128,1024]{1,0:T(8,128)(2,1)S(1)}, u32[]{:S(2)}, u32[]{:S(2)}) collective-permute-start(bf16[128,1024]{1,0:T(8,128)(2,1)} %shard_map.172.own), channel_id=1, source_target_pairs={{0,2},{2,0},{1,3},{3,1},{4,6},{6,4},{5,7},{7,5},{8,10},{10,8},{9,1... | collective-permute-start | bytes 786440 | tf_op jit(solution)/shard_map/ppermute | solution.py:679
  (8 other events, 13.6 us)
